TPU v7x, 128 devices: a whole 4x4x4 slice. The times are simulated.
128 devices in a mesh: dp: 8 (over x, core), expert: 16 (over z, y).
Axes of the slice: x: 4, y: 4, z: 4, core: 2. Of those that a mesh axis runs over, the one named last changes fastest.
Arguments:
- tokens: bfloat16 [128, 197, 768], P(('dp', 'expert')), may hold values from -6 to 6
- norm_attn_a: bfloat16 [768], P('dp'), may hold values from 0.5 to 1.5
- in_proj_a: bfloat16 [768, 2304], P('dp'), may hold values from -0.21875 to 0.21875
- out_proj_a: bfloat16 [768, 768], P('dp'), may hold values from -1.25 to 1.25
- norm_dense: bfloat16 [768], P('dp'), may hold values from 0.5 to 1.5
- dense_up: bfloat16 [768, 3072], P('dp'), may hold values from -0.21875 to 0.21875
- dense_down: bfloat16 [3072, 768], P('dp'), may hold values from -0.109375 to 0.109375
- norm_attn_b: bfloat16 [768], P('dp'), may hold values from 0.5 to 1.5
- in_proj_b: bfloat16 [768, 2304], P('dp'), may hold values from -0.21875 to 0.21875
- out_proj_b: bfloat16 [768, 768], P('dp'), may hold values from -1.25 to 1.25
- norm_moe: bfloat16 [768], P('dp'), may hold values from 0.5 to 1.5
- router: bfloat16 [768, 16], P('dp'), may hold values from -0.15625 to 0.15625
- expert_up: bfloat16 [16, 768, 3072], P('expert', None, 'dp'), may hold values from -0.21875 to 0.21875
- expert_down: bfloat16 [16, 3072, 768], P('expert', 'dp'), may hold values from -0.875 to 0.875
- routes: int32 [128, 197, 2], P(('dp', 'expert')), may hold values from 0 to 15, as said below
- slot_index: int32 [128, 197, 2], P(('dp', 'expert')), may hold values from 0 to 29, as said below
- keep_mask: int32 [128, 197, 2], P(('dp', 'expert')), may hold values 0 or 1
- output_grad: bfloat16 [128, 197, 768], P(('dp', 'expert')), may hold values from -6 to 6
Outputs:
- output: bfloat16 [128, 197, 768], P(('dp', 'expert'))
- input_grad: float32 [128, 197, 768], P(('dp', 'expert'))
- grad_norm_attn_a: float32 [768], P('dp')
- grad_in_proj_a: float32 [768, 2304], P('dp')
- grad_out_proj_a: float32 [768, 768], P('dp')
- grad_norm_dense: float32 [768], P('dp')
- grad_dense_up: float32 [768, 3072], P('dp')
- grad_dense_down: float32 [3072, 768], P('dp')
- grad_norm_attn_b: float32 [768], P('dp')
- grad_in_proj_b: float32 [768, 2304], P('dp')
- grad_out_proj_b: float32 [768, 768], P('dp')
- grad_norm_moe: float32 [768], P('dp')
- grad_router: float32 [768, 16], P('dp')
- grad_expert_up: float32 [16, 768, 3072], P('expert', None, 'dp')
- grad_expert_down: float32 [16, 3072, 768], P('expert', 'dp')
Inputs may be any that keep to these rules, and one draw needn't show every extreme that they name: `routes`: each token names two different experts; of the 197 tokens of one device, at most 15 name an expert as first choice and at most 15 as second. `slot_index`: first choices take slots below 15, second choices slots from 15 on; two choices of one device for one expert never share a slot; every device uses slot 29 of some expert.
All inputs are finite; a program needn't handle non-finite values. No bound on the sum of `keep_mask` on one device may be relied on, other than what follows from the above.
Results may differ from a plain program's by a relative error of at most 0.03.
Values may be sent and summed in bfloat16 or wider, within the bound.
No kernel may reach another device: no remote copies, remote signals or barrier semaphores. Data moves between devices by JAX's collectives and lax.ppermute only.
A program may use at most 192 MiB of HBM per device.

v0:
```python
import math

import jax
import jax.numpy as jnp
from jax import lax
from jax.sharding import PartitionSpec as P

HEAD_DIM = 64


epsilon = 1e-06
exact_precision = lax.Precision.HIGHEST


def product(left, right):
    return jnp.dot(left, right, preferred_element_type=jnp.float32)


def product_t(left, right):
    return lax.dot_general(
        left, right, (((0,), (0,)), ((), ())), preferred_element_type=jnp.float32
    )


def product_bt(left, right):
    return lax.dot_general(
        left, right, (((1,), (1,)), ((), ())), preferred_element_type=jnp.float32
    )


def norm_rows(stream, gain):
    center = jnp.mean(stream, axis=-1, keepdims=True)
    centred = stream - center
    spread = jnp.mean(centred * centred, axis=-1, keepdims=True)
    inverse = lax.rsqrt(spread + epsilon)
    scaled = centred * inverse
    return (scaled * gain.astype(jnp.float32), (scaled, inverse))


def norm_back(grad, gain, saved):
    scaled, inverse = saved
    shifted = grad * gain.astype(jnp.float32)
    gain_grad = jnp.sum(grad * scaled, axis=0)
    inner = (
        shifted
        - jnp.mean(shifted, axis=-1, keepdims=True)
        - scaled * jnp.mean(shifted * scaled, axis=-1, keepdims=True)
    )
    return (inner * inverse, gain_grad)


def gelu_slope(value):
    normal_cdf = 0.5 * (1.0 + lax.erf(value * (1.0 / math.sqrt(2.0))))
    return normal_cdf + value * jnp.exp(-0.5 * value * value) * (1.0 / math.sqrt(2.0 * math.pi))


def split_heads(joined, images, length):
    heads = joined.shape[1] // (3 * HEAD_DIM)
    parts = joined.reshape(images, length, 3, heads, HEAD_DIM)
    return (parts[:, :, 0], parts[:, :, 1], parts[:, :, 2])


def attend_forward(stream, gain, in_proj, out_proj, images, length):
    rows, width = stream.shape
    scale = HEAD_DIM ** (-0.5)
    normed_f, saved = norm_rows(stream, gain)
    normed = normed_f.astype(jnp.bfloat16)
    joined = product(normed, in_proj).astype(jnp.bfloat16)
    query, key, value = split_heads(joined, images, length)
    scores = jnp.einsum("sqhd,skhd->shqk", query, key, preferred_element_type=jnp.float32) * scale
    top = jnp.max(scores, axis=-1, keepdims=True)
    expo = jnp.exp(scores - top)
    total = jnp.sum(expo, axis=-1, keepdims=True)
    weights = expo / total
    log_total = top + jnp.log(total)
    mixed = jnp.einsum(
        "shqk,skhd->sqhd", weights.astype(jnp.bfloat16), value, preferred_element_type=jnp.float32
    )
    mixed = mixed.reshape(rows, width).astype(jnp.bfloat16)
    return (stream + product(mixed, out_proj), (normed, saved, joined, log_total, mixed))


def attend_backward(grad, gain, in_proj, out_proj, kept, images, length):
    normed, saved, joined, log_total, mixed = kept
    rows, width = grad.shape
    scale = HEAD_DIM ** (-0.5)
    grad_low = grad.astype(jnp.bfloat16)
    out_grad_w = product_t(mixed, grad_low)
    query, key, value = split_heads(joined, images, length)
    mixed_grad = product_bt(grad_low, out_proj).astype(jnp.bfloat16).reshape(query.shape)
    scores = jnp.einsum("sqhd,skhd->shqk", query, key, preferred_element_type=jnp.float32) * scale
    weights = jnp.exp(scores - log_total)
    weight_grad = jnp.einsum(
        "sqhd,skhd->shqk", mixed_grad, value, preferred_element_type=jnp.float32
    )
    value_grad = jnp.einsum(
        "shqk,sqhd->skhd",
        weights.astype(jnp.bfloat16),
        mixed_grad,
        preferred_element_type=jnp.float32,
    )
    score_grad = weights * (weight_grad - jnp.sum(weights * weight_grad, axis=-1, keepdims=True))
    score_grad = score_grad.astype(jnp.bfloat16)
    query_grad = (
        jnp.einsum("shqk,skhd->sqhd", score_grad, key, preferred_element_type=jnp.float32) * scale
    )
    key_grad = (
        jnp.einsum("shqk,sqhd->skhd", score_grad, query, preferred_element_type=jnp.float32) * scale
    )
    joined_grad = (
        jnp.stack([query_grad, key_grad, value_grad], axis=2)
        .reshape(rows, 3 * width)
        .astype(jnp.bfloat16)
    )
    in_grad_w = product_t(normed, joined_grad)
    stream_grad, gain_grad = norm_back(product_bt(joined_grad, in_proj), gain, saved)
    return (grad + stream_grad, (gain_grad, in_grad_w, out_grad_w))


def dense_forward(stream, gain, up_w, down_w):
    normed_f, saved = norm_rows(stream, gain)
    normed = normed_f.astype(jnp.bfloat16)
    pre = product(normed, up_w)
    hidden = jax.nn.gelu(pre, approximate=False).astype(jnp.bfloat16)
    return (stream + product(hidden, down_w), (normed, saved, pre, hidden))


def dense_backward(grad, gain, up_w, down_w, kept):
    normed, saved, pre, hidden = kept
    grad_low = grad.astype(jnp.bfloat16)
    down_grad = product_t(hidden, grad_low)
    pre_grad = (product_bt(grad_low, down_w) * gelu_slope(pre)).astype(jnp.bfloat16)
    up_grad = product_t(normed, pre_grad)
    stream_grad, gain_grad = norm_back(product_bt(pre_grad, up_w), gain, saved)
    return (grad + stream_grad, (gain_grad, up_grad, down_grad))


def expert_forward(received, up_local, down_local):
    width = received.shape[2]
    gathered = lax.all_gather(received, "dp", axis=0, tiled=True)
    flat = gathered.reshape(-1, width)
    pre = product(flat, up_local)
    hidden = jax.nn.gelu(pre, approximate=False).astype(jnp.bfloat16)
    partial_out = product(hidden, down_local).reshape(gathered.shape)
    result = lax.psum_scatter(
        partial_out.astype(jnp.bfloat16), "dp", scatter_dimension=0, tiled=True
    )
    return (result, (flat, pre, hidden, up_local, down_local))


def expert_backward(result_grad, kept):
    flat, pre, hidden, up_used, down_used = kept
    width = result_grad.shape[2]
    grad_all = lax.all_gather(result_grad, "dp", axis=0, tiled=True)
    grad_flat = grad_all.reshape(-1, width)
    down_grad = product_t(hidden, grad_flat)
    pre_grad = (product_bt(grad_flat, down_used) * gelu_slope(pre)).astype(jnp.bfloat16)
    up_grad = product_t(flat, pre_grad)
    partial_in = product_bt(pre_grad, up_used).reshape(grad_all.shape)
    in_grad = lax.psum_scatter(
        partial_in.astype(jnp.bfloat16), "dp", scatter_dimension=0, tiled=True
    )
    return (in_grad, up_grad, down_grad)


def moe_forward(stream, gain, router, up_local, down_local, routes, slot_index, keep_mask):
    rows, width = stream.shape
    experts = router.shape[1]
    capacity = 2 * ((rows + experts - 1) // experts + 2)
    normed_f, saved = norm_rows(stream, gain)
    normed = normed_f.astype(jnp.bfloat16)
    logits = product(normed, router)
    top = jnp.max(logits, axis=-1, keepdims=True)
    expo = jnp.exp(logits - top)
    probs = expo / jnp.sum(expo, axis=-1, keepdims=True)
    expert_ids = lax.broadcasted_iota(jnp.int32, (rows, experts), 1)
    keep_float = keep_mask.astype(jnp.float32)
    hot_first = (expert_ids == routes[:, 0:1]).astype(jnp.float32)
    hot_second = (expert_ids == routes[:, 1:2]).astype(jnp.float32)
    gate_first = jnp.sum(probs * hot_first, axis=-1, keepdims=True) * keep_float[:, 0:1]
    gate_second = jnp.sum(probs * hot_second, axis=-1, keepdims=True) * keep_float[:, 1:2]
    columns = lax.broadcasted_iota(jnp.int32, (rows, experts * capacity), 1)
    target = routes * capacity + slot_index
    pick_first = (columns == target[:, 0:1]).astype(jnp.float32) * keep_float[:, 0:1]
    pick_second = (columns == target[:, 1:2]).astype(jnp.float32) * keep_float[:, 1:2]
    select = (pick_first + pick_second).astype(jnp.bfloat16)
    send = product_t(select, normed).astype(jnp.bfloat16).reshape(experts, capacity, width)
    received = lax.all_to_all(send, "expert", split_axis=0, concat_axis=0, tiled=True)
    result, expert_kept = expert_forward(received, up_local, down_local)
    returned = lax.all_to_all(result, "expert", split_axis=0, concat_axis=0, tiled=True)
    returned = returned.reshape(experts * capacity, width).astype(jnp.float32)
    first = jnp.dot(
        pick_first, returned, precision=exact_precision, preferred_element_type=jnp.float32
    )
    second = jnp.dot(
        pick_second, returned, precision=exact_precision, preferred_element_type=jnp.float32
    )
    new_stream = stream + gate_first * first + gate_second * second
    kept = (
        normed,
        saved,
        probs,
        hot_first,
        hot_second,
        keep_float,
        gate_first,
        gate_second,
        pick_first,
        pick_second,
        select,
        first,
        second,
        expert_kept,
        received.shape,
        send.shape,
    )
    return (new_stream, kept)


def moe_backward(grad, gain, router, kept):
    (
        normed,
        saved,
        probs,
        hot_first,
        hot_second,
        keep_float,
        gate_first,
        gate_second,
        pick_first,
        pick_second,
        select,
        first,
        second,
        expert_kept,
        received_shape,
        send_shape,
    ) = kept
    dims = (((0,), (0,)), ((), ()))
    gate_grad_first = jnp.sum(grad * first, axis=-1, keepdims=True) * keep_float[:, 0:1]
    gate_grad_second = jnp.sum(grad * second, axis=-1, keepdims=True) * keep_float[:, 1:2]
    rows_grad = lax.dot_general(
        pick_first * gate_first,
        grad,
        dims,
        precision=exact_precision,
        preferred_element_type=jnp.float32,
    )
    rows_grad = rows_grad + lax.dot_general(
        pick_second * gate_second,
        grad,
        dims,
        precision=exact_precision,
        preferred_element_type=jnp.float32,
    )
    rows_grad = rows_grad.astype(jnp.bfloat16).reshape(send_shape)
    at_expert = lax.all_to_all(rows_grad, "expert", split_axis=0, concat_axis=0, tiled=True)
    in_grad, up_grad, down_grad = expert_backward(at_expert, expert_kept)
    back_rows = lax.all_to_all(in_grad, "expert", split_axis=0, concat_axis=0, tiled=True)
    back_rows = back_rows.reshape(select.shape[1], normed.shape[1])
    probs_grad = gate_grad_first * hot_first + gate_grad_second * hot_second
    logit_grad = probs * (probs_grad - jnp.sum(probs * probs_grad, axis=-1, keepdims=True))
    logit_grad = logit_grad.astype(jnp.bfloat16)
    router_grad = product_t(normed, logit_grad)
    normed_grad = product_bt(logit_grad, router) + product(select, back_rows)
    stream_grad, gain_grad = norm_back(normed_grad, gain, saved)
    return (grad + stream_grad, (gain_grad, router_grad, up_grad, down_grad))


def shards(
    tokens,
    norm_attn_a,
    in_proj_a,
    out_proj_a,
    norm_dense,
    dense_up,
    dense_down,
    norm_attn_b,
    in_proj_b,
    out_proj_b,
    norm_moe,
    router,
    expert_up,
    expert_down,
    routes,
    slot_index,
    keep_mask,
    output_grad,
):
    images, length, width = tokens.shape
    rows = images * length
    stream = tokens.reshape(rows, width).astype(jnp.float32)
    flat_routes = routes.reshape(rows, 2)
    flat_slots = slot_index.reshape(rows, 2)
    flat_keep = keep_mask.reshape(rows, 2)
    whole = (
        lax.all_gather(norm_attn_a, "dp", axis=0, tiled=True),
        lax.all_gather(in_proj_a, "dp", axis=0, tiled=True),
        lax.all_gather(out_proj_a, "dp", axis=0, tiled=True),
        lax.all_gather(norm_dense, "dp", axis=0, tiled=True),
        lax.all_gather(dense_up, "dp", axis=0, tiled=True),
        lax.all_gather(dense_down, "dp", axis=0, tiled=True),
        lax.all_gather(norm_attn_b, "dp", axis=0, tiled=True),
        lax.all_gather(in_proj_b, "dp", axis=0, tiled=True),
        lax.all_gather(out_proj_b, "dp", axis=0, tiled=True),
        lax.all_gather(norm_moe, "dp", axis=0, tiled=True),
        lax.all_gather(router, "dp", axis=0, tiled=True),
    )
    (
        gain_aa,
        in_aa,
        out_aa,
        gain_dd,
        up_dd,
        down_dd,
        gain_bb,
        in_bb,
        out_bb,
        gain_mm,
        router_full,
    ) = whole
    up_local = expert_up[0]
    down_local = expert_down[0]
    stream_one, kept_one = attend_forward(stream, gain_aa, in_aa, out_aa, images, length)
    stream_two, kept_two = dense_forward(stream_one, gain_dd, up_dd, down_dd)
    stream_three, kept_three = attend_forward(stream_two, gain_bb, in_bb, out_bb, images, length)
    stream_four, kept_four = moe_forward(
        stream_three, gain_mm, router_full, up_local, down_local, flat_routes, flat_slots, flat_keep
    )
    output = stream_four.astype(jnp.bfloat16).reshape(images, length, width)
    grad = output_grad.reshape(rows, width).astype(jnp.float32)
    grad, moe_grads = moe_backward(grad, gain_mm, router_full, kept_four)
    grad, attn_b_grads = attend_backward(grad, gain_bb, in_bb, out_bb, kept_three, images, length)
    grad, dense_grads = dense_backward(grad, gain_dd, up_dd, down_dd, kept_two)
    grad, attn_a_grads = attend_backward(grad, gain_aa, in_aa, out_aa, kept_one, images, length)
    input_grad = grad.reshape(images, length, width)
    shares = (
        lax.psum_scatter(
            attn_a_grads[0].astype(jnp.bfloat16), "dp", scatter_dimension=0, tiled=True
        ).astype(jnp.float32),
        lax.psum_scatter(
            attn_a_grads[1].astype(jnp.bfloat16), "dp", scatter_dimension=0, tiled=True
        ).astype(jnp.float32),
        lax.psum_scatter(
            attn_a_grads[2].astype(jnp.bfloat16), "dp", scatter_dimension=0, tiled=True
        ).astype(jnp.float32),
        lax.psum_scatter(
            dense_grads[0].astype(jnp.bfloat16), "dp", scatter_dimension=0, tiled=True
        ).astype(jnp.float32),
        lax.psum_scatter(
            dense_grads[1].astype(jnp.bfloat16), "dp", scatter_dimension=0, tiled=True
        ).astype(jnp.float32),
        lax.psum_scatter(
            dense_grads[2].astype(jnp.bfloat16), "dp", scatter_dimension=0, tiled=True
        ).astype(jnp.float32),
        lax.psum_scatter(
            attn_b_grads[0].astype(jnp.bfloat16), "dp", scatter_dimension=0, tiled=True
        ).astype(jnp.float32),
        lax.psum_scatter(
            attn_b_grads[1].astype(jnp.bfloat16), "dp", scatter_dimension=0, tiled=True
        ).astype(jnp.float32),
        lax.psum_scatter(
            attn_b_grads[2].astype(jnp.bfloat16), "dp", scatter_dimension=0, tiled=True
        ).astype(jnp.float32),
        lax.psum_scatter(
            moe_grads[0].astype(jnp.bfloat16), "dp", scatter_dimension=0, tiled=True
        ).astype(jnp.float32),
        lax.psum_scatter(
            moe_grads[1].astype(jnp.bfloat16), "dp", scatter_dimension=0, tiled=True
        ).astype(jnp.float32),
    )
    (
        share_ga,
        share_ia,
        share_oa,
        share_gd,
        share_ud,
        share_dd,
        share_gb,
        share_ib,
        share_ob,
        share_gm,
        share_rt,
    ) = shares
    totals = (
        lax.psum(share_ga.astype(jnp.bfloat16), "expert").astype(jnp.float32),
        lax.psum(share_ia.astype(jnp.bfloat16), "expert").astype(jnp.float32),
        lax.psum(share_oa.astype(jnp.bfloat16), "expert").astype(jnp.float32),
        lax.psum(share_gd.astype(jnp.bfloat16), "expert").astype(jnp.float32),
        lax.psum(share_ud.astype(jnp.bfloat16), "expert").astype(jnp.float32),
        lax.psum(share_dd.astype(jnp.bfloat16), "expert").astype(jnp.float32),
        lax.psum(share_gb.astype(jnp.bfloat16), "expert").astype(jnp.float32),
        lax.psum(share_ib.astype(jnp.bfloat16), "expert").astype(jnp.float32),
        lax.psum(share_ob.astype(jnp.bfloat16), "expert").astype(jnp.float32),
        lax.psum(share_gm.astype(jnp.bfloat16), "expert").astype(jnp.float32),
        lax.psum(share_rt.astype(jnp.bfloat16), "expert").astype(jnp.float32),
    )
    expert_up_grad = moe_grads[2][None]
    expert_down_grad = moe_grads[3][None]
    return (
        output,
        input_grad,
        totals[0],
        totals[1],
        totals[2],
        totals[3],
        totals[4],
        totals[5],
        totals[6],
        totals[7],
        totals[8],
        totals[9],
        totals[10],
        expert_up_grad,
        expert_down_grad,
    )


def solution(mesh):
    return jax.shard_map(
        shards,
        mesh=mesh,
        in_specs=(
            P(("dp", "expert"), None, None),
            P("dp"),
            P("dp", None),
            P("dp", None),
            P("dp"),
            P("dp", None),
            P("dp", None),
            P("dp"),
            P("dp", None),
            P("dp", None),
            P("dp"),
            P("dp", None),
            P("expert", None, "dp"),
            P("expert", "dp", None),
            P(("dp", "expert"), None, None),
            P(("dp", "expert"), None, None),
            P(("dp", "expert"), None, None),
            P(("dp", "expert"), None, None),
        ),
        out_specs=(
            P(("dp", "expert"), None, None),
            P(("dp", "expert"), None, None),
            P("dp"),
            P("dp", None),
            P("dp", None),
            P("dp"),
            P("dp", None),
            P("dp", None),
            P("dp"),
            P("dp", None),
            P("dp", None),
            P("dp"),
            P("dp", None),
            P("expert", None, "dp"),
            P("expert", "dp", None),
        ),
        check_vma=False,
    )
```

profile of v0, /device:TPU:6, one launch (start us, length us, event | category | flops | bytes accessed | tf_op | source)
XLA Modules:
  0.0 911.8 jit_solution(16403183946492195527)
XLA Ops:
  16.6 11.3 %all-reduce.11 = (bf16[768]{0:T(1024)(128)(2,1)S(1)}, bf16[768]{0:T(1024)(128)(2,1)S(1)}, bf16[768]{0:T(1024)(128)(2,1)S(1)}, bf16[768]{0:T(1024)(128)(2,1)S(1)}) all-reduce(bf16[768]{0:T(1024)(128)(2,1)S(1)} %dynamic-update-slice, bf16[768]{0:T(1024)(128)(2,1)S(1)} %dynamic-update-slice.1, ...), channel_id=1, replica_groups=mesh['dp'=8,'expert'=16] {'dp'}, use_global_device_ids=true, to_apply=%add | all-reduce | flops 3072 | bytes 12288
  28.5 11.6 %all-gather.10.cloned.1.call-done = bf16[768,2304]{1,0:T(8,128)(2,1)} async-done(((bf16[96,2304]{1,0:T(8,128)(2,1)}), bf16[768,2304]{1,0:T(8,128)(2,1)}) %all-gather.10.cloned.1.call-update) | async-done | bytes 3538960 | tf_op jit(solution)/shard_map/all_gather | solution.py:298
  49.0 16.2 %all-gather.12.cloned.1.call-done = bf16[768,768]{1,0:T(8,128)(2,1)} async-done(((bf16[96,768]{1,0:T(8,128)(2,1)}), bf16[768,768]{1,0:T(8,128)(2,1)}) %all-gather.12.cloned.1.call-update) | async-done | bytes 1179664 | tf_op jit(solution)/shard_map/all_gather | solution.py:299
  68.2 32.9 %all-gather.14.cloned.1.call-done = bf16[768,3072]{1,0:T(8,128)(2,1)} async-done(((bf16[96,3072]{1,0:T(8,128)(2,1)}), bf16[768,3072]{1,0:T(8,128)(2,1)}) %all-gather.14.cloned.1.call-update) | async-done | bytes 4718608 | tf_op jit(solution)/shard_map/all_gather | solution.py:301
  110.1 26.8 %all-gather.16.cloned.1.call-done = bf16[3072,768]{1,0:T(8,128)(2,1)} async-done(((bf16[384,768]{1,0:T(8,128)(2,1)}), bf16[3072,768]{1,0:T(8,128)(2,1)}) %all-gather.16.cloned.1.call-update) | async-done | bytes 4718608 | tf_op jit(solution)/shard_map/all_gather | solution.py:302
  142.1 26.1 %all-gather.18.cloned.1.call-done = bf16[768,2304]{1,0:T(8,128)(2,1)} async-done(((bf16[96,2304]{1,0:T(8,128)(2,1)}), bf16[768,2304]{1,0:T(8,128)(2,1)}) %all-gather.18.cloned.1.call-update) | async-done | bytes 3538960 | tf_op jit(solution)/shard_map/all_gather | solution.py:304
  180.1 13.1 %all-gather.20.cloned.1.call-done = bf16[768,768]{1,0:T(8,128)(2,1)} async-done(((bf16[96,768]{1,0:T(8,128)(2,1)}), bf16[768,768]{1,0:T(8,128)(2,1)}) %all-gather.20.cloned.1.call-update) | async-done | bytes 1179664 | tf_op jit(solution)/shard_map/all_gather | solution.py:305
  200.4 21.9 %all_to_all.20 = bf16[16,30,768]{2,1,0:T(8,128)(2,1)S(1)} all-to-all(bf16[16,30,768]{2,1,0:T(8,128)(2,1)} %reshape.423), channel_id=1, replica_groups=mesh['dp'=8,'expert'=16] {'expert'}, dimensions={0} | all-to-all | bytes 1474560 | tf_op jit(solution)/shard_map/all_to_all | solution.py:188
  223.7 35.4 %all-gather.22.cloned.1.call-done = bf16[128,30,768]{2,0,1:T(8,128)(2,1)} async-done(((bf16[16,30,768]{2,0,1:T(8,128)(2,1)}), bf16[128,30,768]{2,0,1:T(8,128)(2,1)}) %all-gather.22.cloned.1.call-update) | async-done | bytes 5898256 | tf_op jit(solution)/shard_map/all_gather | solution.py:140
  277.1 17.9 %fusion.2 = (bf16[3840,384]{1,0:T(8,128)(2,1)}, f32[3840,384]{1,0:T(8,128)}) fusion(bf16[3840,768]{1,0:T(8,128)(2,1)} %reshape.424, bf16[1,768,384]{2,1,0:T(8,128)(2,1)S(1)} %copy-done), kind=kOutput, calls=%fused_computation.5 | convolution fusion | flops 2360770560 | bytes 15335424 | tf_op jit(solution)/shard_map/dot_general | solution.py:16
  309.0 40.9 %reduce-scatter.12.cloned.1.call-done = bf16[16,30,768]{2,0,1:T(8,128)(2,1)} async-done(((bf16[128,30,768]{2,0,1:T(8,128)(2,1)}), bf16[16,30,768]{2,0,1:T(8,128)(2,1)}) %reduce-scatter.12.cloned.1.call-update) | async-done | bytes 737296 | tf_op jit(solution)/shard_map/reduce_scatter | solution.py:145
  359.1 12.9 %all-gather = bf16[8,96,16]{1,2,0:T(8,128)(2,1)S(1)} all-gather(bf16[1,96,16]{1,2,0:T(8,128)(2,1)S(1)} %bitcast.287), channel_id=1, replica_groups=mesh['dp'=8,'expert'=16] {'dp'}, dimensions={0}, use_global_device_ids=true | all-gather | bytes 27648 | tf_op jit(solution)/shard_map/all_gather | solution.py:307
  388.5 20.5 %all_to_all.21 = bf16[16,30,768]{2,1,0:T(8,128)(2,1)S(1)} all-to-all(bf16[16,30,768]{2,1,0:T(8,128)(2,1)} %reshape.428), channel_id=1, replica_groups=mesh['dp'=8,'expert'=16] {'expert'}, dimensions={0} | all-to-all | bytes 1474560 | tf_op jit(solution)/shard_map/all_to_all | solution.py:257
  410.4 35.9 %all-gather.24.cloned.1.call-done = bf16[128,30,768]{2,0,1:T(8,128)(2,1)} async-done(((bf16[16,30,768]{2,0,1:T(8,128)(2,1)}), bf16[128,30,768]{2,0,1:T(8,128)(2,1)}) %all-gather.24.cloned.1.call-update) | async-done | bytes 5898256 | tf_op jit(solution)/shard_map/all_gather | solution.py:154
  487.2 40.9 %reduce-scatter.14.cloned.1.call-done = bf16[16,30,768]{2,0,1:T(8,128)(2,1)} async-done(((bf16[128,30,768]{2,0,1:T(8,128)(2,1)}), bf16[16,30,768]{2,0,1:T(8,128)(2,1)}) %reduce-scatter.14.cloned.1.call-update) | async-done | bytes 737296 | tf_op jit(solution)/shard_map/reduce_scatter | solution.py:160
  541.2 12.1 %all-to-all-done.3 = bf16[16,30,768]{2,1,0:T(8,128)(2,1)} async-done(((bf16[16,30,768]{2,1,0:T(8,128)(2,1)}), bf16[16,30,768]{2,1,0:T(8,128)(2,1)}, u32[]{:S(2)}, u32[]{:S(2)}) %all-to-all-start.3) | async-done | bytes 737312 | tf_op jit(solution)/shard_map/all_to_all | solution.py:259
  613.5 26.7 %reduce-scatter.26.cloned.1.call-done = bf16[96,768]{1,0:T(8,128)(2,1)} async-done(((bf16[768,768]{1,0:T(8,128)(2,1)}), bf16[96,768]{1,0:T(8,128)(2,1)}) %reduce-scatter.26.cloned.1.call-update) | async-done | bytes 147472 | tf_op jit(solution)/shard_map/reduce_scatter | solution.py:362
  640.2 37.6 %reduce-scatter.24.cloned.1.call-done = bf16[96,2304]{1,0:T(8,128)(2,1)} async-done(((bf16[768,2304]{1,0:T(8,128)(2,1)}), bf16[96,2304]{1,0:T(8,128)(2,1)}) %reduce-scatter.24.cloned.1.call-update) | async-done | bytes 442384 | tf_op jit(solution)/shard_map/reduce_scatter | solution.py:359
  677.8 37.7 %reduce-scatter.16.cloned.1.call-done = bf16[96,2304]{1,0:T(8,128)(2,1)} async-done(((bf16[768,2304]{1,0:T(8,128)(2,1)}), bf16[96,2304]{1,0:T(8,128)(2,1)}) %reduce-scatter.16.cloned.1.call-update) | async-done | bytes 442384 | tf_op jit(solution)/shard_map/reduce_scatter | solution.py:341
  715.5 40.1 %reduce-scatter.20.cloned.1.call-done = bf16[96,3072]{1,0:T(8,128)(2,1)} async-done(((bf16[768,3072]{1,0:T(8,128)(2,1)}), bf16[96,3072]{1,0:T(8,128)(2,1)}) %reduce-scatter.20.cloned.1.call-update) | async-done | bytes 589840 | tf_op jit(solution)/shard_map/reduce_scatter | solution.py:350
  755.6 40.5 %reduce-scatter.22.cloned.1.call-done = bf16[384,768]{1,0:T(8,128)(2,1)} async-done(((bf16[3072,768]{1,0:T(8,128)(2,1)}), bf16[384,768]{1,0:T(8,128)(2,1)}) %reduce-scatter.22.cloned.1.call-update) | async-done | bytes 589840 | tf_op jit(solution)/shard_map/reduce_scatter | solution.py:353
  811.9 13.4 %all-reduce.10 = (bf16[768]{0:T(1024)(128)(2,1)S(1)}, bf16[768]{0:T(1024)(128)(2,1)S(1)}, bf16[768]{0:T(1024)(128)(2,1)S(1)}, bf16[768]{0:T(1024)(128)(2,1)S(1)}) all-reduce(bf16[768]{0:T(1024)(128)(2,1)S(1)} %get-tuple-element.66, bf16[768]{0:T(1024)(128)(2,1)S(1)} %get-tuple-element.64, ...), channel_id=4, replica_groups=mesh['dp'=8,'expert'=16] {'dp'}, use_global_device_ids=true, to_apply=%region_32.0.clone | all-reduce | flops 3072 | bytes 12288
  825.6 41.4 %all-reduce.8 = (bf16[96]{0:T(256)(128)(2,1)S(1)}, bf16[96]{0:T(256)(128)(2,1)S(1)}, bf16[96]{0:T(256)(128)(2,1)S(1)}, bf16[96]{0:T(256)(128)(2,1)S(1)}, bf16[96,16]{0,1:T(8,128)(2,1)S(1)}) all-reduce(bf16[96]{0:T(256)(128)(2,1)S(1)} %dynamic-slice.5, ...), channel_id=1, replica_groups=mesh['dp'=8,'expert'=16] {'expert'}, use_global_device_ids=true, to_apply=%region_33.0 | all-reduce | flops 1920 | bytes 7680 | tf_op jit(solution)/shard_map/psum | solution.py:386
  871.4 25.2 %all-reduce.14.cloned.1.call-done = (bf16[96,2304]{1,0:T(8,128)(2,1)}, bf16[96,768]{1,0:T(8,128)(2,1)}, bf16[96,3072]{1,0:T(8,128)(2,1)}, bf16[384,768]{1,0:T(8,...) async-done(((bf16[96,2304]{1,0:T(8,128)(2,1)}, bf16[96,768]{1,0:T(8,128)(2,1)}, bf16[96,3072]{1,0:T(8,128)(2,1)}, bf16[384,768]{1,0:T(8,128)(2,1)}, ...) | async-done | bytes 2359312 | tf_op jit(solution)/shard_map/psum | solution.py:387
  (310 shorter events, 255.8 us)
Async XLA Ops:
  7.2 269.9 %copy-start = (bf16[1,768,384]{2,1,0:T(8,128)(2,1)S(1)}, bf16[1,768,384]{2,1,0:T(8,128)(2,1)}, u32[]{:S(2)}) copy-start(bf16[1,768,384]{2,1,0:T(8,128)(2,1)} %param.30) | copy-start | bytes 1769476
  7.2 32.8 %all-gather.10.cloned.1.call-start = ((), (), s32[]{:S(2)}) async-start(), calls=%async_computation.13 | async-start | bytes 3981312 | tf_op jit(solution)/shard_map/all_gather | solution.py:298
  8.0 57.2 %all-gather.12.cloned.1.call-start = ((), (), s32[]{:S(2)}) async-start(), calls=%async_computation.14 | async-start | bytes 1327104 | tf_op jit(solution)/shard_map/all_gather | solution.py:299
  8.7 92.4 %all-gather.14.cloned.1.call-start = ((), (), s32[]{:S(2)}) async-start(), calls=%async_computation.15 | async-start | bytes 5308416 | tf_op jit(solution)/shard_map/all_gather | solution.py:301
  9.5 127.5 %all-gather.16.cloned.1.call-start = ((), (), s32[]{:S(2)}) async-start(), calls=%async_computation.16 | async-start | bytes 5308416 | tf_op jit(solution)/shard_map/all_gather | solution.py:302
  10.0 158.1 %all-gather.18.cloned.1.call-start = ((), (), s32[]{:S(2)}) async-start(), calls=%async_computation.17 | async-start | bytes 3981312 | tf_op jit(solution)/shard_map/all_gather | solution.py:304
  10.6 182.5 %all-gather.20.cloned.1.call-start = ((), (), s32[]{:S(2)}) async-start(), calls=%async_computation.18 | async-start | bytes 1327104 | tf_op jit(solution)/shard_map/all_gather | solution.py:305
  11.2 247.9 %all-gather.22.cloned.1.call-start = ((), (), s32[]{:S(2)}) async-start(), calls=%async_computation.19 | async-start | bytes 6635520 | tf_op jit(solution)/shard_map/all_gather | solution.py:140
  28.4 167.8 %copy-start.50 = (f32[197,1]{0,1:T(1,128)}, f32[197,1]{0,1:T(1,128)S(1)}, u32[]{:S(2)}) copy-start(f32[197,1]{0,1:T(1,128)S(1)} %get-tuple-element.107) | copy-start | bytes 2368
  28.4 350.8 %copy-start.44 = (f32[197,1]{0,1:T(1,128)}, f32[197,1]{0,1:T(1,128)S(1)}, u32[]{:S(2)}) copy-start(f32[197,1]{0,1:T(1,128)S(1)} %get-tuple-element.106) | copy-start | bytes 2368
  28.5 350.8 %copy-start.45 = (s32[197,1]{0,1:T(1,128)}, s32[197,1]{0,1:T(1,128)S(1)}, u32[]{:S(2)}) copy-start(s32[197,1]{0,1:T(1,128)S(1)} %get-tuple-element.104) | copy-start | bytes 2368
  223.7 126.2 %reduce-scatter.12.cloned.1.call-start = ((), (), s32[]{:S(2)}) async-start(), calls=%async_computation.20 | async-start | bytes 6635520 | tf_op jit(solution)/shard_map/reduce_scatter | solution.py:145
  352.1 22.8 %all-to-all-start.1 = ((bf16[16,30,768]{2,1,0:T(8,128)(2,1)}), bf16[16,30,768]{2,1,0:T(8,128)(2,1)}, u32[]{:S(2)}, u32[]{:S(2)}) async-start(bf16[16,30,768]{2,1,0:T(8,128)(2,1)} %copy.80), calls=%async_computation.2 | async-start | bytes 1572864 | tf_op jit(solution)/shard_map/all_to_all | solution.py:190
  359.0 87.3 %all-gather.24.cloned.1.call-start = ((), (), s32[]{:S(2)}) async-start(), calls=%async_computation.21 | async-start | bytes 6635520 | tf_op jit(solution)/shard_map/all_gather | solution.py:154
  410.4 117.7 %reduce-scatter.14.cloned.1.call-start = ((), (), s32[]{:S(2)}) async-start(), calls=%async_computation.22 | async-start | bytes 6635520 | tf_op jit(solution)/shard_map/reduce_scatter | solution.py:160
  530.3 22.9 %all-to-all-start.3 = ((bf16[16,30,768]{2,1,0:T(8,128)(2,1)}), bf16[16,30,768]{2,1,0:T(8,128)(2,1)}, u32[]{:S(2)}, u32[]{:S(2)}) async-start(bf16[16,30,768]{2,1,0:T(8,128)(2,1)} %copy.84), calls=%async_computation.5 | async-start | bytes 1572864 | tf_op jit(solution)/shard_map/all_to_all | solution.py:259
  537.3 75.4 %reduce-scatter.28.cloned.1.call-start = ((), (), s32[]{:S(2)}) async-start(), calls=%async_computation.29 | async-start | bytes 221184
  539.4 74.1 %reduce-scatter.18.cloned.1.call-start = ((), (), s32[]{:S(2)}) async-start(), calls=%async_computation.24 | async-start | bytes 1327104 | tf_op jit(solution)/shard_map/reduce_scatter | solution.py:344
  579.8 60.4 %reduce-scatter.26.cloned.1.call-start = ((), (), s32[]{:S(2)}) async-start(), calls=%async_computation.28 | async-start | bytes 1327104 | tf_op jit(solution)/shard_map/reduce_scatter | solution.py:362
  582.5 95.3 %reduce-scatter.24.cloned.1.call-start = ((), (), s32[]{:S(2)}) async-start(), calls=%async_computation.27 | async-start | bytes 3981312 | tf_op jit(solution)/shard_map/reduce_scatter | solution.py:359
  587.2 128.3 %reduce-scatter.16.cloned.1.call-start = ((), (), s32[]{:S(2)}) async-start(), calls=%async_computation.23 | async-start | bytes 3981312 | tf_op jit(solution)/shard_map/reduce_scatter | solution.py:341
  601.4 154.3 %reduce-scatter.20.cloned.1.call-start = ((), (), s32[]{:S(2)}) async-start(), calls=%async_computation.25 | async-start | bytes 5308416 | tf_op jit(solution)/shard_map/reduce_scatter | solution.py:350
  606.6 189.5 %reduce-scatter.22.cloned.1.call-start = ((), (), s32[]{:S(2)}) async-start(), calls=%async_computation.26 | async-start | bytes 5308416 | tf_op jit(solution)/shard_map/reduce_scatter | solution.py:353
  611.6 284.9 %all-reduce.14.cloned.1.call-start = ((), (), s32[]{:S(2)}) async-start(), calls=%async_computation.30 | async-start | bytes 4718592 | tf_op jit(solution)/shard_map/psum | solution.py:387
  (61 other events, 716.4 us)
Sparse Core Ops, SparseCore 0:
  9.8 30.2 all-gather.9
  41.8 23.3 all-gather.11
  66.9 34.1 all-gather.13
  102.7 34.2 all-gather.15
  138.5 29.6 all-gather.17
  169.7 23.3 all-gather.19
  223.8 35.2 all-gather.21
  309.1 40.7 reduce-scatter.11
  410.5 35.8 all-gather.23
  487.4 40.6 reduce-scatter.13
  541.0 29.3 reduce-scatter.27
  579.9 26.1 reduce-scatter.17
  609.2 30.9 reduce-scatter.25
  642.6 35.1 reduce-scatter.23
  680.1 35.4 reduce-scatter.15
  717.9 37.6 reduce-scatter.19
  758.0 38.0 reduce-scatter.21
  800.6 95.9 all-reduce.13
where the time goes:
time: 924 us; the launch traced here: 912 us
  waiting for transfers between devices  505 us (55%)
  matrix products  144 us (16%)
  blocking collectives  121 us (13%)
  local copies, waits for them, and re-layouts  91.8 us (10%)
  between operations  17.1 us (2%)
  other arithmetic  17 us (2%)
  starting transfers between devices  15.1 us (2%)
    dot_general x10, matrix products, product(): return jnp.dot(left, right, preferred_element_type=jnp.float32)  54.1 us
    psum x1, blocking collectives, shards(): lax.psum(share_ga.astype(jnp.bfloat16), 'expert').astype(jnp.float32)  41.4 us
    reduce_scatter x1, waiting for transfers between devices, expert_backward(): lax.psum_scatter(partial_in.astype(jnp.bfloat16), 'dp', scatter_dimension...  40.9 us
    reduce_scatter x1, waiting for transfers between devices, expert_forward(): lax.psum_scatter(partial_out.astype(jnp.bfloat16), 'dp', scatter_dimensio...  40.9 us
    reduce_scatter x1, waiting for transfers between devices, shards(): lax.psum_scatter(dense_grads[2].astype(jnp.bfloat16), 'dp', scatter_dimen...  40.5 us
    reduce_scatter x1, waiting for transfers between devices, shards(): lax.psum_scatter(dense_grads[1].astype(jnp.bfloat16), 'dp', scatter_dimen...  40.1 us
    reduce_scatter x1, waiting for transfers between devices, shards(): lax.psum_scatter(attn_a_grads[1].astype(jnp.bfloat16), 'dp', scatter_dime...  37.7 us
    reduce_scatter x1, waiting for transfers between devices, shards(): lax.psum_scatter(attn_b_grads[1].astype(jnp.bfloat16), 'dp', scatter_dime...  37.6 us
  transfers between devices with their start and end apart: 20, of which 18 were waited for; matrix products, arithmetic and copies ran while one was open for 13% of the time, Pallas kernels for 0%

commit v1 on v0

v1 whole, which is shorter than its diff:
```python
import math

import jax
import jax.numpy as jnp
from jax import lax
from jax.sharding import Mesh, PartitionSpec as P

HEAD_DIM = 64


epsilon = 1e-06


def product(left, right):
    return jnp.dot(left, right, preferred_element_type=jnp.float32)


def product_t(left, right):
    return lax.dot_general(
        left, right, (((0,), (0,)), ((), ())), preferred_element_type=jnp.float32
    )


def product_bt(left, right):
    return lax.dot_general(
        left, right, (((1,), (1,)), ((), ())), preferred_element_type=jnp.float32
    )


def norm_rows(stream, gain):
    center = jnp.mean(stream, axis=-1, keepdims=True)
    centred = stream - center
    spread = jnp.mean(centred * centred, axis=-1, keepdims=True)
    inverse = lax.rsqrt(spread + epsilon)
    scaled = centred * inverse
    return (scaled * gain.astype(jnp.float32), (scaled, inverse))


def norm_back(grad, gain, saved):
    scaled, inverse = saved
    shifted = grad * gain.astype(jnp.float32)
    gain_grad = jnp.sum(grad * scaled, axis=0)
    inner = (
        shifted
        - jnp.mean(shifted, axis=-1, keepdims=True)
        - scaled * jnp.mean(shifted * scaled, axis=-1, keepdims=True)
    )
    return (inner * inverse, gain_grad)


def gelu_parts(value):
    normal_cdf = 0.5 * (1.0 + lax.erf(value * (1.0 / math.sqrt(2.0))))
    slope = normal_cdf + value * jnp.exp(-0.5 * value * value) * (1.0 / math.sqrt(2.0 * math.pi))
    return value * normal_cdf, slope


def split_heads(joined, images, length):
    heads = joined.shape[1] // (3 * HEAD_DIM)
    parts = joined.reshape(images, length, 3, heads, HEAD_DIM)
    return (parts[:, :, 0], parts[:, :, 1], parts[:, :, 2])


X, CORES = 4, 2
SLOTS = 32


def x_shift(block, step):
    return lax.ppermute(block, "x", [(i, (i + step) % X) for i in range(X)])


def core_swap(block):
    return lax.ppermute(block, "core", [(0, 1), (1, 0)])


def gather_rows(shard):
    xi, ci = lax.axis_index("x"), lax.axis_index("core")
    half = jnp.zeros((X,) + shard.shape, shard.dtype)
    half = lax.dynamic_update_index_in_dim(half, shard, xi, 0)
    for step in range(1, X):
        half = lax.dynamic_update_index_in_dim(half, x_shift(shard, step), (xi - step) % X, 0)
    other = core_swap(half)
    whole = jnp.where(
        ci == 0, jnp.stack([half, other], axis=1), jnp.stack([other, half], axis=1)
    )
    return whole.reshape(X * CORES * shard.shape[0], shard.shape[1])


def split_rows(left):
    xi, ci = lax.axis_index("x"), lax.axis_index("core")
    rows, wide = left.shape
    blocks = left.T.reshape(X, CORES, wide // (X * CORES), rows)
    blocks = lax.dynamic_slice_in_dim(jnp.concatenate([blocks, blocks], axis=0), xi, X, axis=0)
    own = lax.dynamic_index_in_dim(blocks, ci, 1, keepdims=False)
    other = lax.dynamic_index_in_dim(blocks, 1 - ci, 1, keepdims=False)
    return own.reshape(wide // CORES, rows), other.reshape(wide // CORES, rows)


def sum_over_x(first, blocks, sign):
    total = first
    for step in range(1, X):
        total = total + x_shift(blocks[step - 1], sign * step).astype(jnp.float32)
    return total


def scatter_halves(own, other):
    total = own + core_swap(other.astype(jnp.bfloat16)).astype(jnp.float32)
    block = own.shape[0] // X
    low = total[block:].astype(jnp.bfloat16)
    return sum_over_x(total[:block], [low[k * block : (k + 1) * block] for k in range(X - 1)], 1)


def weight_grad(left, right):
    own, other = split_rows(left)
    return scatter_halves(product(own, right), product(other, right))


def attend_forward(stream, gain, in_proj, out_proj, images, length):
    rows, width = stream.shape
    scale = HEAD_DIM ** (-0.5)
    normed_f, saved = norm_rows(stream, gain)
    normed = normed_f.astype(jnp.bfloat16)
    joined = product(normed, in_proj).astype(jnp.bfloat16)
    query, key, value = split_heads(joined, images, length)
    scores = jnp.einsum("sqhd,skhd->shqk", query, key, preferred_element_type=jnp.float32) * scale
    top = jnp.max(scores, axis=-1, keepdims=True)
    expo = jnp.exp(scores - top)
    total = jnp.sum(expo, axis=-1, keepdims=True)
    weights = expo / total
    log_total = top + jnp.log(total)
    mixed = jnp.einsum(
        "shqk,skhd->sqhd", weights.astype(jnp.bfloat16), value, preferred_element_type=jnp.float32
    )
    mixed = mixed.reshape(rows, width).astype(jnp.bfloat16)
    return (stream + product(mixed, out_proj), (normed, saved, joined, log_total, mixed))


def attend_backward(grad, gain, in_proj, out_proj, kept, images, length):
    normed, saved, joined, log_total, mixed = kept
    rows, width = grad.shape
    scale = HEAD_DIM ** (-0.5)
    grad_low = grad.astype(jnp.bfloat16)
    out_grad_w = weight_grad(mixed, grad_low)
    query, key, value = split_heads(joined, images, length)
    mixed_grad = product_bt(grad_low, out_proj).astype(jnp.bfloat16).reshape(query.shape)
    scores = jnp.einsum("sqhd,skhd->shqk", query, key, preferred_element_type=jnp.float32) * scale
    weights = jnp.exp(scores - log_total)
    weight_grad_ = jnp.einsum(
        "sqhd,skhd->shqk", mixed_grad, value, preferred_element_type=jnp.float32
    )
    value_grad = jnp.einsum(
        "shqk,sqhd->skhd",
        weights.astype(jnp.bfloat16),
        mixed_grad,
        preferred_element_type=jnp.float32,
    )
    score_grad = weights * (weight_grad_ - jnp.sum(weights * weight_grad_, axis=-1, keepdims=True))
    score_grad = score_grad.astype(jnp.bfloat16)
    query_grad = (
        jnp.einsum("shqk,skhd->sqhd", score_grad, key, preferred_element_type=jnp.float32) * scale
    )
    key_grad = (
        jnp.einsum("shqk,sqhd->skhd", score_grad, query, preferred_element_type=jnp.float32) * scale
    )
    joined_grad = (
        jnp.stack([query_grad, key_grad, value_grad], axis=2)
        .reshape(rows, 3 * width)
        .astype(jnp.bfloat16)
    )
    in_grad_w = weight_grad(normed, joined_grad)
    stream_grad, gain_grad = norm_back(product_bt(joined_grad, in_proj), gain, saved)
    return (grad + stream_grad, (gain_grad, in_grad_w, out_grad_w))


def dense_forward(stream, gain, up_w, down_w):
    normed_f, saved = norm_rows(stream, gain)
    normed = normed_f.astype(jnp.bfloat16)
    hidden, slope = gelu_parts(product(normed, up_w))
    hidden = hidden.astype(jnp.bfloat16)
    return (stream + product(hidden, down_w), (normed, saved, slope, hidden))


def dense_backward(grad, gain, up_w, down_w, kept):
    normed, saved, slope, hidden = kept
    grad_low = grad.astype(jnp.bfloat16)
    down_grad = weight_grad(hidden, grad_low)
    pre_grad = (product_bt(grad_low, down_w) * slope).astype(jnp.bfloat16)
    up_grad = weight_grad(normed, pre_grad)
    stream_grad, gain_grad = norm_back(product_bt(pre_grad, up_w), gain, saved)
    return (grad + stream_grad, (gain_grad, up_grad, down_grad))


def moe(stream, grad_low, gain, router, up_local, down_local, routes, slot_index, keep_mask):
    rows, width = stream.shape
    experts = router.shape[1]
    slots = experts * SLOTS
    hidden_local = up_local.shape[1]
    grad = grad_low.astype(jnp.float32)
    ups = [up_local] + [x_shift(up_local, k) for k in range(1, X)]
    downs = [down_local] + [x_shift(down_local, k) for k in range(1, X)]
    up_half = jnp.concatenate(ups, axis=1)
    down_half = jnp.concatenate(downs, axis=0)

    normed_f, saved = norm_rows(stream, gain)
    normed = normed_f.astype(jnp.bfloat16)
    logits = product(normed, router)
    top = jnp.max(logits, axis=-1, keepdims=True)
    expo = jnp.exp(logits - top)
    probs = expo / jnp.sum(expo, axis=-1, keepdims=True)
    expert_ids = lax.broadcasted_iota(jnp.int32, (rows, experts), 1)
    keep_float = keep_mask.astype(jnp.float32)
    keep_first, keep_second = keep_float[:, 0:1], keep_float[:, 1:2]
    hot_first = (expert_ids == routes[:, 0:1]).astype(jnp.float32)
    hot_second = (expert_ids == routes[:, 1:2]).astype(jnp.float32)
    gate_first = jnp.sum(probs * hot_first, axis=-1, keepdims=True) * keep_first
    gate_second = jnp.sum(probs * hot_second, axis=-1, keepdims=True) * keep_second
    columns = lax.broadcasted_iota(jnp.int32, (rows, slots), 1)
    target = routes * SLOTS + slot_index
    pick_first = (columns == target[:, 0:1]).astype(jnp.float32) * keep_first
    pick_second = (columns == target[:, 1:2]).astype(jnp.float32) * keep_second
    select = (pick_first + pick_second).astype(jnp.bfloat16)
    slot_gate = jnp.sum(pick_first * gate_first + pick_second * gate_second, axis=0)
    send_rows = product_t(select, normed).astype(jnp.bfloat16)
    send_grad = (product_t(select, grad_low) * slot_gate[:, None]).astype(jnp.bfloat16)
    send = jnp.stack(
        [send_rows.reshape(experts, SLOTS, width), send_grad.reshape(experts, SLOTS, width)], axis=1
    )
    received = lax.all_to_all(send, ("z", "y"), split_axis=0, concat_axis=0, tiled=True)
    partner = core_swap(received)

    flat = jnp.concatenate(
        [received[:, 0].reshape(slots, width), partner[:, 0].reshape(slots, width)], axis=0
    )
    flat_grad = jnp.concatenate(
        [received[:, 1].reshape(slots, width), partner[:, 1].reshape(slots, width)], axis=0
    )
    hidden, slope = gelu_parts(product(flat, up_half))
    hidden = hidden.astype(jnp.bfloat16)
    partial_out = product(hidden, down_half)
    pre_grad = (product_bt(flat_grad, down_half) * slope).astype(jnp.bfloat16)
    partial_in = product_bt(pre_grad, up_half)
    other_half = jnp.stack(
        [
            partial_out[slots:].astype(jnp.bfloat16).reshape(experts, SLOTS, width),
            partial_in[slots:].astype(jnp.bfloat16).reshape(experts, SLOTS, width),
        ],
        axis=1,
    )
    own_half = jnp.stack(
        [
            partial_out[:slots].reshape(experts, SLOTS, width),
            partial_in[:slots].reshape(experts, SLOTS, width),
        ],
        axis=1,
    )
    back = (own_half + core_swap(other_half).astype(jnp.float32)).astype(jnp.bfloat16)
    returned = lax.all_to_all(back, ("z", "y"), split_axis=0, concat_axis=0, tiled=True)
    result_rows = returned[:, 0].reshape(slots, width)
    back_rows = returned[:, 1].reshape(slots, width)

    cuts = [slice(k * hidden_local, (k + 1) * hidden_local) for k in range(X)]
    up_parts = [product_t(flat, pre_grad[:, cut]) for cut in cuts]
    down_parts = [product_t(hidden[:, cut], flat_grad) for cut in cuts]
    up_grad = sum_over_x(up_parts[0], [p.astype(jnp.bfloat16) for p in up_parts[1:]], -1)
    down_grad = sum_over_x(down_parts[0], [p.astype(jnp.bfloat16) for p in down_parts[1:]], -1)

    first = product(pick_first.astype(jnp.bfloat16), result_rows)
    second = product(pick_second.astype(jnp.bfloat16), result_rows)
    new_stream = stream + gate_first * first + gate_second * second
    gate_grad_first = jnp.sum(grad * first, axis=-1, keepdims=True) * keep_first
    gate_grad_second = jnp.sum(grad * second, axis=-1, keepdims=True) * keep_second
    probs_grad = gate_grad_first * hot_first + gate_grad_second * hot_second
    logit_grad = probs * (probs_grad - jnp.sum(probs * probs_grad, axis=-1, keepdims=True))
    logit_grad = logit_grad.astype(jnp.bfloat16)
    router_grad = product_t(normed, logit_grad)
    normed_grad = product_bt(logit_grad, router) + product(select, back_rows)
    stream_grad, gain_grad = norm_back(normed_grad, gain, saved)
    return (new_stream, grad + stream_grad, (gain_grad, router_grad, up_grad, down_grad))


def shards(
    tokens,
    norm_attn_a,
    in_proj_a,
    out_proj_a,
    norm_dense,
    dense_up,
    dense_down,
    norm_attn_b,
    in_proj_b,
    out_proj_b,
    norm_moe,
    router,
    expert_up,
    expert_down,
    routes,
    slot_index,
    keep_mask,
    output_grad,
):
    images, length, width = tokens.shape
    rows = images * length
    stream = tokens.reshape(rows, width).astype(jnp.float32)
    flat_routes = routes.reshape(rows, 2)
    flat_slots = slot_index.reshape(rows, 2)
    flat_keep = keep_mask.reshape(rows, 2)
    experts = router.shape[1]
    small = jnp.concatenate(
        [
            jnp.stack([norm_attn_a, norm_dense, norm_attn_b, norm_moe], axis=1),
            router,
            jnp.zeros((router.shape[0], 128 - 4 - experts), router.dtype),
        ],
        axis=1,
    )
    wide_in, wide_out = in_proj_a.shape[1], out_proj_a.shape[1]
    first = gather_rows(jnp.concatenate([in_proj_a, out_proj_a, small], axis=1))
    in_aa, out_aa = first[:, :wide_in], first[:, wide_in : wide_in + wide_out]
    small_all = first[:, wide_in + wide_out :]
    gain_aa, gain_dd, gain_bb, gain_mm = (small_all[:, k] for k in range(4))
    router_full = small_all[:, 4 : 4 + experts]
    up_dd = gather_rows(dense_up)
    down_dd = gather_rows(dense_down)
    second = gather_rows(jnp.concatenate([in_proj_b, out_proj_b], axis=1))
    in_bb, out_bb = second[:, :wide_in], second[:, wide_in:]

    stream_one, kept_one = attend_forward(stream, gain_aa, in_aa, out_aa, images, length)
    stream_two, kept_two = dense_forward(stream_one, gain_dd, up_dd, down_dd)
    stream_three, kept_three = attend_forward(stream_two, gain_bb, in_bb, out_bb, images, length)
    stream_four, grad, moe_grads = moe(
        stream_three,
        output_grad.reshape(rows, width),
        gain_mm,
        router_full,
        expert_up[0],
        expert_down[0],
        flat_routes,
        flat_slots,
        flat_keep,
    )
    output = stream_four.astype(jnp.bfloat16).reshape(images, length, width)
    grad, attn_b_grads = attend_backward(grad, gain_bb, in_bb, out_bb, kept_three, images, length)
    grad, dense_grads = dense_backward(grad, gain_dd, up_dd, down_dd, kept_two)
    grad, attn_a_grads = attend_backward(grad, gain_aa, in_aa, out_aa, kept_one, images, length)
    input_grad = grad.reshape(images, length, width)
    small_grad = jnp.concatenate(
        [
            jnp.stack([attn_a_grads[0], dense_grads[0], attn_b_grads[0], moe_grads[0]], axis=0),
            moe_grads[1].T,
            jnp.zeros((128 - 4 - experts, width), jnp.float32),
        ],
        axis=0,
    )
    small_share = scatter_halves(*split_rows(small_grad))
    shares = [
        attn_a_grads[1],
        attn_a_grads[2],
        dense_grads[1],
        dense_grads[2],
        attn_b_grads[1],
        attn_b_grads[2],
        small_share,
    ]
    totals = lax.psum([share.astype(jnp.bfloat16) for share in shares], ("z", "y"))
    in_a, out_a, up, down, in_b, out_b, small_total = [t.astype(jnp.float32) for t in totals]
    return (
        output,
        input_grad,
        small_total[:, 0],
        in_a,
        out_a,
        small_total[:, 1],
        up,
        down,
        small_total[:, 2],
        in_b,
        out_b,
        small_total[:, 3],
        small_total[:, 4 : 4 + experts],
        moe_grads[2][None],
        moe_grads[3][None],
    )


def solution(mesh):
    places = Mesh(mesh.devices.reshape(X, CORES, 4, 4), ("x", "core", "z", "y"))
    dp, expert = ("x", "core"), ("z", "y")
    images = P(dp + expert, None, None)
    return jax.shard_map(
        shards,
        mesh=places,
        in_specs=(
            images,
            P(dp),
            P(dp, None),
            P(dp, None),
            P(dp),
            P(dp, None),
            P(dp, None),
            P(dp),
            P(dp, None),
            P(dp, None),
            P(dp),
            P(dp, None),
            P(expert, None, dp),
            P(expert, dp, None),
            images,
            images,
            images,
            images,
        ),
        out_specs=(
            images,
            images,
            P(dp),
            P(dp, None),
            P(dp, None),
            P(dp),
            P(dp, None),
            P(dp, None),
            P(dp),
            P(dp, None),
            P(dp, None),
            P(dp),
            P(dp, None),
            P(expert, None, dp),
            P(expert, dp, None),
        ),
        check_vma=False,
    )
```

time: 924 us -> 661 us (0.72)
  waiting for transfers between devices: 505 us -> 240 us
  starting transfers between devices: 15.1 us -> 62.4 us
  matrix products: 144 us -> 104 us
  other arithmetic: 17 us -> 44.9 us
  blocking collectives: 121 us -> 106 us
  local copies, waits for them, and re-layouts: 91.8 us -> 77.5 us
    reduce_scatter x8 -> x0, waiting for transfers between devices: 264 us -> none  [the longest x1 40.9 us: expert_backward(): lax.psum_scatter(partial_in.astype(jnp.bfloat16), 'dp', scatter_dimension...]
    ppermute x0 -> x58, waiting for transfers between devices: none -> 237 us  [the longest x45 235 us: x_shift(): return lax.ppermute(block, 'x', [(i, (i + step) % X) for i in range(X)])]
    all_gather x8 -> x0, waiting for transfers between devices: 198 us -> none  [the longest x1 35.9 us: expert_backward(): grad_all = lax.all_gather(result_grad, 'dp', axis=0, tiled=True)]
    ppermute x0 -> x58, starting transfers between devices: none -> 58 us  [the longest x45 55.6 us: x_shift(): return lax.ppermute(block, 'x', [(i, (i + step) % X) for i in range(X)])]
    psum x1, blocking collectives: 41.4 us -> 74.6 us  [shards(): lax.psum([share.astype(jnp.bfloat16) for share in shares], ('z', 'y'))]
    psum x1, waiting for transfers between devices: 25.2 us -> 0.01 us  [shards(): lax.psum([share.astype(jnp.bfloat16) for share in shares], ('z', 'y'))]
    unnamed x2 -> x0, blocking collectives: 24.7 us -> none
    all_gather x3 -> x0, local copies, waits for them, and re-layouts: 17.3 us -> none  [the longest x1 8.64 us: expert_forward(): gathered = lax.all_gather(received, 'dp', axis=0, tiled=True)]
  transfers between devices with their start and end apart: 20 -> 60, of which waited for: 18 -> 29; matrix products, arithmetic and copies ran while one was open for 13% -> 19% of each run, Pallas kernels for 0% -> 0%
where the time goes in v1:
time: 661 us; the launch traced here: 651 us
  waiting for transfers between devices  240 us (36%)
  blocking collectives  106 us (16%)
  matrix products  104 us (16%)
  local copies, waits for them, and re-layouts  77.5 us (12%)
  starting transfers between devices  62.4 us (9%)
  other arithmetic  44.9 us (7%)
  between operations  16.6 us (3%)
    ppermute x45, waiting for transfers between devices, x_shift(): return lax.ppermute(block, 'x', [(i, (i + step) % X) for i in range(X)])  235 us
    psum x1, blocking collectives, shards(): lax.psum([share.astype(jnp.bfloat16) for share in shares], ('z', 'y'))  74.6 us
    ppermute x45, starting transfers between devices, x_shift(): return lax.ppermute(block, 'x', [(i, (i + step) % X) for i in range(X)])  55.6 us
    dot_general x24, matrix products, product(): return jnp.dot(left, right, preferred_element_type=jnp.float32)  39.3 us
    all_to_all x1, blocking collectives, moe(): lax.all_to_all(send, ('z', 'y'), split_axis=0, concat_axis=0, tiled=True)  31.5 us
    dot_general x9, matrix products, product_bt(): lax.dot_general(left, right, (((1,), (1,)), ((), ())), preferred_element_...  25.5 us
    dot_general x11, matrix products, product_t(): lax.dot_general(left, right, (((0,), (0,)), ((), ())), preferred_element_...  20.8 us
    unnamed x247, local copies, waits for them, and re-layouts  18.3 us
  transfers between devices with their start and end apart: 60, of which 29 were waited for; matrix products, arithmetic and copies ran while one was open for 19% of the time, Pallas kernels for 0%

profile of v1, /device:TPU:6, one launch (start us, length us, event | category | flops | bytes accessed | tf_op | source)
XLA Modules:
  0.0 650.6 jit_solution(87771416259603080)
XLA Ops:
  29.1 12.7 %collective-permute-done.8 = bf16[384,768]{1,0:T(8,128)(2,1)} collective-permute-done((bf16[384,768]{1,0:T(8,128)(2,1)}, bf16[384,768]{1,0:T(8,128)(2,1)}, u32[]{:S(2)}, u32[]{:S(2)}) %collective-permute-start.8) | collective-permute-done | bytes 589856 | tf_op jit(solution)/shard_map/ppermute | solution.py:68
  45.6 18.1 %collective-permute-done.9 = bf16[384,768]{1,0:T(8,128)(2,1)} collective-permute-done((bf16[384,768]{1,0:T(8,128)(2,1)}, bf16[384,768]{1,0:T(8,128)(2,1)}, u32[]{:S(2)}, u32[]{:S(2)}) %collective-permute-start.9) | collective-permute-done | bytes 589856 | tf_op jit(solution)/shard_map/ppermute | solution.py:68
  71.5 8.6 %collective-permute-done.12 = bf16[96,3072]{1,0:T(8,128)(2,1)S(1)} collective-permute-done((bf16[96,3072]{1,0:T(8,128)(2,1)}, bf16[96,3072]{1,0:T(8,128)(2,1)S(1)}, u32[]{:S(2)}, u32[]{:S(2)}) %collective-permute-start.12) | collective-permute-done | bytes 589856 | tf_op jit(solution)/shard_map/ppermute | solution.py:68
  80.2 4.1 collective-permute-start.1
  87.8 8.6 %collective-permute-done.5 = bf16[96,3072]{1,0:T(8,128)(2,1)S(1)} collective-permute-done((bf16[96,3072]{1,0:T(8,128)(2,1)S(1)}, bf16[96,3072]{1,0:T(8,128)(2,1)S(1)}, u32[]{:S(2)}, u32[]{:S(2)}) %collective-permute-start.5) | collective-permute-done | bytes 589856 | tf_op jit(solution)/shard_map/ppermute | solution.py:68
  98.7 18.6 %collective-permute-done = bf16[96,3200]{1,0:T(8,128)(2,1)S(1)} collective-permute-done((bf16[96,3200]{1,0:T(8,128)(2,1)S(1)}, bf16[96,3200]{1,0:T(8,128)(2,1)S(1)}, u32[]{:S(2)}, u32[]{:S(2)}) %collective-permute-start) | collective-permute-done | bytes 614432 | tf_op jit(solution)/shard_map/ppermute | solution.py:68
  126.9 5.6 maximum_select_fusion.1
  164.4 31.5 %all_to_all.10 = bf16[16,2,32,768]{3,2,1,0:T(8,128)(2,1)S(1)} all-to-all(bf16[16,2,32,768]{3,2,1,0:T(8,128)(2,1)S(1)} %pad_maximum_fusion.2), channel_id=1, replica_groups=mesh['x'=4,'core'=2,'z'=4,'y'=4] {'z','y'}, dimensions={0} | all-to-all | bytes 3145728 | tf_op jit(solution)/shard_map/all_to_all | solution.py:227
  202.4 23.5 %collective-permute-done.19 = bf16[768,384]{1,0:T(8,128)(2,1)S(1)} collective-permute-done((bf16[768,384]{1,0:T(8,128)(2,1)S(1)}, bf16[768,384]{1,0:T(8,128)(2,1)S(1)}, u32[]{:S(2)}, u32[]{:S(2)}) %collective-permute-start.19) | collective-permute-done | bytes 589856 | tf_op jit(solution)/shard_map/ppermute | solution.py:68
  229.7 21.1 %collective-permute-done.22 = bf16[384,768]{1,0:T(8,128)(2,1)S(1)} collective-permute-done((bf16[384,768]{1,0:T(8,128)(2,1)S(1)}, bf16[384,768]{1,0:T(8,128)(2,1)S(1)}, u32[]{:S(2)}, u32[]{:S(2)}) %collective-permute-start.22) | collective-permute-done | bytes 589856 | tf_op jit(solution)/shard_map/ppermute | solution.py:68
  251.5 6.5 %fusion.5 = bf16[1024,1536]{1,0:T(8,128)(2,1)S(1)} fusion(f32[1024,1536]{1,0:T(8,128)S(1)} %get-tuple-element.194, bf16[384,768]{1,0:T(8,128)(2,1)S(1)} %collective-permute-done.22, bf16[384,768]{1,0:T(8,128)(2,1)S(1)} %collective-permute-done.21, bf16[384,768]{1,0:T(8,128)(2,1)S(1)} %collective-permute-done.20, bf16[384,768]{1,0:T(8,128)(2,1)S(1)} %bitcast.501, ...), kind=kOutput, calls=%fused_computation.6 | convolution fusion | flops 2444230656 | bytes 13369344 | tf_op jit(solution)/shard_map/dot_general | solution.py:25
  266.3 4.2 reshape.569
  291.9 4.4 all-to-all-start.1
  304.4 9.2 %collective-permute-done.53 = bf16[768,384]{1,0:T(8,128)(2,1)} collective-permute-done((bf16[768,384]{1,0:T(8,128)(2,1)}, bf16[768,384]{1,0:T(8,128)(2,1)}, u32[]{:S(2)}, u32[]{:S(2)}) %collective-permute-start.53) | collective-permute-done | bytes 589856 | tf_op jit(solution)/shard_map/ppermute | solution.py:68
  374.3 3.7 fusion.11
  381.2 3.7 dynamic-slice_reduce_fusion.4
  411.6 4.3 collective-permute-done.35
  425.0 7.1 %collective-permute-done.29 = bf16[96,2304]{1,0:T(8,128)(2,1)S(1)} collective-permute-done((bf16[96,2304]{1,0:T(8,128)(2,1)S(1)}, bf16[96,2304]{1,0:T(8,128)(2,1)S(1)}, u32[]{:S(2)}, u32[]{:S(2)}) %collective-permute-start.29) | collective-permute-done | bytes 442400 | tf_op jit(solution)/shard_map/ppermute | solution.py:68
  433.1 9.3 %collective-permute-done.31 = bf16[96,2304]{1,0:T(8,128)(2,1)S(1)} collective-permute-done((bf16[96,2304]{1,0:T(8,128)(2,1)S(1)}, bf16[96,2304]{1,0:T(8,128)(2,1)S(1)}, u32[]{:S(2)}, u32[]{:S(2)}) %collective-permute-start.31) | collective-permute-done | bytes 442400 | tf_op jit(solution)/shard_map/ppermute | solution.py:68
  452.2 14.2 %collective-permute-done.47 = bf16[96,2304]{1,0:T(8,128)(2,1)S(1)} collective-permute-done((bf16[96,2304]{1,0:T(8,128)(2,1)S(1)}, bf16[96,2304]{1,0:T(8,128)(2,1)S(1)}, u32[]{:S(2)}, u32[]{:S(2)}) %collective-permute-start.47) | collective-permute-done | bytes 442400 | tf_op jit(solution)/shard_map/ppermute | solution.py:68
  466.8 6.4 collective-permute-done.41
  475.8 40.7 %collective-permute-done.43 = bf16[384,768]{1,0:T(8,128)(2,1)S(1)} collective-permute-done((bf16[384,768]{1,0:T(8,128)(2,1)S(1)}, bf16[384,768]{1,0:T(8,128)(2,1)S(1)}, u32[]{:S(2)}, u32[]{:S(2)}) %collective-permute-start.43) | collective-permute-done | bytes 589856 | tf_op jit(solution)/shard_map/ppermute | solution.py:68
  522.2 17.7 %collective-permute-done.55 = bf16[384,768]{1,0:T(8,128)(2,1)} collective-permute-done((bf16[384,768]{1,0:T(8,128)(2,1)}, bf16[384,768]{1,0:T(8,128)(2,1)}, u32[]{:S(2)}, u32[]{:S(2)}) %collective-permute-start.55) | collective-permute-done | bytes 589856 | tf_op jit(solution)/shard_map/ppermute | solution.py:68
  558.6 74.6 %psum.49 = bf16[96,128]{1,0:T(8,128)(2,1)S(1)} all-reduce(bf16[96,128]{1,0:T(8,128)(2,1)S(1)} %fusion.131), channel_id=1, replica_groups=mesh['x'=4,'core'=2,'z'=4,'y'=4] {'z','y'}, use_global_device_ids=true, to_apply=%region_34.35 | all-reduce | flops 12288 | bytes 49152 | tf_op jit(solution)/shard_map/psum | solution.py:363
  (555 shorter events, 275.5 us)
Async XLA Ops:
  10.6 74.9 %collective-permute-start.14 = (bf16[96,3072]{1,0:T(8,128)(2,1)}, bf16[96,3072]{1,0:T(8,128)(2,1)}, u32[]{:S(2)}, u32[]{:S(2)}) collective-permute-start(bf16[96,3072]{1,0:T(8,128)(2,1)} %constant_dynamic-update-slice_fusion), channel_id=1, source_target_pairs={{0,96},{32,0},{64,32},{96,64},{1,97},{33,1},{65,33},{97,65},{2,98}... | collective-permute-start | bytes 1769480 | tf_op jit(solution)/shard_map/ppermute | solution.py:68
  11.4 68.8 %collective-permute-start.13 = (bf16[96,3072]{1,0:T(8,128)(2,1)}, bf16[96,3072]{1,0:T(8,128)(2,1)}, u32[]{:S(2)}, u32[]{:S(2)}) collective-permute-start(bf16[96,3072]{1,0:T(8,128)(2,1)} %constant_dynamic-update-slice_fusion), channel_id=1, source_target_pairs={{0,64},{32,96},{64,0},{96,32},{1,65},{33,97},{65,1},{97,33},{2,66}... | collective-permute-start | bytes 1769480 | tf_op jit(solution)/shard_map/ppermute | solution.py:68
  14.6 50.5 %collective-permute-start.10 = (bf16[384,768]{1,0:T(8,128)(2,1)}, bf16[384,768]{1,0:T(8,128)(2,1)}, u32[]{:S(2)}, u32[]{:S(2)}) collective-permute-start(bf16[384,768]{1,0:T(8,128)(2,1)} %param.24), channel_id=1, source_target_pairs={{0,96},{32,0},{64,32},{96,64},{1,97},{33,1},{65,33},{97,65},{2,98}... | collective-permute-start | bytes 1769480 | tf_op jit(solution)/shard_map/ppermute | solution.py:68
  14.7 49.0 %collective-permute-start.9 = (bf16[384,768]{1,0:T(8,128)(2,1)}, bf16[384,768]{1,0:T(8,128)(2,1)}, u32[]{:S(2)}, u32[]{:S(2)}) collective-permute-start(bf16[384,768]{1,0:T(8,128)(2,1)} %param.24), channel_id=1, source_target_pairs={{0,64},{32,96},{64,0},{96,32},{1,65},{33,97},{65,1},{97,33},{2,66}... | collective-permute-start | bytes 1769480 | tf_op jit(solution)/shard_map/ppermute | solution.py:68
  65.1 32.2 %collective-permute-start.6 = (bf16[96,3072]{1,0:T(8,128)(2,1)S(1)}, bf16[96,3072]{1,0:T(8,128)(2,1)S(1)}, u32[]{:S(2)}, u32[]{:S(2)}) collective-permute-start(bf16[96,3072]{1,0:T(8,128)(2,1)S(1)} %copy-done.67), channel_id=1, source_target_pairs={{0,96},{32,0},{64,32},{96,64},{1,97},{33,1},{65,33},{97,65},{2,98}... | collective-permute-start | bytes 1769480 | tf_op jit(solution)/shard_map/ppermute | solution.py:68
  80.2 40.3 %collective-permute-start.2 = (bf16[96,3200]{1,0:T(8,128)(2,1)S(1)}, bf16[96,3200]{1,0:T(8,128)(2,1)S(1)}, u32[]{:S(2)}, u32[]{:S(2)}) collective-permute-start(bf16[96,3200]{1,0:T(8,128)(2,1)S(1)} %concatenate.54), channel_id=1, source_target_pairs={{0,96},{32,0},{64,32},{96,64},{1,97},{33,1},{65,33},{97,65},{2,98}... | collective-permute-start | bytes 1843208 | tf_op jit(solution)/shard_map/ppermute | solution.py:68
  80.2 40.1 %collective-permute-start.1 = (bf16[96,3200]{1,0:T(8,128)(2,1)S(1)}, bf16[96,3200]{1,0:T(8,128)(2,1)S(1)}, u32[]{:S(2)}, u32[]{:S(2)}) collective-permute-start(bf16[96,3200]{1,0:T(8,128)(2,1)S(1)} %concatenate.54), channel_id=1, source_target_pairs={{0,64},{32,96},{64,0},{96,32},{1,65},{33,97},{65,1},{97,33},{2,66}... | collective-permute-start | bytes 1843208 | tf_op jit(solution)/shard_map/ppermute | solution.py:68
  85.5 31.8 %collective-permute-start = (bf16[96,3200]{1,0:T(8,128)(2,1)S(1)}, bf16[96,3200]{1,0:T(8,128)(2,1)S(1)}, u32[]{:S(2)}, u32[]{:S(2)}) collective-permute-start(bf16[96,3200]{1,0:T(8,128)(2,1)S(1)} %concatenate.54), channel_id=1, source_target_pairs={{0,32},{32,64},{64,96},{96,0},{1,33},{33,65},{65,97},{97,1},{2,34}... | collective-permute-start | bytes 1843208 | tf_op jit(solution)/shard_map/ppermute | solution.py:68
  195.9 30.0 %collective-permute-start.19 = (bf16[768,384]{1,0:T(8,128)(2,1)S(1)}, bf16[768,384]{1,0:T(8,128)(2,1)S(1)}, u32[]{:S(2)}, u32[]{:S(2)}) collective-permute-start(bf16[768,384]{1,0:T(8,128)(2,1)S(1)} %bitcast.493), channel_id=1, source_target_pairs={{0,96},{32,0},{64,32},{96,64},{1,97},{33,1},{65,33},{97,65},{2,98}... | collective-permute-start | bytes 1769480 | tf_op jit(solution)/shard_map/ppermute | solution.py:68
  195.9 30.0 %collective-permute-start.18 = (bf16[768,384]{1,0:T(8,128)(2,1)S(1)}, bf16[768,384]{1,0:T(8,128)(2,1)S(1)}, u32[]{:S(2)}, u32[]{:S(2)}) collective-permute-start(bf16[768,384]{1,0:T(8,128)(2,1)S(1)} %bitcast.494), channel_id=1, source_target_pairs={{0,64},{32,96},{64,0},{96,32},{1,65},{33,97},{65,1},{97,33},{2,66}... | collective-permute-start | bytes 1769480 | tf_op jit(solution)/shard_map/ppermute | solution.py:68
  197.2 29.7 %collective-permute-start.17 = (bf16[768,384]{1,0:T(8,128)(2,1)S(1)}, bf16[768,384]{1,0:T(8,128)(2,1)S(1)}, u32[]{:S(2)}, u32[]{:S(2)}) collective-permute-start(bf16[768,384]{1,0:T(8,128)(2,1)S(1)} %bitcast.495), channel_id=1, source_target_pairs={{0,32},{32,64},{64,96},{96,0},{1,33},{33,65},{65,97},{97,1},{2,34}... | collective-permute-start | bytes 1769480 | tf_op jit(solution)/shard_map/ppermute | solution.py:68
  199.7 51.1 %collective-permute-start.22 = (bf16[384,768]{1,0:T(8,128)(2,1)S(1)}, bf16[384,768]{1,0:T(8,128)(2,1)S(1)}, u32[]{:S(2)}, u32[]{:S(2)}) collective-permute-start(bf16[384,768]{1,0:T(8,128)(2,1)S(1)} %bitcast.498), channel_id=1, source_target_pairs={{0,96},{32,0},{64,32},{96,64},{1,97},{33,1},{65,33},{97,65},{2,98}... | collective-permute-start | bytes 1769480 | tf_op jit(solution)/shard_map/ppermute | solution.py:68
  200.2 50.6 %collective-permute-start.21 = (bf16[384,768]{1,0:T(8,128)(2,1)S(1)}, bf16[384,768]{1,0:T(8,128)(2,1)S(1)}, u32[]{:S(2)}, u32[]{:S(2)}) collective-permute-start(bf16[384,768]{1,0:T(8,128)(2,1)S(1)} %bitcast.499), channel_id=1, source_target_pairs={{0,64},{32,96},{64,0},{96,32},{1,65},{33,97},{65,1},{97,33},{2,66}... | collective-permute-start | bytes 1769480 | tf_op jit(solution)/shard_map/ppermute | solution.py:68
  291.9 29.8 %all-to-all-start.1 = ((bf16[16,2,32,768]{3,2,1,0:T(8,128)(2,1)}), bf16[16,2,32,768]{3,2,1,0:T(8,128)(2,1)}, u32[]{:S(2)}, u32[]{:S(2)}) async-start(bf16[16,2,32,768]{3,2,1,0:T(8,128)(2,1)} %fusion.7), calls=%async_computation.1 | async-start | bytes 3145728 | tf_op jit(solution)/shard_map/all_to_all | solution.py:256
  296.3 338.4 %all-reduce.3.cloned.1.call-start = ((), (), s32[]{:S(2)}) async-start(), calls=%async_computation.2 | async-start | bytes 4718592 | tf_op jit(solution)/shard_map/psum | solution.py:363
  360.6 35.4 %collective-permute-start.48 = (bf16[384,768]{1,0:T(8,128)(2,1)}, bf16[384,768]{1,0:T(8,128)(2,1)}, u32[]{:S(2)}, u32[]{:S(2)}) collective-permute-start(bf16[384,768]{1,0:T(8,128)(2,1)} %convolution_convert_fusion.13), channel_id=1, source_target_pairs={{0,16},{16,0},{1,17},{17,1},{2,18},{18,2},{3,19},{19,3},{4,20},{20... | collective-permute-start | bytes 1769480 | tf_op jit(solution)/shard_map/ppermute | solution.py:72
  362.7 37.1 %collective-permute-start.32 = (bf16[384,768]{1,0:T(8,128)(2,1)}, bf16[384,768]{1,0:T(8,128)(2,1)}, u32[]{:S(2)}, u32[]{:S(2)}) collective-permute-start(bf16[384,768]{1,0:T(8,128)(2,1)} %convolution_convert_fusion.14), channel_id=1, source_target_pairs={{0,16},{16,0},{1,17},{17,1},{2,18},{18,2},{3,19},{19,3},{4,20},{20... | collective-permute-start | bytes 1769480 | tf_op jit(solution)/shard_map/ppermute | solution.py:72
  387.0 29.7 %collective-permute-start.28 = (bf16[384,2304]{1,0:T(8,128)(2,1)}, bf16[384,2304]{1,0:T(8,128)(2,1)}, u32[]{:S(2)}, u32[]{:S(2)}) collective-permute-start(bf16[384,2304]{1,0:T(8,128)(2,1)} %convolution_convert_fusion.2), channel_id=1, source_target_pairs={{0,16},{16,0},{1,17},{17,1},{2,18},{18,2},{3,19},{19,3},{4,20},{20... | collective-permute-start | bytes 5308424 | tf_op jit(solution)/shard_map/ppermute | solution.py:72
  411.6 36.3 %collective-permute-start.36 = (bf16[384,3072]{1,0:T(8,128)(2,1)S(1)}, bf16[384,3072]{1,0:T(8,128)(2,1)S(1)}, u32[]{:S(2)}, u32[]{:S(2)}) collective-permute-start(bf16[384,3072]{1,0:T(8,128)(2,1)S(1)} %copy-done.26), channel_id=1, source_target_pairs={{0,16},{16,0},{1,17},{17,1},{2,18},{18,2},{3,19},{19,3},{4,20},{20... | collective-permute-start | bytes 7077896 | tf_op jit(solution)/shard_map/ppermute | solution.py:72
  448.9 69.8 %collective-permute-start.37 = (bf16[96,3072]{1,0:T(8,128)(2,1)S(1)}, bf16[96,3072]{1,0:T(8,128)(2,1)S(1)}, u32[]{:S(2)}, u32[]{:S(2)}) collective-permute-start(bf16[96,3072]{1,0:T(8,128)(2,1)S(1)} %get-tuple-element.137), channel_id=1, source_target_pairs={{0,32},{32,64},{64,96},{96,0},{1,33},{33,65},{65,97},{97,1},{2,34}... | collective-permute-start | bytes 1769480 | tf_op jit(solution)/shard_map/ppermute | solution.py:68
  451.0 69.9 %collective-permute-start.39 = (bf16[96,3072]{1,0:T(8,128)(2,1)S(1)}, bf16[96,3072]{1,0:T(8,128)(2,1)S(1)}, u32[]{:S(2)}, u32[]{:S(2)}) collective-permute-start(bf16[96,3072]{1,0:T(8,128)(2,1)S(1)} %get-tuple-element.138), channel_id=1, source_target_pairs={{0,96},{32,0},{64,32},{96,64},{1,97},{33,1},{65,33},{97,65},{2,98}... | collective-permute-start | bytes 1769480 | tf_op jit(solution)/shard_map/ppermute | solution.py:68
  466.4 54.5 %collective-permute-start.38 = (bf16[96,3072]{1,0:T(8,128)(2,1)S(1)}, bf16[96,3072]{1,0:T(8,128)(2,1)S(1)}, u32[]{:S(2)}, u32[]{:S(2)}) collective-permute-start(bf16[96,3072]{1,0:T(8,128)(2,1)S(1)} %get-tuple-element.139), channel_id=1, source_target_pairs={{0,64},{32,96},{64,0},{96,32},{1,65},{33,97},{65,1},{97,33},{2,66}... | collective-permute-start | bytes 1769480 | tf_op jit(solution)/shard_map/ppermute | solution.py:68
  466.4 50.1 %collective-permute-start.43 = (bf16[384,768]{1,0:T(8,128)(2,1)S(1)}, bf16[384,768]{1,0:T(8,128)(2,1)S(1)}, u32[]{:S(2)}, u32[]{:S(2)}) collective-permute-start(bf16[384,768]{1,0:T(8,128)(2,1)S(1)} %get-tuple-element.135), channel_id=1, source_target_pairs={{0,96},{32,0},{64,32},{96,64},{1,97},{33,1},{65,33},{97,65},{2,98}... | collective-permute-start | bytes 1769480 | tf_op jit(solution)/shard_map/ppermute | solution.py:68
  473.2 43.4 %collective-permute-start.42 = (bf16[384,768]{1,0:T(8,128)(2,1)S(1)}, bf16[384,768]{1,0:T(8,128)(2,1)S(1)}, u32[]{:S(2)}, u32[]{:S(2)}) collective-permute-start(bf16[384,768]{1,0:T(8,128)(2,1)S(1)} %get-tuple-element.136), channel_id=1, source_target_pairs={{0,64},{32,96},{64,0},{96,32},{1,65},{33,97},{65,1},{97,33},{2,66}... | collective-permute-start | bytes 1769480 | tf_op jit(solution)/shard_map/ppermute | solution.py:68
  (156 other events, 2543.8 us)
Sparse Core Ops, SparseCore 0:
  522.2 91.6 all-reduce.2

commit v2 on v1

--- a/solution.py
+++ b/solution.py
@@ -3,6 +3,8 @@
 import jax
 import jax.numpy as jnp
 from jax import lax
+from jax.experimental import pallas as pl
+from jax.experimental.pallas import tpu as pltpu
 from jax.sharding import Mesh, PartitionSpec as P
 
 HEAD_DIM = 64
@@ -72,17 +74,70 @@
     return lax.ppermute(block, "core", [(0, 1), (1, 0)])
 
 
-def gather_rows(shard):
+def after(block, earlier):
+    return jnp.where(earlier == earlier, block, jnp.zeros_like(block))
+
+
+def mark(*blocks):
+    return sum(block[(0,) * block.ndim].astype(jnp.float32) for block in blocks)
+
+
+def place(spots, sources, shapes, moves):
+    kind = sources[0].dtype
+    blocks = [(n, k) for n, source in enumerate(sources) for k in range(source.shape[0])]
+    count = sum(len(listed) for listed in moves([0] * spots.shape[0]))
+    staged = 2 * sum(math.prod(source.shape) for source in sources)
+
+    def kernel(spots_ref, *refs):
+        ins, refs = refs[: len(sources)], refs[len(sources) :]
+        outs, refs = refs[: len(shapes)], refs[len(shapes) :]
+        stages, (in_sems, out_sems) = refs[: len(sources)], refs[len(sources) :]
+        loads = [
+            pltpu.make_async_copy(ins[n].at[k], stages[n].at[k], in_sems.at[at])
+            for at, (n, k) in enumerate(blocks)
+        ]
+        for load in loads:
+            load.start()
+        stores = []
+        listed = moves([spots_ref[k] for k in range(spots.shape[0])])
+        for load, (n, k), targets in zip(loads, blocks, listed):
+            load.wait()
+            for cut, at, spot in targets:
+                store = pltpu.make_async_copy(
+                    stages[n].at[(k,) + cut], outs[at].at[spot], out_sems.at[len(stores)]
+                )
+                store.start()
+                stores.append(store)
+        for store in stores:
+            store.wait()
+
+    return pl.pallas_call(
+        kernel,
+        out_shape=[jax.ShapeDtypeStruct(shape, kind) for shape in shapes],
+        in_specs=[pl.BlockSpec(memory_space=pltpu.SMEM)]
+        + [pl.BlockSpec(memory_space=pl.ANY)] * len(sources),
+        out_specs=[pl.BlockSpec(memory_space=pl.ANY)] * len(shapes),
+        scratch_shapes=[pltpu.VMEM(source.shape, kind) for source in sources]
+        + [pltpu.SemaphoreType.DMA((len(blocks),)), pltpu.SemaphoreType.DMA((count,))],
+        compiler_params=pltpu.CompilerParams(vmem_limit_bytes=staged + (2 << 20)),
+        cost_estimate=pl.CostEstimate(flops=0, bytes_accessed=2 * staged, transcendentals=0),
+    )(spots, *sources)
+
+
+def gather_pieces(shard):
+    return [shard] + [x_shift(shard, step) for step in range(1, X)]
+
+
+def both_cores(pieces, shapes, targets):
     xi, ci = lax.axis_index("x"), lax.axis_index("core")
-    half = jnp.zeros((X,) + shard.shape, shard.dtype)
-    half = lax.dynamic_update_index_in_dim(half, shard, xi, 0)
-    for step in range(1, X):
-        half = lax.dynamic_update_index_in_dim(half, x_shift(shard, step), (xi - step) % X, 0)
-    other = core_swap(half)
-    whole = jnp.where(
-        ci == 0, jnp.stack([half, other], axis=1), jnp.stack([other, half], axis=1)
-    )
-    return whole.reshape(X * CORES * shard.shape[0], shard.shape[1])
+    own = jnp.stack(pieces)
+    spots = [((xi - k) % X) * CORES + (ci if mine else 1 - ci) for mine in (1, 0) for k in range(X)]
+    return place(
+        jnp.stack(spots).astype(jnp.int32),
+        [own, core_swap(own)],
+        shapes,
+        lambda spots: [targets(spot) for spot in spots],
+    )
 
 
 def split_rows(left):
@@ -95,23 +150,48 @@
     return own.reshape(wide // CORES, rows), other.reshape(wide // CORES, rows)
 
 
-def sum_over_x(first, blocks, sign):
-    total = first
-    for step in range(1, X):
-        total = total + x_shift(blocks[step - 1], sign * step).astype(jnp.float32)
-    return total
-
-
-def scatter_halves(own, other):
-    total = own + core_swap(other.astype(jnp.bfloat16)).astype(jnp.float32)
-    block = own.shape[0] // X
-    low = total[block:].astype(jnp.bfloat16)
-    return sum_over_x(total[:block], [low[k * block : (k + 1) * block] for k in range(X - 1)], 1)
+def scatter_halves(own, other, before=None):
+    block = own[0].shape[0] // X
+    starts = [sum(part.shape[1] for part in own[:k]) for k in range(len(own))]
+    got = core_swap(jnp.concatenate([part.astype(jnp.bfloat16) for part in other], axis=1))
+    totals = [
+        part + got[:, start : start + part.shape[1]].astype(jnp.float32)
+        for part, start in zip(own, starts)
+    ]
+    low = jnp.concatenate([t[block:].astype(jnp.bfloat16) for t in totals], axis=1)
+    if before is not None:
+        low = after(low, before)
+    arrived = [x_shift(low[(k - 1) * block : k * block], k) for k in range(1, X)]
+    sums = []
+    for t, start in zip(totals, starts):
+        cut = slice(start, start + t.shape[1])
+        sums.append(t[:block] + sum(a[:, cut].astype(jnp.float32) for a in arrived))
+    return sums, mark(*arrived)
+
+
+def scatter_dense(up, down):
+    (up_own, up_other), (down_own, down_other) = up, down
+    width = down_own.shape[1]
+    depth, deep = up_own.shape[0] // X, down_own.shape[0] // X
+    stripes = up_own.shape[1] // width
+    up_total = up_own + core_swap(up_other.astype(jnp.bfloat16)).astype(jnp.float32)
+    down_total = down_own + core_swap(down_other.astype(jnp.bfloat16)).astype(jnp.float32)
+    arrived = []
+    for k in range(1, X):
+        up_low = up_total[k * depth : (k + 1) * depth].astype(jnp.bfloat16)
+        down_low = down_total[k * deep : (k + 1) * deep].astype(jnp.bfloat16)
+        pack = [up_low[:, n * width : (n + 1) * width] for n in range(stripes)] + [down_low]
+        arrived.append(x_shift(jnp.concatenate(pack, axis=0), k))
+    total = sum(a.astype(jnp.float32) for a in arrived)
+    up_sum = up_total[:depth] + jnp.concatenate(
+        [total[n * depth : (n + 1) * depth] for n in range(stripes)], axis=1
+    )
+    return up_sum, down_total[:deep] + total[stripes * depth :], mark(*arrived)
 
 
 def weight_grad(left, right):
     own, other = split_rows(left)
-    return scatter_halves(product(own, right), product(other, right))
+    return product(own, right), product(other, right)
 
 
 def attend_forward(stream, gain, in_proj, out_proj, images, length):
@@ -189,17 +269,13 @@
     return (grad + stream_grad, (gain_grad, up_grad, down_grad))
 
 
-def moe(stream, grad_low, gain, router, up_local, down_local, routes, slot_index, keep_mask):
+def moe(stream, grad_low, gain, router, up_half, down_half, ready, routes, slot_index, keep_mask):
     rows, width = stream.shape
     experts = router.shape[1]
     slots = experts * SLOTS
-    hidden_local = up_local.shape[1]
+    hidden_local = up_half.shape[1] // X
     grad = grad_low.astype(jnp.float32)
-    ups = [up_local] + [x_shift(up_local, k) for k in range(1, X)]
-    downs = [down_local] + [x_shift(down_local, k) for k in range(1, X)]
-    up_half = jnp.concatenate(ups, axis=1)
-    down_half = jnp.concatenate(downs, axis=0)
-
+    half = width // 2
     normed_f, saved = norm_rows(stream, gain)
     normed = normed_f.astype(jnp.bfloat16)
     logits = product(normed, router)
@@ -221,47 +297,47 @@
     slot_gate = jnp.sum(pick_first * gate_first + pick_second * gate_second, axis=0)
     send_rows = product_t(select, normed).astype(jnp.bfloat16)
     send_grad = (product_t(select, grad_low) * slot_gate[:, None]).astype(jnp.bfloat16)
-    send = jnp.stack(
+    send = jnp.concatenate(
         [send_rows.reshape(experts, SLOTS, width), send_grad.reshape(experts, SLOTS, width)], axis=1
     )
+    send = after(send, ready)
     received = lax.all_to_all(send, ("z", "y"), split_axis=0, concat_axis=0, tiled=True)
     partner = core_swap(received)
 
-    flat = jnp.concatenate(
-        [received[:, 0].reshape(slots, width), partner[:, 0].reshape(slots, width)], axis=0
-    )
-    flat_grad = jnp.concatenate(
-        [received[:, 1].reshape(slots, width), partner[:, 1].reshape(slots, width)], axis=0
-    )
+    flat = jnp.concatenate([received[:, :SLOTS], partner[:, :SLOTS]], axis=0).reshape(-1, width)
+    flat_grad = jnp.concatenate([received[:, SLOTS:], partner[:, SLOTS:]], axis=0).reshape(-1, width)
     hidden, slope = gelu_parts(product(flat, up_half))
     hidden = hidden.astype(jnp.bfloat16)
     partial_out = product(hidden, down_half)
+    got_out = core_swap(partial_out[slots:].astype(jnp.bfloat16))
     pre_grad = (product_bt(flat_grad, down_half) * slope).astype(jnp.bfloat16)
     partial_in = product_bt(pre_grad, up_half)
-    other_half = jnp.stack(
-        [
-            partial_out[slots:].astype(jnp.bfloat16).reshape(experts, SLOTS, width),
-            partial_in[slots:].astype(jnp.bfloat16).reshape(experts, SLOTS, width),
-        ],
-        axis=1,
-    )
-    own_half = jnp.stack(
-        [
-            partial_out[:slots].reshape(experts, SLOTS, width),
-            partial_in[:slots].reshape(experts, SLOTS, width),
-        ],
-        axis=1,
-    )
-    back = (own_half + core_swap(other_half).astype(jnp.float32)).astype(jnp.bfloat16)
+    got_in = core_swap(partial_in[slots:].astype(jnp.bfloat16))
+    result = (partial_out[:slots] + got_out.astype(jnp.float32)).astype(jnp.bfloat16)
+    in_grad = (partial_in[:slots] + got_in.astype(jnp.float32)).astype(jnp.bfloat16)
+    back = jnp.concatenate(
+        [result.reshape(experts, SLOTS, width), in_grad.reshape(experts, SLOTS, width)], axis=1
+    )
     returned = lax.all_to_all(back, ("z", "y"), split_axis=0, concat_axis=0, tiled=True)
-    result_rows = returned[:, 0].reshape(slots, width)
-    back_rows = returned[:, 1].reshape(slots, width)
+    result_rows = returned[:, :SLOTS].reshape(slots, width)
+    back_rows = returned[:, SLOTS:].reshape(slots, width)
 
     cuts = [slice(k * hidden_local, (k + 1) * hidden_local) for k in range(X)]
     up_parts = [product_t(flat, pre_grad[:, cut]) for cut in cuts]
     down_parts = [product_t(hidden[:, cut], flat_grad) for cut in cuts]
-    up_grad = sum_over_x(up_parts[0], [p.astype(jnp.bfloat16) for p in up_parts[1:]], -1)
-    down_grad = sum_over_x(down_parts[0], [p.astype(jnp.bfloat16) for p in down_parts[1:]], -1)
+    arrived = []
+    for k in range(1, X):
+        low_up = up_parts[k].astype(jnp.bfloat16)
+        pack = jnp.concatenate(
+            [low_up[:half], low_up[half:], down_parts[k].astype(jnp.bfloat16)], axis=1
+        )
+        arrived.append(x_shift(pack, -k))
+    total = sum(a.astype(jnp.float32) for a in arrived)
+    up_grad = up_parts[0] + jnp.concatenate(
+        [total[:, :hidden_local], total[:, hidden_local : 2 * hidden_local]], axis=0
+    )
+    down_grad = down_parts[0] + total[:, 2 * hidden_local :]
+    sent = mark(*arrived)
 
     first = product(pick_first.astype(jnp.bfloat16), result_rows)
     second = product(pick_second.astype(jnp.bfloat16), result_rows)
@@ -274,7 +350,7 @@
     router_grad = product_t(normed, logit_grad)
     normed_grad = product_bt(logit_grad, router) + product(select, back_rows)
     stream_grad, gain_grad = norm_back(normed_grad, gain, saved)
-    return (new_stream, grad + stream_grad, (gain_grad, router_grad, up_grad, down_grad))
+    return (new_stream, grad + stream_grad, (gain_grad, router_grad, up_grad, down_grad), sent)
 
 
 def shards(
@@ -313,33 +389,101 @@
         axis=1,
     )
     wide_in, wide_out = in_proj_a.shape[1], out_proj_a.shape[1]
-    first = gather_rows(jnp.concatenate([in_proj_a, out_proj_a, small], axis=1))
-    in_aa, out_aa = first[:, :wide_in], first[:, wide_in : wide_in + wide_out]
-    small_all = first[:, wide_in + wide_out :]
+    blocks, depth = X * CORES, in_proj_a.shape[0]
+    every = slice(None)
+
+    def side_by_side(widths):
+        starts = [sum(widths[:at]) for at in range(len(widths))]
+        return lambda spot: [
+            ((every, pl.ds(start, wide)), at, (spot,))
+            for at, (start, wide) in enumerate(zip(starts, widths))
+        ]
+
+    pieces = gather_pieces(jnp.concatenate([in_proj_a, out_proj_a, small], axis=1))
+    reached = mark(*pieces[1:])
+    widths = [wide_in, wide_out, 128]
+    in_aa, out_aa, small_all = both_cores(
+        pieces, [(blocks, depth, wide) for wide in widths], side_by_side(widths)
+    )
+    in_aa, out_aa, small_all = (w.reshape(width, -1) for w in (in_aa, out_aa, small_all))
     gain_aa, gain_dd, gain_bb, gain_mm = (small_all[:, k] for k in range(4))
     router_full = small_all[:, 4 : 4 + experts]
-    up_dd = gather_rows(dense_up)
-    down_dd = gather_rows(dense_down)
-    second = gather_rows(jnp.concatenate([in_proj_b, out_proj_b], axis=1))
-    in_bb, out_bb = second[:, :wide_in], second[:, wide_in:]
+
+    stripes = dense_up.shape[1] // width
+    high = stripes * depth
+    pieces = gather_pieces(
+        after(
+            jnp.concatenate(
+                [dense_up[:, k * width : (k + 1) * width] for k in range(stripes)] + [dense_down], axis=0
+            ),
+            reached,
+        )
+    )
+    reached = mark(*pieces[1:])
+    (up_dd,) = both_cores(
+        [piece[:high] for piece in pieces],
+        [(blocks, depth, stripes * width)],
+        lambda spot: [
+            ((pl.ds(k * depth, depth), every), 0, (spot, every, pl.ds(k * width, width)))
+            for k in range(stripes)
+        ],
+    )
+    (down_dd,) = both_cores(
+        [piece[high:] for piece in pieces],
+        [(blocks, dense_down.shape[0], width)],
+        lambda spot: [((every, every), 0, (spot,))],
+    )
+    up_dd, down_dd = up_dd.reshape(width, -1), down_dd.reshape(-1, width)
+
+    pieces = gather_pieces(after(jnp.concatenate([in_proj_b, out_proj_b], axis=1), reached))
+    widths = [wide_in, wide_out]
+    in_bb, out_bb = both_cores(
+        pieces, [(blocks, depth, wide) for wide in widths], side_by_side(widths)
+    )
+    in_bb, out_bb = in_bb.reshape(width, -1), out_bb.reshape(width, -1)
+
+    up_local, down_local = expert_up[0], expert_down[0]
+    half, units = width // 2, up_local.shape[1]
+    packs = gather_pieces(
+        after(jnp.concatenate([up_local[:half], up_local[half:], down_local], axis=1), reached)
+    )
+
+    def unpack(k):
+        parts = [
+            ((every, pl.ds(part * units, units)), 0, (pl.ds(part * half, half), pl.ds(k * units, units)))
+            for part in range(2)
+        ]
+        return parts + [((every, pl.ds(2 * units, width)), 1, (pl.ds(k * units, units),))]
+
+    up_half, down_half = place(
+        jnp.zeros((1,), jnp.int32),
+        [pack[None] for pack in packs],
+        [(width, X * units), (X * units, width)],
+        lambda _: [unpack(k) for k in range(X)],
+    )
 
     stream_one, kept_one = attend_forward(stream, gain_aa, in_aa, out_aa, images, length)
     stream_two, kept_two = dense_forward(stream_one, gain_dd, up_dd, down_dd)
     stream_three, kept_three = attend_forward(stream_two, gain_bb, in_bb, out_bb, images, length)
-    stream_four, grad, moe_grads = moe(
+    stream_four, grad, moe_grads, sent = moe(
         stream_three,
         output_grad.reshape(rows, width),
         gain_mm,
         router_full,
-        expert_up[0],
-        expert_down[0],
+        up_half,
+        down_half,
+        mark(*packs[1:]),
         flat_routes,
         flat_slots,
         flat_keep,
     )
     output = stream_four.astype(jnp.bfloat16).reshape(images, length, width)
     grad, attn_b_grads = attend_backward(grad, gain_bb, in_bb, out_bb, kept_three, images, length)
+    (in_b, out_b), sent_b = scatter_halves(*zip(attn_b_grads[1], attn_b_grads[2]))
+    grad = after(grad, sent)
     grad, dense_grads = dense_backward(grad, gain_dd, up_dd, down_dd, kept_two)
+    up, down, sent_d = scatter_dense(dense_grads[1], dense_grads[2])
+    grad = after(grad, sent_b)
     grad, attn_a_grads = attend_backward(grad, gain_aa, in_aa, out_aa, kept_one, images, length)
     input_grad = grad.reshape(images, length, width)
     small_grad = jnp.concatenate(
@@ -350,18 +494,13 @@
         ],
         axis=0,
     )
-    small_share = scatter_halves(*split_rows(small_grad))
-    shares = [
-        attn_a_grads[1],
-        attn_a_grads[2],
-        dense_grads[1],
-        dense_grads[2],
-        attn_b_grads[1],
-        attn_b_grads[2],
-        small_share,
-    ]
+    (in_a, out_a, small_share), _ = scatter_halves(
+        *zip(attn_a_grads[1], attn_a_grads[2], split_rows(small_grad)), before=sent_d
+    )
+    shares = [in_a, jnp.concatenate([out_a, small_share], axis=1), up, down, in_b, out_b]
     totals = lax.psum([share.astype(jnp.bfloat16) for share in shares], ("z", "y"))
-    in_a, out_a, up, down, in_b, out_b, small_total = [t.astype(jnp.float32) for t in totals]
+    in_a, out_a, up, down, in_b, out_b = [t.astype(jnp.float32) for t in totals]
+    out_a, small_total = out_a[:, :wide_out], out_a[:, wide_out:]
     return (
         output,
         input_grad,

time: 661 us -> 714 us (1.080)
  waiting for transfers between devices: 240 us -> 321 us
  blocking collectives: 106 us -> 31.3 us
  local copies, waits for them, and re-layouts: 77.5 us -> 106 us
  starting transfers between devices: 62.4 us -> 37.6 us
  other arithmetic: 44.9 us -> 65.6 us
  Pallas kernels: 0 us -> 15 us
  between operations: 16.6 us -> 29 us
    psum x1, waiting for transfers between devices: 0.01 us -> 78.4 us  [shards(): lax.psum([share.astype(jnp.bfloat16) for share in shares], ('z', 'y'))]
    psum x1 -> x0, blocking collectives: 74.6 us -> none  [shards(): lax.psum([share.astype(jnp.bfloat16) for share in shares], ('z', 'y'))]
    slice x16 -> x39, local copies, waits for them, and re-layouts: 2.37 us -> 28.3 us  [the longest x18 14.2 us: mark(): block[(0,) * block.ndim].astype(jnp.float32)]
    ppermute x45 -> x24, starting transfers between devices: 55.6 us -> 30.8 us  [x_shift(): return lax.ppermute(block, 'x', [(i, (i + step) % X) for i in range(X)])]
    pallas_call x0 -> x5, Pallas kernels: none -> 15 us  [place(): pl.pallas_call(kernel, out_shape=[jax.ShapeDtypeStruct(shape, kind) for s...]
    unnamed x247 -> x368, local copies, waits for them, and re-layouts: 18.3 us -> 32.5 us
    concatenate x0 -> x9, other arithmetic: none -> 12.8 us  [the longest x3 5.76 us: moe(): jnp.concatenate([low_up[:half], low_up[half:], down_parts[k].astype(jnp.b...]
    dynamic_update_slice x16 -> x0, local copies, waits for them, and re-layouts: 10.5 us -> none  [the longest x12 8.32 us: gather_rows(): lax.dynamic_update_index_in_dim(half, x_shift(shard, step), (xi - step) %...]
  transfers between devices with their start and end apart: 60 -> 37, of which waited for: 29 -> 15; matrix products, arithmetic and copies ran while one was open for 19% -> 21% of each run, Pallas kernels for 0% -> 2%
where the time goes in v2:
time: 714 us; the launch traced here: 705 us
  waiting for transfers between devices  321 us (45%)
  local copies, waits for them, and re-layouts  106 us (15%)
  matrix products  99.5 us (14%)
  other arithmetic  65.6 us (9%)
  starting transfers between devices  37.6 us (5%)
  blocking collectives  31.3 us (4%)
  between operations  29 us (4%)
  Pallas kernels  15 us (2%)
    ppermute x24, waiting for transfers between devices, x_shift(): return lax.ppermute(block, 'x', [(i, (i + step) % X) for i in range(X)])  241 us
    psum x1, waiting for transfers between devices, shards(): lax.psum([share.astype(jnp.bfloat16) for share in shares], ('z', 'y'))  78.4 us
    dot_general x24, matrix products, product(): return jnp.dot(left, right, preferred_element_type=jnp.float32)  45.4 us
    unnamed x368, local copies, waits for them, and re-layouts  32.5 us
    all_to_all x1, blocking collectives, moe(): lax.all_to_all(send, ('z', 'y'), split_axis=0, concat_axis=0, tiled=True)  31.3 us
    ppermute x24, starting transfers between devices, x_shift(): return lax.ppermute(block, 'x', [(i, (i + step) % X) for i in range(X)])  30.8 us
    dot_general x11, matrix products, product_t(): lax.dot_general(left, right, (((0,), (0,)), ((), ())), preferred_element_...  20.5 us
    dot_general x9, matrix products, product_bt(): lax.dot_general(left, right, (((1,), (1,)), ((), ())), preferred_element_...  18.8 us
  transfers between devices with their start and end apart: 37, of which 15 were waited for; matrix products, arithmetic and copies ran while one was open for 21% of the time, Pallas kernels for 2%

profile of v2, /device:TPU:6, one launch (start us, length us, event | category | flops | bytes accessed | tf_op | source)
XLA Modules:
  0.0 704.8 jit_solution(1882791029030815083)
XLA Ops:
  26.1 17.1 %collective-permute-done = bf16[96,3200]{1,0:T(8,128)(2,1)} collective-permute-done((bf16[96,3200]{1,0:T(8,128)(2,1)S(1)}, bf16[96,3200]{1,0:T(8,128)(2,1)}, u32[]{:S(2)}, u32[]{:S(2)}) %collective-permute-start) | collective-permute-done | bytes 614432 | tf_op jit(solution)/shard_map/ppermute | solution.py:70
  48.4 3.3 collective-permute-start.5
  54.7 47.7 %collective-permute-done.4 = bf16[768,768]{1,0:T(8,128)(2,1)S(1)} collective-permute-done((bf16[768,768]{1,0:T(8,128)(2,1)S(1)}, bf16[768,768]{1,0:T(8,128)(2,1)S(1)}, u32[]{:S(2)}, u32[]{:S(2)}) %collective-permute-start.4) | collective-permute-done | bytes 1179680 | tf_op jit(solution)/shard_map/ppermute | solution.py:70
  112.7 9.5 %collective-permute-done.11 = bf16[96,3072]{1,0:T(8,128)(2,1)S(1)} collective-permute-done((bf16[96,3072]{1,0:T(8,128)(2,1)S(1)}, bf16[96,3072]{1,0:T(8,128)(2,1)S(1)}, u32[]{:S(2)}, u32[]{:S(2)}) %collective-permute-start.11) | collective-permute-done | bytes 589856 | tf_op jit(solution)/shard_map/ppermute | solution.py:70
  123.1 14.0 %collective-permute-done.10 = bf16[96,3072]{1,0:T(8,128)(2,1)S(1)} collective-permute-done((bf16[96,3072]{1,0:T(8,128)(2,1)S(1)}, bf16[96,3072]{1,0:T(8,128)(2,1)S(1)}, u32[]{:S(2)}, u32[]{:S(2)}) %collective-permute-start.10) | collective-permute-done | bytes 589856 | tf_op jit(solution)/shard_map/ppermute | solution.py:70
  140.6 45.6 %collective-permute-done.9 = bf16[96,3072]{1,0:T(8,128)(2,1)S(1)} collective-permute-done((bf16[96,3072]{1,0:T(8,128)(2,1)S(1)}, bf16[96,3072]{1,0:T(8,128)(2,1)S(1)}, u32[]{:S(2)}, u32[]{:S(2)}) %collective-permute-start.9) | collective-permute-done | bytes 589856 | tf_op jit(solution)/shard_map/ppermute | solution.py:70
  216.4 4.4 shard_map.290
  242.8 31.3 %all_to_all.10 = bf16[16,64,768]{2,1,0:T(8,128)(2,1)S(1)} all-to-all(bf16[16,64,768]{2,1,0:T(8,128)(2,1)S(1)} %maximum_select_fusion.1), channel_id=1, replica_groups=mesh['x'=4,'core'=2,'z'=4,'y'=4] {'z','y'}, dimensions={0} | all-to-all | bytes 3145728 | tf_op jit(solution)/shard_map/all_to_all | solution.py:304
  278.0 3.6 multiply_convert_fusion
  286.1 5.2 fusion.5
  309.7 3.7 collective-permute-start.24
  324.0 4.4 all-to-all-start.1
  338.5 24.9 %collective-permute-done.24 = bf16[384,1536]{1,0:T(8,128)(2,1)} collective-permute-done((bf16[384,1536]{1,0:T(8,128)(2,1)}, bf16[384,1536]{1,0:T(8,128)(2,1)}, u32[]{:S(2)}, u32[]{:S(2)}) %collective-permute-start.24) | collective-permute-done | bytes 1179680 | tf_op jit(solution)/shard_map/ppermute | solution.py:70
  392.6 3.5 dynamic-slice_reduce_fusion.4
  406.1 3.5 convolution_convert_fusion
  410.5 4.1 reshape.759
  438.1 4.7 fusion.158
  445.3 5.6 fusion.177
  456.3 9.5 %collective-permute-done.22 = bf16[96,3072]{1,0:T(8,128)(2,1)S(1)} collective-permute-done((bf16[96,3072]{1,0:T(8,128)(2,1)S(1)}, bf16[96,3072]{1,0:T(8,128)(2,1)S(1)}, u32[]{:S(2)}, u32[]{:S(2)}) %collective-permute-start.22) | collective-permute-done | bytes 589856 | tf_op jit(solution)/shard_map/ppermute | solution.py:70
  503.8 45.4 %collective-permute-done.29 = bf16[768,768]{1,0:T(8,128)(2,1)} collective-permute-done((bf16[768,768]{1,0:T(8,128)(2,1)}, bf16[768,768]{1,0:T(8,128)(2,1)}, u32[]{:S(2)}, u32[]{:S(2)}) %collective-permute-start.29) | collective-permute-done | bytes 1179680 | tf_op jit(solution)/shard_map/ppermute | solution.py:70
  565.0 4.8 collective-permute-start.33
  572.2 11.2 %collective-permute-done.34 = bf16[96,3200]{1,0:T(8,128)(2,1)S(1)} collective-permute-done((bf16[96,3200]{1,0:T(8,128)(2,1)S(1)}, bf16[96,3200]{1,0:T(8,128)(2,1)S(1)}, u32[]{:S(2)}, u32[]{:S(2)}) %collective-permute-start.34) | collective-permute-done | bytes 614432 | tf_op jit(solution)/shard_map/ppermute | solution.py:70
  583.4 11.5 %collective-permute-done.33 = bf16[96,3200]{1,0:T(8,128)(2,1)S(1)} collective-permute-done((bf16[96,3200]{1,0:T(8,128)(2,1)S(1)}, bf16[96,3200]{1,0:T(8,128)(2,1)S(1)}, u32[]{:S(2)}, u32[]{:S(2)}) %collective-permute-start.33) | collective-permute-done | bytes 614432 | tf_op jit(solution)/shard_map/ppermute | solution.py:70
  608.5 78.4 %all-reduce.3.cloned.1.call-done = (bf16[96,896]{1,0:T(8,128)(2,1)}, bf16[96,2304]{1,0:T(8,128)(2,1)}, bf16[96,3072]{1,0:T(8,128)(2,1)}, bf16[384,768]{1,0:T(8,1...) async-done(((bf16[96,896]{1,0:T(8,128)(2,1)}, bf16[96,2304]{1,0:T(8,128)(2,1)}, bf16[96,3072]{1,0:T(8,128)(2,1)}, bf16[384,768]{1,0:T(8,128)(2,1)}, ...) | async-done | bytes 2383888 | tf_op jit(solution)/shard_map/psum | solution.py:501
  (657 shorter events, 279.0 us)
Async XLA Ops:
  12.4 33.8 %collective-permute-start.2 = (bf16[96,3200]{1,0:T(8,128)(2,1)S(1)}, bf16[96,3200]{1,0:T(8,128)(2,1)S(1)}, u32[]{:S(2)}, u32[]{:S(2)}) collective-permute-start(bf16[96,3200]{1,0:T(8,128)(2,1)S(1)} %concatenate.124), channel_id=1, source_target_pairs={{0,96},{32,0},{64,32},{96,64},{1,97},{33,1},{65,33},{97,65},{2,98}... | collective-permute-start | bytes 1843208 | tf_op jit(solution)/shard_map/ppermute | solution.py:70
  13.3 31.1 %collective-permute-start.1 = (bf16[96,3200]{1,0:T(8,128)(2,1)S(1)}, bf16[96,3200]{1,0:T(8,128)(2,1)S(1)}, u32[]{:S(2)}, u32[]{:S(2)}) collective-permute-start(bf16[96,3200]{1,0:T(8,128)(2,1)S(1)} %concatenate.124), channel_id=1, source_target_pairs={{0,64},{32,96},{64,0},{96,32},{1,65},{33,97},{65,1},{97,33},{2,66}... | collective-permute-start | bytes 1843208 | tf_op jit(solution)/shard_map/ppermute | solution.py:70
  47.6 57.2 %collective-permute-start.6 = (bf16[768,768]{1,0:T(8,128)(2,1)S(1)}, bf16[768,768]{1,0:T(8,128)(2,1)S(1)}, u32[]{:S(2)}, u32[]{:S(2)}) collective-permute-start(bf16[768,768]{1,0:T(8,128)(2,1)S(1)} %broadcast_select_fusion), channel_id=1, source_target_pairs={{0,96},{32,0},{64,32},{96,64},{1,97},{33,1},{65,33},{97,65},{2,98}... | collective-permute-start | bytes 3538952 | tf_op jit(solution)/shard_map/ppermute | solution.py:70
  48.4 54.5 %collective-permute-start.5 = (bf16[768,768]{1,0:T(8,128)(2,1)S(1)}, bf16[768,768]{1,0:T(8,128)(2,1)S(1)}, u32[]{:S(2)}, u32[]{:S(2)}) collective-permute-start(bf16[768,768]{1,0:T(8,128)(2,1)S(1)} %broadcast_select_fusion), channel_id=1, source_target_pairs={{0,64},{32,96},{64,0},{96,32},{1,65},{33,97},{65,1},{97,33},{2,66}... | collective-permute-start | bytes 3538952 | tf_op jit(solution)/shard_map/ppermute | solution.py:70
  51.7 50.7 %collective-permute-start.4 = (bf16[768,768]{1,0:T(8,128)(2,1)S(1)}, bf16[768,768]{1,0:T(8,128)(2,1)S(1)}, u32[]{:S(2)}, u32[]{:S(2)}) collective-permute-start(bf16[768,768]{1,0:T(8,128)(2,1)S(1)} %broadcast_select_fusion), channel_id=1, source_target_pairs={{0,32},{32,64},{64,96},{96,0},{1,33},{33,65},{65,97},{97,1},{2,34}... | collective-permute-start | bytes 3538952 | tf_op jit(solution)/shard_map/ppermute | solution.py:70
  54.5 137.8 %collective-permute-start.3 = (bf16[4,96,3200]{2,1,0:T(8,128)(2,1)S(1)}, bf16[4,96,3200]{2,1,0:T(8,128)(2,1)S(1)}, u32[]{:S(2)}, u32[]{:S(2)}) collective-permute-start(bf16[4,96,3200]{2,1,0:T(8,128)(2,1)S(1)} %pad_maximum_fusion.refs_0_), channel_id=1, source_target_pairs={{0,16},{16,0},{1,17},{17,1},{2,18},{18,2},{3,19},{19,3},{4,20},{20... | collective-permute-start | bytes 7372808 | tf_op jit(solution)/shard_map/ppermute | solution.py:74
  106.9 30.2 %collective-permute-start.10 = (bf16[96,3072]{1,0:T(8,128)(2,1)S(1)}, bf16[96,3072]{1,0:T(8,128)(2,1)S(1)}, u32[]{:S(2)}, u32[]{:S(2)}) collective-permute-start(bf16[96,3072]{1,0:T(8,128)(2,1)S(1)} %maximum_select_fusion.5), channel_id=1, source_target_pairs={{0,64},{32,96},{64,0},{96,32},{1,65},{33,97},{65,1},{97,33},{2,66}... | collective-permute-start | bytes 1769480 | tf_op jit(solution)/shard_map/ppermute | solution.py:70
  110.4 77.5 %collective-permute-start.13 = (bf16[384,1536]{1,0:T(8,128)(2,1)S(1)}, bf16[384,1536]{1,0:T(8,128)(2,1)S(1)}, u32[]{:S(2)}, u32[]{:S(2)}) collective-permute-start(bf16[384,1536]{1,0:T(8,128)(2,1)S(1)} %maximum_select_fusion.2), channel_id=1, source_target_pairs={{0,32},{32,64},{64,96},{96,0},{1,33},{33,65},{65,97},{97,1},{2,34}... | collective-permute-start | bytes 3538952 | tf_op jit(solution)/shard_map/ppermute | solution.py:70
  110.5 78.4 %collective-permute-start.14 = (bf16[384,1536]{1,0:T(8,128)(2,1)S(1)}, bf16[384,1536]{1,0:T(8,128)(2,1)S(1)}, u32[]{:S(2)}, u32[]{:S(2)}) collective-permute-start(bf16[384,1536]{1,0:T(8,128)(2,1)S(1)} %maximum_select_fusion.2), channel_id=1, source_target_pairs={{0,64},{32,96},{64,0},{96,32},{1,65},{33,97},{65,1},{97,33},{2,66}... | collective-permute-start | bytes 3538952 | tf_op jit(solution)/shard_map/ppermute | solution.py:70
  122.2 68.8 %collective-permute-start.15 = (bf16[384,1536]{1,0:T(8,128)(2,1)S(1)}, bf16[384,1536]{1,0:T(8,128)(2,1)S(1)}, u32[]{:S(2)}, u32[]{:S(2)}) collective-permute-start(bf16[384,1536]{1,0:T(8,128)(2,1)S(1)} %maximum_select_fusion.2), channel_id=1, source_target_pairs={{0,96},{32,0},{64,32},{96,64},{1,97},{33,1},{65,33},{97,65},{2,98}... | collective-permute-start | bytes 3538952 | tf_op jit(solution)/shard_map/ppermute | solution.py:70
  137.1 49.1 %collective-permute-start.9 = (bf16[96,3072]{1,0:T(8,128)(2,1)S(1)}, bf16[96,3072]{1,0:T(8,128)(2,1)S(1)}, u32[]{:S(2)}, u32[]{:S(2)}) collective-permute-start(bf16[96,3072]{1,0:T(8,128)(2,1)S(1)} %maximum_select_fusion.5), channel_id=1, source_target_pairs={{0,32},{32,64},{64,96},{96,0},{1,33},{33,65},{65,97},{97,1},{2,34}... | collective-permute-start | bytes 1769480 | tf_op jit(solution)/shard_map/ppermute | solution.py:70
  188.9 36.2 %collective-permute-start.12 = (bf16[4,96,3072]{2,1,0:T(8,128)(2,1)}, bf16[4,96,3072]{2,1,0:T(8,128)(2,1)}, u32[]{:S(2)}, u32[]{:S(2)}) collective-permute-start(bf16[4,96,3072]{2,1,0:T(8,128)(2,1)} %pad_maximum_fusion.4.refs_0_), channel_id=1, source_target_pairs={{0,16},{16,0},{1,17},{17,1},{2,18},{18,2},{3,19},{19,3},{4,20},{20... | collective-permute-start | bytes 7077896 | tf_op jit(solution)/shard_map/ppermute | solution.py:74
  307.8 29.6 %collective-permute-start.23 = (bf16[384,1536]{1,0:T(8,128)(2,1)}, bf16[384,1536]{1,0:T(8,128)(2,1)}, u32[]{:S(2)}, u32[]{:S(2)}) collective-permute-start(bf16[384,1536]{1,0:T(8,128)(2,1)} %pad_maximum_fusion.10), channel_id=1, source_target_pairs={{0,96},{32,0},{64,32},{96,64},{1,97},{33,1},{65,33},{97,65},{2,98}... | collective-permute-start | bytes 3538952 | tf_op jit(solution)/shard_map/ppermute | solution.py:70
  309.7 53.7 %collective-permute-start.24 = (bf16[384,1536]{1,0:T(8,128)(2,1)}, bf16[384,1536]{1,0:T(8,128)(2,1)}, u32[]{:S(2)}, u32[]{:S(2)}) collective-permute-start(bf16[384,1536]{1,0:T(8,128)(2,1)} %pad_maximum_fusion.11), channel_id=1, source_target_pairs={{0,64},{32,96},{64,0},{96,32},{1,65},{33,97},{65,1},{97,33},{2,66}... | collective-permute-start | bytes 3538952 | tf_op jit(solution)/shard_map/ppermute | solution.py:70
  324.0 43.8 %all-to-all-start.1 = ((bf16[16,64,768]{2,1,0:T(8,128)(2,1)}), bf16[16,64,768]{2,1,0:T(8,128)(2,1)}, u32[]{:S(2)}, u32[]{:S(2)}) async-start(bf16[16,64,768]{2,1,0:T(8,128)(2,1)} %pad_maximum_fusion.8), calls=%async_computation.1 | async-start | bytes 3145728 | tf_op jit(solution)/shard_map/all_to_all | solution.py:321
  328.4 358.4 %all-reduce.3.cloned.1.call-start = ((), (), s32[]{:S(2)}) async-start(), calls=%async_computation.2 | async-start | bytes 4767744 | tf_op jit(solution)/shard_map/psum | solution.py:501
  331.8 34.1 %collective-permute-start.25 = (bf16[384,1536]{1,0:T(8,128)(2,1)}, bf16[384,1536]{1,0:T(8,128)(2,1)}, u32[]{:S(2)}, u32[]{:S(2)}) collective-permute-start(bf16[384,1536]{1,0:T(8,128)(2,1)} %pad_maximum_fusion.12), channel_id=1, source_target_pairs={{0,32},{32,64},{64,96},{96,0},{1,33},{33,65},{65,97},{97,1},{2,34}... | collective-permute-start | bytes 3538952 | tf_op jit(solution)/shard_map/ppermute | solution.py:70
  398.7 29.5 %collective-permute-start.19 = (bf16[384,3072]{1,0:T(8,128)(2,1)}, bf16[384,3072]{1,0:T(8,128)(2,1)}, u32[]{:S(2)}, u32[]{:S(2)}) collective-permute-start(bf16[384,3072]{1,0:T(8,128)(2,1)} %pad_maximum_fusion.5), channel_id=1, source_target_pairs={{0,16},{16,0},{1,17},{17,1},{2,18},{18,2},{3,19},{19,3},{4,20},{20... | collective-permute-start | bytes 7077896 | tf_op jit(solution)/shard_map/ppermute | solution.py:74
  436.9 28.9 %collective-permute-start.22 = (bf16[96,3072]{1,0:T(8,128)(2,1)S(1)}, bf16[96,3072]{1,0:T(8,128)(2,1)S(1)}, u32[]{:S(2)}, u32[]{:S(2)}) collective-permute-start(bf16[96,3072]{1,0:T(8,128)(2,1)S(1)} %get-tuple-element.147), channel_id=1, source_target_pairs={{0,96},{32,0},{64,32},{96,64},{1,97},{33,1},{65,33},{97,65},{2,98}... | collective-permute-start | bytes 1769480 | tf_op jit(solution)/shard_map/ppermute | solution.py:70
  492.6 66.8 %collective-permute-start.26 = (bf16[384,3200]{1,0:T(8,128)(2,1)}, bf16[384,3200]{1,0:T(8,128)(2,1)}, u32[]{:S(2)}, u32[]{:S(2)}) collective-permute-start(bf16[384,3200]{1,0:T(8,128)(2,1)} %pad_maximum_fusion.1), channel_id=1, source_target_pairs={{0,16},{16,0},{1,17},{17,1},{2,18},{18,2},{3,19},{19,3},{4,20},{20... | collective-permute-start | bytes 7372808 | tf_op jit(solution)/shard_map/ppermute | solution.py:74
  495.7 53.4 %collective-permute-start.29 = (bf16[768,768]{1,0:T(8,128)(2,1)}, bf16[768,768]{1,0:T(8,128)(2,1)}, u32[]{:S(2)}, u32[]{:S(2)}) collective-permute-start(bf16[768,768]{1,0:T(8,128)(2,1)} %get-tuple-element.131), channel_id=1, source_target_pairs={{0,32},{32,64},{64,96},{96,0},{1,33},{33,65},{65,97},{97,1},{2,34}... | collective-permute-start | bytes 3538952 | tf_op jit(solution)/shard_map/ppermute | solution.py:70
  497.6 52.7 %collective-permute-start.30 = (bf16[768,768]{1,0:T(8,128)(2,1)}, bf16[768,768]{1,0:T(8,128)(2,1)}, u32[]{:S(2)}, u32[]{:S(2)}) collective-permute-start(bf16[768,768]{1,0:T(8,128)(2,1)} %get-tuple-element.130), channel_id=1, source_target_pairs={{0,64},{32,96},{64,0},{96,32},{1,65},{33,97},{65,1},{97,33},{2,66}... | collective-permute-start | bytes 3538952 | tf_op jit(solution)/shard_map/ppermute | solution.py:70
  497.6 55.2 %collective-permute-start.31 = (bf16[768,768]{1,0:T(8,128)(2,1)}, bf16[768,768]{1,0:T(8,128)(2,1)}, u32[]{:S(2)}, u32[]{:S(2)}) collective-permute-start(bf16[768,768]{1,0:T(8,128)(2,1)} %get-tuple-element.129), channel_id=1, source_target_pairs={{0,96},{32,0},{64,32},{96,64},{1,97},{33,1},{65,33},{97,65},{2,98}... | collective-permute-start | bytes 3538952 | tf_op jit(solution)/shard_map/ppermute | solution.py:70
  565.0 29.8 %collective-permute-start.33 = (bf16[96,3200]{1,0:T(8,128)(2,1)S(1)}, bf16[96,3200]{1,0:T(8,128)(2,1)S(1)}, u32[]{:S(2)}, u32[]{:S(2)}) collective-permute-start(bf16[96,3200]{1,0:T(8,128)(2,1)S(1)} %get-tuple-element.146), channel_id=1, source_target_pairs={{0,64},{32,96},{64,0},{96,32},{1,65},{33,97},{65,1},{97,33},{2,66}... | collective-permute-start | bytes 1843208 | tf_op jit(solution)/shard_map/ppermute | solution.py:70
  (186 other events, 1933.9 us)
Sparse Core Ops, SparseCore 0:
  596.8 90.0 all-reduce.2

commit v3 on v2

--- a/solution.py
+++ b/solution.py
@@ -66,26 +66,26 @@
 SLOTS = 32
 
 
+def shift(block, axis, step):
+    return lax.ppermute(block, axis, [(i, (i + step) % X) for i in range(X)])
+
+
 def x_shift(block, step):
-    return lax.ppermute(block, "x", [(i, (i + step) % X) for i in range(X)])
+    return shift(block, "x", step)
+
+
+def rolled(array, start, axis):
+    doubled = jnp.concatenate([array, array], axis=axis)
+    return lax.dynamic_slice_in_dim(doubled, start, X, axis=axis)
 
 
 def core_swap(block):
     return lax.ppermute(block, "core", [(0, 1), (1, 0)])
 
 
-def after(block, earlier):
-    return jnp.where(earlier == earlier, block, jnp.zeros_like(block))
-
-
-def mark(*blocks):
-    return sum(block[(0,) * block.ndim].astype(jnp.float32) for block in blocks)
-
-
-def place(spots, sources, shapes, moves):
+def place(spots, sources, shapes, moves, count):
     kind = sources[0].dtype
     blocks = [(n, k) for n, source in enumerate(sources) for k in range(source.shape[0])]
-    count = sum(len(listed) for listed in moves([0] * spots.shape[0]))
     staged = 2 * sum(math.prod(source.shape) for source in sources)
 
     def kernel(spots_ref, *refs):
@@ -128,7 +128,7 @@
     return [shard] + [x_shift(shard, step) for step in range(1, X)]
 
 
-def both_cores(pieces, shapes, targets):
+def both_cores(pieces, shapes, targets, each):
     xi, ci = lax.axis_index("x"), lax.axis_index("core")
     own = jnp.stack(pieces)
     spots = [((xi - k) % X) * CORES + (ci if mine else 1 - ci) for mine in (1, 0) for k in range(X)]
@@ -137,7 +137,47 @@
         [own, core_swap(own)],
         shapes,
         lambda spots: [targets(spot) for spot in spots],
-    )
+        CORES * X * each,
+    )
+
+
+def gather_dense(up_shard, down_shard):
+    xi, ci, zi, yi = (lax.axis_index(name) for name in ("x", "core", "z", "y"))
+    depth, width = up_shard.shape[0], down_shard.shape[1]
+    up_part = lax.dynamic_slice_in_dim(up_shard, zi * width, width, axis=1)
+    down_part = lax.dynamic_slice_in_dim(down_shard, yi * depth, depth, axis=0)
+    pieces = gather_pieces(jnp.concatenate([up_part, down_part], axis=0))
+    up_x = jnp.stack([piece[:depth] for piece in pieces])
+    down_x = jnp.stack([piece[depth:] for piece in pieces])
+    up_own = lax.all_gather(up_x, "z", axis=0, tiled=True)
+    down_own = lax.all_gather(down_x, "y", axis=0, tiled=True)
+    rows = [
+        ((xi - k) % X) * CORES + (ci if mine else 1 - ci)
+        for mine in (1, 0)
+        for _ in range(X)
+        for k in range(X)
+    ]
+    every = slice(None)
+    count = CORES * X * X
+    parts = [n // X % X for n in range(count)]
+
+    def columns(spots):
+        return [
+            [((every, every), 0, (spots[n], every, pl.ds(parts[n] * width, width)))]
+            for n in range(count)
+        ]
+
+    def stripes(spots):
+        return [[((every, every), 0, (spots[n], parts[n]))] for n in range(count)]
+
+    rows = jnp.stack(rows).astype(jnp.int32)
+    (up,) = place(
+        rows, [up_own, core_swap(up_own)], [(X * CORES, depth, X * width)], columns, count
+    )
+    (down,) = place(
+        rows, [down_own, core_swap(down_own)], [(X * CORES, X, depth, width)], stripes, count
+    )
+    return up.reshape(-1, X * width), down.reshape(-1, width)
 
 
 def split_rows(left):
@@ -150,7 +190,7 @@
     return own.reshape(wide // CORES, rows), other.reshape(wide // CORES, rows)
 
 
-def scatter_halves(own, other, before=None):
+def scatter_halves(own, other):
     block = own[0].shape[0] // X
     starts = [sum(part.shape[1] for part in own[:k]) for k in range(len(own))]
     got = core_swap(jnp.concatenate([part.astype(jnp.bfloat16) for part in other], axis=1))
@@ -159,34 +199,47 @@
         for part, start in zip(own, starts)
     ]
     low = jnp.concatenate([t[block:].astype(jnp.bfloat16) for t in totals], axis=1)
-    if before is not None:
-        low = after(low, before)
     arrived = [x_shift(low[(k - 1) * block : k * block], k) for k in range(1, X)]
     sums = []
     for t, start in zip(totals, starts):
         cut = slice(start, start + t.shape[1])
         sums.append(t[:block] + sum(a[:, cut].astype(jnp.float32) for a in arrived))
-    return sums, mark(*arrived)
-
-
-def scatter_dense(up, down):
-    (up_own, up_other), (down_own, down_other) = up, down
-    width = down_own.shape[1]
-    depth, deep = up_own.shape[0] // X, down_own.shape[0] // X
-    stripes = up_own.shape[1] // width
-    up_total = up_own + core_swap(up_other.astype(jnp.bfloat16)).astype(jnp.float32)
-    down_total = down_own + core_swap(down_other.astype(jnp.bfloat16)).astype(jnp.float32)
-    arrived = []
-    for k in range(1, X):
-        up_low = up_total[k * depth : (k + 1) * depth].astype(jnp.bfloat16)
-        down_low = down_total[k * deep : (k + 1) * deep].astype(jnp.bfloat16)
-        pack = [up_low[:, n * width : (n + 1) * width] for n in range(stripes)] + [down_low]
-        arrived.append(x_shift(jnp.concatenate(pack, axis=0), k))
-    total = sum(a.astype(jnp.float32) for a in arrived)
-    up_sum = up_total[:depth] + jnp.concatenate(
-        [total[n * depth : (n + 1) * depth] for n in range(stripes)], axis=1
-    )
-    return up_sum, down_total[:deep] + total[stripes * depth :], mark(*arrived)
+    return sums
+
+
+def scatter_whole(part):
+    return lax.psum_scatter(
+        part.astype(jnp.bfloat16), ("x", "core"), scatter_dimension=0, tiled=True
+    )
+
+
+def sum_over_zy(shares, small):
+    spots, wide = 16, 768
+    parts = []
+    for share in shares:
+        low = share.astype(jnp.bfloat16)
+        stripes = [low[:, k : k + wide] for k in range(0, low.shape[1], wide)]
+        parts.append(jnp.concatenate(stripes, axis=0).reshape(spots, -1, wide))
+    if small is not None:
+        last = small.astype(jnp.bfloat16).reshape(spots, -1, wide)
+        parts.append(jnp.pad(last, ((0, 0), (0, 8 - last.shape[1]), (0, 0))))
+    packed = jnp.concatenate(parts, axis=1)
+    came = lax.all_to_all(packed, ("z", "y"), split_axis=0, concat_axis=0, tiled=True)
+    mine = jnp.sum(came.astype(jnp.float32), axis=0).astype(jnp.bfloat16)
+    copies = jnp.broadcast_to(mine[None], packed.shape)
+    back = lax.all_to_all(copies, ("z", "y"), split_axis=0, concat_axis=0, tiled=True)
+    sums, start = [], 0
+    for share, part in zip(shares, parts):
+        depth, high = share.shape[0], part.shape[1]
+        rows = back[:, start : start + high].reshape(-1, wide).astype(jnp.float32)
+        start += high
+        sums.append(
+            jnp.concatenate([rows[k : k + depth] for k in range(0, rows.shape[0], depth)], axis=1)
+        )
+    if small is None:
+        return sums
+    rest = back[:, start : start + last.shape[1]]
+    return sums, rest.reshape(small.shape).astype(jnp.float32)
 
 
 def weight_grad(left, right):
@@ -214,7 +267,7 @@
     return (stream + product(mixed, out_proj), (normed, saved, joined, log_total, mixed))
 
 
-def attend_backward(grad, gain, in_proj, out_proj, kept, images, length):
+def attend_backward(grad, gain, in_proj, out_proj, kept, images, length, weight_grad):
     normed, saved, joined, log_total, mixed = kept
     rows, width = grad.shape
     scale = HEAD_DIM ** (-0.5)
@@ -262,20 +315,18 @@
 def dense_backward(grad, gain, up_w, down_w, kept):
     normed, saved, slope, hidden = kept
     grad_low = grad.astype(jnp.bfloat16)
-    down_grad = weight_grad(hidden, grad_low)
     pre_grad = (product_bt(grad_low, down_w) * slope).astype(jnp.bfloat16)
-    up_grad = weight_grad(normed, pre_grad)
+    up_grad = scatter_whole(product_t(normed, pre_grad))
+    down_grad = scatter_whole(product_t(hidden, grad_low))
     stream_grad, gain_grad = norm_back(product_bt(pre_grad, up_w), gain, saved)
     return (grad + stream_grad, (gain_grad, up_grad, down_grad))
 
 
-def moe(stream, grad_low, gain, router, up_half, down_half, ready, routes, slot_index, keep_mask):
+def moe(stream, grad_low, gain, router, up_half, down_half, routes, slot_index, keep_mask):
     rows, width = stream.shape
     experts = router.shape[1]
     slots = experts * SLOTS
-    hidden_local = up_half.shape[1] // X
     grad = grad_low.astype(jnp.float32)
-    half = width // 2
     normed_f, saved = norm_rows(stream, gain)
     normed = normed_f.astype(jnp.bfloat16)
     logits = product(normed, router)
@@ -300,18 +351,17 @@
     send = jnp.concatenate(
         [send_rows.reshape(experts, SLOTS, width), send_grad.reshape(experts, SLOTS, width)], axis=1
     )
-    send = after(send, ready)
     received = lax.all_to_all(send, ("z", "y"), split_axis=0, concat_axis=0, tiled=True)
     partner = core_swap(received)
 
     flat = jnp.concatenate([received[:, :SLOTS], partner[:, :SLOTS]], axis=0).reshape(-1, width)
     flat_grad = jnp.concatenate([received[:, SLOTS:], partner[:, SLOTS:]], axis=0).reshape(-1, width)
-    hidden, slope = gelu_parts(product(flat, up_half))
+    hidden, slope = gelu_parts(product_bt(flat, up_half))
     hidden = hidden.astype(jnp.bfloat16)
     partial_out = product(hidden, down_half)
     got_out = core_swap(partial_out[slots:].astype(jnp.bfloat16))
     pre_grad = (product_bt(flat_grad, down_half) * slope).astype(jnp.bfloat16)
-    partial_in = product_bt(pre_grad, up_half)
+    partial_in = product(pre_grad, up_half)
     got_in = core_swap(partial_in[slots:].astype(jnp.bfloat16))
     result = (partial_out[:slots] + got_out.astype(jnp.float32)).astype(jnp.bfloat16)
     in_grad = (partial_in[:slots] + got_in.astype(jnp.float32)).astype(jnp.bfloat16)
@@ -322,22 +372,13 @@
     result_rows = returned[:, :SLOTS].reshape(slots, width)
     back_rows = returned[:, SLOTS:].reshape(slots, width)
 
-    cuts = [slice(k * hidden_local, (k + 1) * hidden_local) for k in range(X)]
-    up_parts = [product_t(flat, pre_grad[:, cut]) for cut in cuts]
-    down_parts = [product_t(hidden[:, cut], flat_grad) for cut in cuts]
-    arrived = []
-    for k in range(1, X):
-        low_up = up_parts[k].astype(jnp.bfloat16)
-        pack = jnp.concatenate(
-            [low_up[:half], low_up[half:], down_parts[k].astype(jnp.bfloat16)], axis=1
-        )
-        arrived.append(x_shift(pack, -k))
-    total = sum(a.astype(jnp.float32) for a in arrived)
-    up_grad = up_parts[0] + jnp.concatenate(
-        [total[:, :hidden_local], total[:, hidden_local : 2 * hidden_local]], axis=0
-    )
-    down_grad = down_parts[0] + total[:, 2 * hidden_local :]
-    sent = mark(*arrived)
+    down_grad = lax.psum_scatter(
+        product_t(hidden, flat_grad).astype(jnp.bfloat16), "x", scatter_dimension=0, tiled=True
+    ).astype(jnp.float32)
+    up_grad = lax.psum_scatter(
+        product_t(pre_grad, flat).astype(jnp.bfloat16), "x", scatter_dimension=0, tiled=True
+    )
+    up_grad = up_grad.astype(jnp.float32).T
 
     first = product(pick_first.astype(jnp.bfloat16), result_rows)
     second = product(pick_second.astype(jnp.bfloat16), result_rows)
@@ -350,7 +391,7 @@
     router_grad = product_t(normed, logit_grad)
     normed_grad = product_bt(logit_grad, router) + product(select, back_rows)
     stream_grad, gain_grad = norm_back(normed_grad, gain, saved)
-    return (new_stream, grad + stream_grad, (gain_grad, router_grad, up_grad, down_grad), sent)
+    return (new_stream, grad + stream_grad, (gain_grad, router_grad, up_grad, down_grad))
 
 
 def shards(
@@ -400,91 +441,49 @@
         ]
 
     pieces = gather_pieces(jnp.concatenate([in_proj_a, out_proj_a, small], axis=1))
-    reached = mark(*pieces[1:])
     widths = [wide_in, wide_out, 128]
     in_aa, out_aa, small_all = both_cores(
-        pieces, [(blocks, depth, wide) for wide in widths], side_by_side(widths)
+        pieces, [(blocks, depth, wide) for wide in widths], side_by_side(widths), len(widths)
     )
     in_aa, out_aa, small_all = (w.reshape(width, -1) for w in (in_aa, out_aa, small_all))
     gain_aa, gain_dd, gain_bb, gain_mm = (small_all[:, k] for k in range(4))
     router_full = small_all[:, 4 : 4 + experts]
 
-    stripes = dense_up.shape[1] // width
-    high = stripes * depth
-    pieces = gather_pieces(
-        after(
-            jnp.concatenate(
-                [dense_up[:, k * width : (k + 1) * width] for k in range(stripes)] + [dense_down], axis=0
-            ),
-            reached,
-        )
-    )
-    reached = mark(*pieces[1:])
-    (up_dd,) = both_cores(
-        [piece[:high] for piece in pieces],
-        [(blocks, depth, stripes * width)],
-        lambda spot: [
-            ((pl.ds(k * depth, depth), every), 0, (spot, every, pl.ds(k * width, width)))
-            for k in range(stripes)
-        ],
-    )
-    (down_dd,) = both_cores(
-        [piece[high:] for piece in pieces],
-        [(blocks, dense_down.shape[0], width)],
-        lambda spot: [((every, every), 0, (spot,))],
-    )
-    up_dd, down_dd = up_dd.reshape(width, -1), down_dd.reshape(-1, width)
-
-    pieces = gather_pieces(after(jnp.concatenate([in_proj_b, out_proj_b], axis=1), reached))
+    up_dd, down_dd = gather_dense(dense_up, dense_down)
+
+    pieces = gather_pieces(jnp.concatenate([in_proj_b, out_proj_b], axis=1))
     widths = [wide_in, wide_out]
     in_bb, out_bb = both_cores(
-        pieces, [(blocks, depth, wide) for wide in widths], side_by_side(widths)
+        pieces, [(blocks, depth, wide) for wide in widths], side_by_side(widths), len(widths)
     )
     in_bb, out_bb = in_bb.reshape(width, -1), out_bb.reshape(width, -1)
 
-    up_local, down_local = expert_up[0], expert_down[0]
-    half, units = width // 2, up_local.shape[1]
-    packs = gather_pieces(
-        after(jnp.concatenate([up_local[:half], up_local[half:], down_local], axis=1), reached)
-    )
-
-    def unpack(k):
-        parts = [
-            ((every, pl.ds(part * units, units)), 0, (pl.ds(part * half, half), pl.ds(k * units, units)))
-            for part in range(2)
-        ]
-        return parts + [((every, pl.ds(2 * units, width)), 1, (pl.ds(k * units, units),))]
-
-    up_half, down_half = place(
-        jnp.zeros((1,), jnp.int32),
-        [pack[None] for pack in packs],
-        [(width, X * units), (X * units, width)],
-        lambda _: [unpack(k) for k in range(X)],
-    )
+    up_half = lax.all_gather(expert_up[0].T, "x", axis=0, tiled=True)
+    down_half = lax.all_gather(expert_down[0], "x", axis=0, tiled=True)
 
     stream_one, kept_one = attend_forward(stream, gain_aa, in_aa, out_aa, images, length)
     stream_two, kept_two = dense_forward(stream_one, gain_dd, up_dd, down_dd)
     stream_three, kept_three = attend_forward(stream_two, gain_bb, in_bb, out_bb, images, length)
-    stream_four, grad, moe_grads, sent = moe(
+    stream_four, grad, moe_grads = moe(
         stream_three,
         output_grad.reshape(rows, width),
         gain_mm,
         router_full,
         up_half,
         down_half,
-        mark(*packs[1:]),
         flat_routes,
         flat_slots,
         flat_keep,
     )
     output = stream_four.astype(jnp.bfloat16).reshape(images, length, width)
-    grad, attn_b_grads = attend_backward(grad, gain_bb, in_bb, out_bb, kept_three, images, length)
-    (in_b, out_b), sent_b = scatter_halves(*zip(attn_b_grads[1], attn_b_grads[2]))
-    grad = after(grad, sent)
+    grad, attn_b_grads = attend_backward(
+        grad, gain_bb, in_bb, out_bb, kept_three, images, length, product_t
+    )
+    share_b = scatter_whole(jnp.concatenate(attn_b_grads[1:], axis=1))
     grad, dense_grads = dense_backward(grad, gain_dd, up_dd, down_dd, kept_two)
-    up, down, sent_d = scatter_dense(dense_grads[1], dense_grads[2])
-    grad = after(grad, sent_b)
-    grad, attn_a_grads = attend_backward(grad, gain_aa, in_aa, out_aa, kept_one, images, length)
+    grad, attn_a_grads = attend_backward(
+        grad, gain_aa, in_aa, out_aa, kept_one, images, length, weight_grad
+    )
     input_grad = grad.reshape(images, length, width)
     small_grad = jnp.concatenate(
         [
@@ -494,13 +493,14 @@
         ],
         axis=0,
     )
-    (in_a, out_a, small_share), _ = scatter_halves(
-        *zip(attn_a_grads[1], attn_a_grads[2], split_rows(small_grad)), before=sent_d
-    )
-    shares = [in_a, jnp.concatenate([out_a, small_share], axis=1), up, down, in_b, out_b]
-    totals = lax.psum([share.astype(jnp.bfloat16) for share in shares], ("z", "y"))
-    in_a, out_a, up, down, in_b, out_b = [t.astype(jnp.float32) for t in totals]
-    out_a, small_total = out_a[:, :wide_out], out_a[:, wide_out:]
+    in_a, out_a, small_share = scatter_halves(
+        *zip(attn_a_grads[1], attn_a_grads[2], split_rows(small_grad))
+    )
+    share_a = jnp.concatenate([in_a, out_a], axis=1)
+    (share_a, share_b), small_total = sum_over_zy([share_a, share_b], small_share)
+    up, down = sum_over_zy(dense_grads[1:], None)
+    in_a, out_a = share_a[:, :wide_in], share_a[:, wide_in:]
+    in_b, out_b = share_b[:, :wide_in], share_b[:, wide_in:]
     return (
         output,
         input_grad,

time: 714 us -> 533 us (0.75)
  waiting for transfers between devices: 321 us -> 231 us
  local copies, waits for them, and re-layouts: 106 us -> 65.9 us
  blocking collectives: 31.3 us -> 0 us
  other arithmetic: 65.6 us -> 47.7 us
  between operations: 29 us -> 16.7 us
  starting transfers between devices: 37.6 us -> 49.5 us
  matrix products: 99.5 us -> 91.5 us
  Pallas kernels: 15 us -> 22.6 us
    ppermute x24 -> x12, waiting for transfers between devices: 241 us -> 91.3 us  [shift(): return lax.ppermute(block, axis, [(i, (i + step) % X) for i in range(X)])]
    psum x1 -> x0, waiting for transfers between devices: 78.4 us -> none  [shards(): lax.psum([share.astype(jnp.bfloat16) for share in shares], ('z', 'y'))]
    all_to_all x0 -> x5, waiting for transfers between devices: none -> 76.5 us  [the longest x2 30.6 us: sum_over_zy(): lax.all_to_all(copies, ('z', 'y'), split_axis=0, concat_axis=0, tiled=True)]
    reduce_scatter x0 -> x5, waiting for transfers between devices: none -> 31.9 us  [the longest x3 29.1 us: scatter_whole(): lax.psum_scatter(part.astype(jnp.bfloat16), ('x', 'core'), scatter_dimens...]
    all_to_all x1 -> x0, blocking collectives: 31.3 us -> none  [moe(): lax.all_to_all(send, ('z', 'y'), split_axis=0, concat_axis=0, tiled=True)]
    all_to_all x0 -> x5, starting transfers between devices: none -> 28.7 us  [the longest x2 12.4 us: sum_over_zy(): lax.all_to_all(packed, ('z', 'y'), split_axis=0, concat_axis=0, tiled=True)]
    all_to_all x1, waiting for transfers between devices: 0.01 us -> 24.3 us  [moe(): lax.all_to_all(back, ('z', 'y'), split_axis=0, concat_axis=0, tiled=True)]
    dot_general x24 -> x16, matrix products: 45.4 us -> 23.5 us  [product(): return jnp.dot(left, right, preferred_element_type=jnp.float32)]
  transfers between devices with their start and end apart: 37 -> 35, of which waited for: 15 -> 19; matrix products, arithmetic and copies ran while one was open for 21% -> 27% of each run, Pallas kernels for 2% -> 4%
where the time goes in v3:
time: 533 us; the launch traced here: 524 us
  waiting for transfers between devices  231 us (43%)
  matrix products  91.5 us (17%)
  local copies, waits for them, and re-layouts  65.9 us (12%)
  starting transfers between devices  49.5 us (9%)
  other arithmetic  47.7 us (9%)
  Pallas kernels  22.6 us (4%)
  between operations  16.7 us (3%)
    ppermute x12, waiting for transfers between devices, shift(): return lax.ppermute(block, axis, [(i, (i + step) % X) for i in range(X)])  91.3 us
    unnamed x328, local copies, waits for them, and re-layouts  32.5 us
    all_to_all x2, waiting for transfers between devices, sum_over_zy(): lax.all_to_all(copies, ('z', 'y'), split_axis=0, concat_axis=0, tiled=True)  30.6 us
    reduce_scatter x3, waiting for transfers between devices, scatter_whole(): lax.psum_scatter(part.astype(jnp.bfloat16), ('x', 'core'), scatter_dimens...  29.1 us
    dot_general x9, matrix products, product_bt(): lax.dot_general(left, right, (((1,), (1,)), ((), ())), preferred_element_...  28.3 us
    all_to_all x1, waiting for transfers between devices, moe(): lax.all_to_all(send, ('z', 'y'), split_axis=0, concat_axis=0, tiled=True)  24.5 us
    all_to_all x1, waiting for transfers between devices, moe(): lax.all_to_all(back, ('z', 'y'), split_axis=0, concat_axis=0, tiled=True)  24.3 us
    dot_general x16, matrix products, product(): return jnp.dot(left, right, preferred_element_type=jnp.float32)  23.5 us
  transfers between devices with their start and end apart: 35, of which 19 were waited for; matrix products, arithmetic and copies ran while one was open for 27% of the time, Pallas kernels for 4%

profile of v3, /device:TPU:6, one launch (start us, length us, event | category | flops | bytes accessed | tf_op | source)
XLA Modules:
  0.0 524.5 jit_solution(5819398933209612323)
XLA Ops:
  12.4 12.2 %collective-permute-done.6 = bf16[192,768]{1,0:T(8,128)(2,1)S(1)} collective-permute-done((bf16[192,768]{1,0:T(8,128)(2,1)S(1)}, bf16[192,768]{1,0:T(8,128)(2,1)S(1)}, u32[]{:S(2)}, u32[]{:S(2)}) %collective-permute-start.6) | collective-permute-done | bytes 294944 | tf_op jit(solution)/shard_map/ppermute | solution.py:70
  34.7 23.8 %collective-permute-done.2 = bf16[96,3200]{1,0:T(8,128)(2,1)S(1)} collective-permute-done((bf16[96,3200]{1,0:T(8,128)(2,1)S(1)}, bf16[96,3200]{1,0:T(8,128)(2,1)S(1)}, u32[]{:S(2)}, u32[]{:S(2)}) %collective-permute-start.2) | collective-permute-done | bytes 614432 | tf_op jit(solution)/shard_map/ppermute | solution.py:70
  60.8 9.9 %collective-permute-done.11 = bf16[96,3072]{1,0:T(8,128)(2,1)S(1)} collective-permute-done((bf16[96,3072]{1,0:T(8,128)(2,1)S(1)}, bf16[96,3072]{1,0:T(8,128)(2,1)S(1)}, u32[]{:S(2)}, u32[]{:S(2)}) %collective-permute-start.11) | collective-permute-done | bytes 589856 | tf_op jit(solution)/shard_map/ppermute | solution.py:70
  70.7 13.9 %collective-permute-done.10 = bf16[96,3072]{1,0:T(8,128)(2,1)S(1)} collective-permute-done((bf16[96,3072]{1,0:T(8,128)(2,1)S(1)}, bf16[96,3072]{1,0:T(8,128)(2,1)S(1)}, u32[]{:S(2)}, u32[]{:S(2)}) %collective-permute-start.10) | collective-permute-done | bytes 589856 | tf_op jit(solution)/shard_map/ppermute | solution.py:70
  121.5 5.9 %shard_map.290 = bf16[8,96,3072]{2,1,0:T(8,128)(2,1)S(1)} custom-call(s32[32]{0:T(128)S(1)} %stack.197.spots_ref, bf16[16,96,768]{2,1,0:T(8,128)(2,1)S(1)} %copy-done.16, bf16[16,96,768]{2,1,0:T(8,128)(2,1)} %collective-permute-done.7.refs_1_), custom_call_target="tpu_custom_call" | custom-call | bytes 9437184 | tf_op jit(solution)/shard_map/pallas_call | solution.py:114
  130.8 10.4 %shard_map.291 = bf16[8,4,96,768]{3,2,1,0:T(8,128)(2,1)S(1)} custom-call(s32[32]{0:T(128)S(1)} %stack.197.spots_ref, bf16[16,96,768]{2,1,0:T(8,128)(2,1)S(1)} %copy-done.17, bf16[16,96,768]{2,1,0:T(8,128)(2,1)} %collective-permute-done.8.refs_1_), custom_call_target="tpu_custom_call" | custom-call | bytes 9437184 | tf_op jit(solution)/shard_map/pallas_call | solution.py:114
  159.6 8.1 %all-to-all-start = ((bf16[16,64,768]{2,1,0:T(8,128)(2,1)}), bf16[16,64,768]{2,1,0:T(8,128)(2,1)}, u32[]{:S(2)}, u32[]{:S(2)}) async-start(bf16[16,64,768]{2,1,0:T(8,128)(2,1)} %pad_maximum_fusion.5), calls=%async_computation | async-start | bytes 3145728 | tf_op jit(solution)/shard_map/all_to_all | solution.py:354
  168.3 24.5 %all-to-all-done = bf16[16,64,768]{2,1,0:T(8,128)(2,1)} async-done(((bf16[16,64,768]{2,1,0:T(8,128)(2,1)}), bf16[16,64,768]{2,1,0:T(8,128)(2,1)}, u32[]{:S(2)}, u32[]{:S(2)}) %all-to-all-start) | async-done | bytes 1572896 | tf_op jit(solution)/shard_map/all_to_all | solution.py:354
  199.2 7.0 %multiply_convert_fusion = (bf16[1024,1536]{1,0:T(8,128)(2,1)}, f32[1024,1536]{1,0:T(8,128)}) fusion(bf16[1024,768]{1,0:T(8,128)(2,1)} %bitcast.364, bf16[1536,768]{0,1:T(8,128)(2,1)} %all-gather.10.cloned.1.call-done), kind=kOutput, calls=%fused_computation.7 | convolution fusion | flops 2423783424 | bytes 13369344 | tf_op jit(solution)/shard_map/dot_general | solution.py:27
  206.3 6.8 %fusion.5 = bf16[1024,1536]{1,0:T(8,128)(2,1)S(1)} fusion(f32[1024,1536]{1,0:T(8,128)} %get-tuple-element.197, bf16[1024,768]{1,0:T(8,128)(2,1)} %bitcast.362, bf16[1,1536,768]{2,1,0:T(8,128)(2,1)} %all-gather.12.cloned.1.call-done), kind=kOutput, calls=%fused_computation.6 | convolution fusion | flops 2431647744 | bytes 13369344 | tf_op jit(solution)/shard_map/dot_general | solution.py:27
  223.3 4.4 all-to-all-start.1
  229.4 24.3 %all-to-all-done.1 = bf16[16,64,768]{2,1,0:T(8,128)(2,1)} async-done(((bf16[16,64,768]{2,1,0:T(8,128)(2,1)}), bf16[16,64,768]{2,1,0:T(8,128)(2,1)}, u32[]{:S(2)}, u32[]{:S(2)}) %all-to-all-start.1) | async-done | bytes 1572896 | tf_op jit(solution)/shard_map/all_to_all | solution.py:371
  282.5 5.1 convolution_convert_fusion
  298.5 5.5 %multiply_reduce_fusion.6 = (f32[768]{0:T(1024)}, f32[197]{0:T(256)S(1)}, f32[197]{0:T(256)S(1)}, f32[197,768]{1,0:T(8,128)S(1)}) fusion(f32[197,768]{1,0:T(8,128)} %copy-done.26, f32[197]{0:T(256)} %copy-done.111, f32[197]{0:T(256)} %copy-done.92, f32[768]{0:T(1024)} %copy-done.71, bf16[197,3072]{1,0:T(8,128)(2,1)} %copy-done.64, ...), kind=kOutput, calls=%fused_computation.146 | convolution fusion | flops 930771840 | bytes 7148624 | tf_op jit(solution)/shard_map/dot_general | solution.py:27
  332.7 4.0 convolution_convert_fusion.7
  353.0 15.3 %collective-permute-done.19 = bf16[96,3200]{1,0:T(8,128)(2,1)} collective-permute-done((bf16[96,3200]{1,0:T(8,128)(2,1)}, bf16[96,3200]{1,0:T(8,128)(2,1)}, u32[]{:S(2)}, u32[]{:S(2)}) %collective-permute-start.19) | collective-permute-done | bytes 614432 | tf_op jit(solution)/shard_map/ppermute | solution.py:70
  368.3 13.9 %collective-permute-done.18 = bf16[96,3200]{1,0:T(8,128)(2,1)} collective-permute-done((bf16[96,3200]{1,0:T(8,128)(2,1)}, bf16[96,3200]{1,0:T(8,128)(2,1)}, u32[]{:S(2)}, u32[]{:S(2)}) %collective-permute-start.18) | collective-permute-done | bytes 614432 | tf_op jit(solution)/shard_map/ppermute | solution.py:70
  388.2 5.4 %all-to-all-start.4 = ((bf16[16,48,768]{2,1,0:T(8,128)(2,1)}), bf16[16,48,768]{2,1,0:T(8,128)(2,1)S(1)}, u32[]{:S(2)}, u32[]{:S(2)}) async-start(bf16[16,48,768]{2,1,0:T(8,128)(2,1)} %pad_maximum_fusion.10), calls=%async_computation.7 | async-start | bytes 2359296 | tf_op jit(solution)/shard_map/all_to_all | solution.py:227
  394.8 29.0 %reduce-scatter.6.cloned.1.call-done = bf16[96,3072]{1,0:T(8,128)(2,1)} async-done(((bf16[768,3072]{1,0:T(8,128)(2,1)}), bf16[96,3072]{1,0:T(8,128)(2,1)}) %reduce-scatter.6.cloned.1.call-update) | async-done | bytes 589840 | tf_op jit(solution)/shard_map/reduce_scatter | solution.py:211
  427.3 7.0 %all-to-all-start.2 = ((bf16[16,56,768]{2,1,0:T(8,128)(2,1)}), bf16[16,56,768]{2,1,0:T(8,128)(2,1)S(1)}, u32[]{:S(2)}, u32[]{:S(2)}) async-start(bf16[16,56,768]{2,1,0:T(8,128)(2,1)} %fusion.21), calls=%async_computation.3 | async-start | bytes 2752512 | tf_op jit(solution)/shard_map/all_to_all | solution.py:227
  435.8 21.3 %all-to-all-done.2 = bf16[16,56,768]{2,1,0:T(8,128)(2,1)S(1)} async-done(((bf16[16,56,768]{2,1,0:T(8,128)(2,1)}), bf16[16,56,768]{2,1,0:T(8,128)(2,1)S(1)}, u32[]{:S(2)}, u32[]{:S(2)}) %all-to-all-start.2) | async-done | bytes 1376288 | tf_op jit(solution)/shard_map/all_to_all | solution.py:227
  458.3 4.4 all-to-all-start.5
  466.8 18.3 %all-to-all-done.5 = bf16[16,48,768]{2,1,0:T(8,128)(2,1)} async-done(((bf16[16,48,768]{2,1,0:T(8,128)(2,1)}), bf16[16,48,768]{2,1,0:T(8,128)(2,1)}, u32[]{:S(2)}, u32[]{:S(2)}) %all-to-all-start.5) | async-done | bytes 1179680 | tf_op jit(solution)/shard_map/all_to_all | solution.py:230
  500.2 12.3 %all-to-all-done.3 = bf16[16,56,768]{2,1,0:T(8,128)(2,1)S(1)} async-done(((bf16[16,56,768]{2,1,0:T(8,128)(2,1)}), bf16[16,56,768]{2,1,0:T(8,128)(2,1)S(1)}, u32[]{:S(2)}, u32[]{:S(2)}) %all-to-all-start.3) | async-done | bytes 1376288 | tf_op jit(solution)/shard_map/all_to_all | solution.py:230
  (569 shorter events, 215.0 us)
Async XLA Ops:
  7.2 98.7 %all-gather.6.cloned.1.call-start = ((), (), s32[]{:S(2)}) async-start(), calls=%async_computation.11 | async-start | bytes 2949120 | tf_op jit(solution)/shard_map/all_gather | solution.py:152
  26.2 85.0 %all-gather.8.cloned.1.call-start = ((), (), s32[]{:S(2)}) async-start(), calls=%async_computation.12 | async-start | bytes 2949120 | tf_op jit(solution)/shard_map/all_gather | solution.py:153
  27.2 172.1 %all-gather.10.cloned.1.call-start = ((), (), s32[]{:S(2)}) async-start(), calls=%async_computation.13 | async-start | bytes 2949120 | tf_op jit(solution)/shard_map/all_gather | solution.py:461
  28.2 30.4 %collective-permute-start.2 = (bf16[96,3200]{1,0:T(8,128)(2,1)S(1)}, bf16[96,3200]{1,0:T(8,128)(2,1)S(1)}, u32[]{:S(2)}, u32[]{:S(2)}) collective-permute-start(bf16[96,3200]{1,0:T(8,128)(2,1)S(1)} %concatenate.82), channel_id=1, source_target_pairs={{0,96},{32,0},{64,32},{96,64},{1,97},{33,1},{65,33},{97,65},{2,98}... | collective-permute-start | bytes 1843208 | tf_op jit(solution)/shard_map/ppermute | solution.py:70
  29.0 31.2 %collective-permute-start.1 = (bf16[96,3200]{1,0:T(8,128)(2,1)S(1)}, bf16[96,3200]{1,0:T(8,128)(2,1)S(1)}, u32[]{:S(2)}, u32[]{:S(2)}) collective-permute-start(bf16[96,3200]{1,0:T(8,128)(2,1)S(1)} %concatenate.82), channel_id=1, source_target_pairs={{0,64},{32,96},{64,0},{96,32},{1,65},{33,97},{65,1},{97,33},{2,66}... | collective-permute-start | bytes 1843208 | tf_op jit(solution)/shard_map/ppermute | solution.py:70
  32.3 28.0 %collective-permute-start = (bf16[96,3200]{1,0:T(8,128)(2,1)S(1)}, bf16[96,3200]{1,0:T(8,128)(2,1)S(1)}, u32[]{:S(2)}, u32[]{:S(2)}) collective-permute-start(bf16[96,3200]{1,0:T(8,128)(2,1)S(1)} %concatenate.82), channel_id=1, source_target_pairs={{0,32},{32,64},{64,96},{96,0},{1,33},{33,65},{65,97},{97,1},{2,34}... | collective-permute-start | bytes 1843208 | tf_op jit(solution)/shard_map/ppermute | solution.py:70
  32.4 38.3 %collective-permute-start.11 = (bf16[96,3072]{1,0:T(8,128)(2,1)S(1)}, bf16[96,3072]{1,0:T(8,128)(2,1)S(1)}, u32[]{:S(2)}, u32[]{:S(2)}) collective-permute-start(bf16[96,3072]{1,0:T(8,128)(2,1)S(1)} %constant_dynamic-update-slice_fusion), channel_id=1, source_target_pairs={{0,96},{32,0},{64,32},{96,64},{1,97},{33,1},{65,33},{97,65},{2,98}... | collective-permute-start | bytes 1769480 | tf_op jit(solution)/shard_map/ppermute | solution.py:70
  34.5 50.1 %collective-permute-start.10 = (bf16[96,3072]{1,0:T(8,128)(2,1)S(1)}, bf16[96,3072]{1,0:T(8,128)(2,1)S(1)}, u32[]{:S(2)}, u32[]{:S(2)}) collective-permute-start(bf16[96,3072]{1,0:T(8,128)(2,1)S(1)} %constant_dynamic-update-slice_fusion), channel_id=1, source_target_pairs={{0,64},{32,96},{64,0},{96,32},{1,65},{33,97},{65,1},{97,33},{2,66}... | collective-permute-start | bytes 1769480 | tf_op jit(solution)/shard_map/ppermute | solution.py:70
  58.5 26.0 %collective-permute-start.9 = (bf16[96,3072]{1,0:T(8,128)(2,1)S(1)}, bf16[96,3072]{1,0:T(8,128)(2,1)S(1)}, u32[]{:S(2)}, u32[]{:S(2)}) collective-permute-start(bf16[96,3072]{1,0:T(8,128)(2,1)S(1)} %constant_dynamic-update-slice_fusion), channel_id=1, source_target_pairs={{0,32},{32,64},{64,96},{96,0},{1,33},{33,65},{65,97},{97,1},{2,34}... | collective-permute-start | bytes 1769480 | tf_op jit(solution)/shard_map/ppermute | solution.py:70
  60.7 36.5 %collective-permute-start.3 = (bf16[4,96,3200]{2,1,0:T(8,128)(2,1)S(1)}, bf16[4,96,3200]{2,1,0:T(8,128)(2,1)}, u32[]{:S(2)}, u32[]{:S(2)}) collective-permute-start(bf16[4,96,3200]{2,1,0:T(8,128)(2,1)S(1)} %pad_maximum_fusion.1.refs_0_), channel_id=1, source_target_pairs={{0,16},{16,0},{1,17},{17,1},{2,18},{18,2},{3,19},{19,3},{4,20},{20... | collective-permute-start | bytes 7372808 | tf_op jit(solution)/shard_map/ppermute | solution.py:83
  159.6 33.2 %all-to-all-start = ((bf16[16,64,768]{2,1,0:T(8,128)(2,1)}), bf16[16,64,768]{2,1,0:T(8,128)(2,1)}, u32[]{:S(2)}, u32[]{:S(2)}) async-start(bf16[16,64,768]{2,1,0:T(8,128)(2,1)} %pad_maximum_fusion.5), calls=%async_computation | async-start | bytes 3145728 | tf_op jit(solution)/shard_map/all_to_all | solution.py:354
  167.7 38.6 %all-gather.12.cloned.1.call-start = ((), (), s32[]{:S(2)}) async-start(), calls=%async_computation.19 | async-start | bytes 2949120 | tf_op jit(solution)/shard_map/all_gather | solution.py:462
  223.3 30.4 %all-to-all-start.1 = ((bf16[16,64,768]{2,1,0:T(8,128)(2,1)}), bf16[16,64,768]{2,1,0:T(8,128)(2,1)}, u32[]{:S(2)}, u32[]{:S(2)}) async-start(bf16[16,64,768]{2,1,0:T(8,128)(2,1)} %pad_maximum_fusion.8), calls=%async_computation.1 | async-start | bytes 3145728 | tf_op jit(solution)/shard_map/all_to_all | solution.py:371
  227.7 157.0 %reduce-scatter.8.cloned.1.call-start = ((), (), s32[]{:S(2)}) async-start(), calls=%async_computation.15 | async-start | bytes 5308416 | tf_op jit(solution)/shard_map/reduce_scatter | solution.py:211
  282.5 103.5 %reduce-scatter.10.cloned.1.call-start = ((), (), s32[]{:S(2)}) async-start(), calls=%async_computation.16 | async-start | bytes 5308416 | tf_op jit(solution)/shard_map/reduce_scatter | solution.py:211
  287.6 136.2 %reduce-scatter.6.cloned.1.call-start = ((), (), s32[]{:S(2)}) async-start(), calls=%async_computation.14 | async-start | bytes 5308416 | tf_op jit(solution)/shard_map/reduce_scatter | solution.py:211
  294.6 169.8 %reduce-scatter.12.cloned.1.call-start = ((), (), s32[]{:S(2)}) async-start(), calls=%async_computation.17 | async-start | bytes 2949120 | tf_op jit(solution)/shard_map/reduce_scatter | solution.py:378
  336.7 156.3 %reduce-scatter.14.cloned.1.call-start = ((), (), s32[]{:S(2)}) async-start(), calls=%async_computation.18 | async-start | bytes 2949120 | tf_op jit(solution)/shard_map/reduce_scatter | solution.py:375
  345.8 36.4 %collective-permute-start.18 = (bf16[96,3200]{1,0:T(8,128)(2,1)}, bf16[96,3200]{1,0:T(8,128)(2,1)}, u32[]{:S(2)}, u32[]{:S(2)}) collective-permute-start(bf16[96,3200]{1,0:T(8,128)(2,1)} %get-tuple-element.124), channel_id=1, source_target_pairs={{0,64},{32,96},{64,0},{96,32},{1,65},{33,97},{65,1},{97,33},{2,66}... | collective-permute-start | bytes 1843208 | tf_op jit(solution)/shard_map/ppermute | solution.py:70
  349.0 33.2 %collective-permute-start.17 = (bf16[96,3200]{1,0:T(8,128)(2,1)S(1)}, bf16[96,3200]{1,0:T(8,128)(2,1)}, u32[]{:S(2)}, u32[]{:S(2)}) collective-permute-start(bf16[96,3200]{1,0:T(8,128)(2,1)S(1)} %get-tuple-element.122), channel_id=1, source_target_pairs={{0,32},{32,64},{64,96},{96,0},{1,33},{33,65},{65,97},{97,1},{2,34}... | collective-permute-start | bytes 1843208 | tf_op jit(solution)/shard_map/ppermute | solution.py:70
  388.2 38.1 %all-to-all-start.4 = ((bf16[16,48,768]{2,1,0:T(8,128)(2,1)}), bf16[16,48,768]{2,1,0:T(8,128)(2,1)S(1)}, u32[]{:S(2)}, u32[]{:S(2)}) async-start(bf16[16,48,768]{2,1,0:T(8,128)(2,1)} %pad_maximum_fusion.10), calls=%async_computation.7 | async-start | bytes 2359296 | tf_op jit(solution)/shard_map/all_to_all | solution.py:227
  427.3 29.9 %all-to-all-start.2 = ((bf16[16,56,768]{2,1,0:T(8,128)(2,1)}), bf16[16,56,768]{2,1,0:T(8,128)(2,1)S(1)}, u32[]{:S(2)}, u32[]{:S(2)}) async-start(bf16[16,56,768]{2,1,0:T(8,128)(2,1)} %fusion.21), calls=%async_computation.3 | async-start | bytes 2752512 | tf_op jit(solution)/shard_map/all_to_all | solution.py:227
  458.3 26.9 %all-to-all-start.5 = ((bf16[16,48,768]{2,1,0:T(8,128)(2,1)}), bf16[16,48,768]{2,1,0:T(8,128)(2,1)}, u32[]{:S(2)}, u32[]{:S(2)}) async-start(bf16[16,48,768]{2,1,0:T(8,128)(2,1)} %broadcast_in_dim.33), calls=%async_computation.8 | async-start | bytes 2359296 | tf_op jit(solution)/shard_map/all_to_all | solution.py:230
  486.3 26.2 %all-to-all-start.3 = ((bf16[16,56,768]{2,1,0:T(8,128)(2,1)}), bf16[16,56,768]{2,1,0:T(8,128)(2,1)S(1)}, u32[]{:S(2)}, u32[]{:S(2)}) async-start(bf16[16,56,768]{2,1,0:T(8,128)(2,1)} %broadcast_in_dim.32), calls=%async_computation.4 | async-start | bytes 2752512 | tf_op jit(solution)/shard_map/all_to_all | solution.py:230
  (170 other events, 913.7 us)
Sparse Core Ops, SparseCore 0:
  26.3 35.4 all-gather.5
  64.1 32.9 all-gather.7
  98.7 31.1 all-gather.9
  169.9 32.2 all-gather.11
  282.6 32.5 reduce-scatter.7
  317.5 55.1 reduce-scatter.9
  375.1 48.7 reduce-scatter.5
  426.3 32.6 reduce-scatter.11
  461.4 31.5 reduce-scatter.13

commit v4 on v3

--- a/solution.py
+++ b/solution.py
@@ -81,6 +81,14 @@
 
 def core_swap(block):
     return lax.ppermute(block, "core", [(0, 1), (1, 0)])
+
+
+def after(block, earlier):
+    return jnp.where(earlier == earlier, block, jnp.zeros_like(block))
+
+
+def mark(*blocks):
+    return sum(block[(0,) * block.ndim].astype(jnp.float32) for block in blocks)
 
 
 def place(spots, sources, shapes, moves, count):
@@ -207,10 +215,9 @@
     return sums
 
 
-def scatter_whole(part):
-    return lax.psum_scatter(
-        part.astype(jnp.bfloat16), ("x", "core"), scatter_dimension=0, tiled=True
-    )
+def scatter_whole(part, earlier):
+    low = after(part.astype(jnp.bfloat16), earlier)
+    return lax.psum_scatter(low, ("x", "core"), scatter_dimension=0, tiled=True)
 
 
 def sum_over_zy(shares, small):
@@ -312,12 +319,12 @@
     return (stream + product(hidden, down_w), (normed, saved, slope, hidden))
 
 
-def dense_backward(grad, gain, up_w, down_w, kept):
+def dense_backward(grad, gain, up_w, down_w, kept, earlier):
     normed, saved, slope, hidden = kept
     grad_low = grad.astype(jnp.bfloat16)
     pre_grad = (product_bt(grad_low, down_w) * slope).astype(jnp.bfloat16)
-    up_grad = scatter_whole(product_t(normed, pre_grad))
-    down_grad = scatter_whole(product_t(hidden, grad_low))
+    up_grad = scatter_whole(product_t(normed, pre_grad), earlier)
+    down_grad = scatter_whole(product_t(hidden, grad_low), earlier)
     stream_grad, gain_grad = norm_back(product_bt(pre_grad, up_w), gain, saved)
     return (grad + stream_grad, (gain_grad, up_grad, down_grad))
 
@@ -372,12 +379,12 @@
     result_rows = returned[:, :SLOTS].reshape(slots, width)
     back_rows = returned[:, SLOTS:].reshape(slots, width)
 
-    down_grad = lax.psum_scatter(
-        product_t(hidden, flat_grad).astype(jnp.bfloat16), "x", scatter_dimension=0, tiled=True
-    ).astype(jnp.float32)
-    up_grad = lax.psum_scatter(
-        product_t(pre_grad, flat).astype(jnp.bfloat16), "x", scatter_dimension=0, tiled=True
-    )
+    down_low = product_t(hidden, flat_grad).astype(jnp.bfloat16)
+    up_low = product_t(pre_grad, flat).astype(jnp.bfloat16)
+    made = mark(down_low, up_low)
+    down_grad = lax.psum_scatter(down_low, "x", scatter_dimension=0, tiled=True)
+    up_grad = lax.psum_scatter(up_low, "x", scatter_dimension=0, tiled=True)
+    down_grad = down_grad.astype(jnp.float32)
     up_grad = up_grad.astype(jnp.float32).T
 
     first = product(pick_first.astype(jnp.bfloat16), result_rows)
@@ -391,7 +398,7 @@
     router_grad = product_t(normed, logit_grad)
     normed_grad = product_bt(logit_grad, router) + product(select, back_rows)
     stream_grad, gain_grad = norm_back(normed_grad, gain, saved)
-    return (new_stream, grad + stream_grad, (gain_grad, router_grad, up_grad, down_grad))
+    return (new_stream, grad + stream_grad, (gain_grad, router_grad, up_grad, down_grad), made)
 
 
 def shards(
@@ -464,7 +471,7 @@
     stream_one, kept_one = attend_forward(stream, gain_aa, in_aa, out_aa, images, length)
     stream_two, kept_two = dense_forward(stream_one, gain_dd, up_dd, down_dd)
     stream_three, kept_three = attend_forward(stream_two, gain_bb, in_bb, out_bb, images, length)
-    stream_four, grad, moe_grads = moe(
+    stream_four, grad, moe_grads, made = moe(
         stream_three,
         output_grad.reshape(rows, width),
         gain_mm,
@@ -476,11 +483,13 @@
         flat_keep,
     )
     output = stream_four.astype(jnp.bfloat16).reshape(images, length, width)
+    grad = after(grad, made)
     grad, attn_b_grads = attend_backward(
         grad, gain_bb, in_bb, out_bb, kept_three, images, length, product_t
     )
-    share_b = scatter_whole(jnp.concatenate(attn_b_grads[1:], axis=1))
-    grad, dense_grads = dense_backward(grad, gain_dd, up_dd, down_dd, kept_two)
+    sent = mark(moe_grads[2], moe_grads[3])
+    share_b = scatter_whole(jnp.concatenate(attn_b_grads[1:], axis=1), sent)
+    grad, dense_grads = dense_backward(grad, gain_dd, up_dd, down_dd, kept_two, sent)
     grad, attn_a_grads = attend_backward(
         grad, gain_aa, in_aa, out_aa, kept_one, images, length, weight_grad
     )

time: 533 us -> 546 us (1.024)
  matrix products: 91.5 us -> 98.1 us
    all_to_all x1, waiting for transfers between devices: 24.3 us -> 15.5 us  [moe(): lax.all_to_all(back, ('z', 'y'), split_axis=0, concat_axis=0, tiled=True)]
    all_to_all x2, waiting for transfers between devices: 30.6 us -> 36.4 us  [sum_over_zy(): lax.all_to_all(copies, ('z', 'y'), split_axis=0, concat_axis=0, tiled=True)]
    reduce_scatter x5 -> x4, waiting for transfers between devices: 31.9 us -> 27.9 us  [the longest x3 27.9 us: scatter_whole(): return lax.psum_scatter(low, ('x', 'core'), scatter_dimension=0, tiled=True)]
    unnamed x328 -> x320, local copies, waits for them, and re-layouts: 32.5 us -> 32.2 us
  transfers between devices with their start and end apart: 35 -> 35, of which waited for: 19 -> 21; matrix products, arithmetic and copies ran while one was open for 27% -> 31% of each run, Pallas kernels for 4% -> 4%
where the time goes in v4:
time: 546 us; the launch traced here: 538 us
  waiting for transfers between devices  231 us (42%)
  matrix products  98.1 us (18%)
  local copies, waits for them, and re-layouts  71.3 us (13%)
  starting transfers between devices  50.2 us (9%)
  other arithmetic  45.2 us (8%)
  Pallas kernels  22.7 us (4%)
  between operations  19.3 us (4%)
    ppermute x12, waiting for transfers between devices, shift(): return lax.ppermute(block, axis, [(i, (i + step) % X) for i in range(X)])  92.7 us
    all_to_all x2, waiting for transfers between devices, sum_over_zy(): lax.all_to_all(copies, ('z', 'y'), split_axis=0, concat_axis=0, tiled=True)  36.4 us
    unnamed x320, local copies, waits for them, and re-layouts  32.2 us
    dot_general x9, matrix products, product_bt(): lax.dot_general(left, right, (((1,), (1,)), ((), ())), preferred_element_...  29.9 us
    reduce_scatter x3, waiting for transfers between devices, scatter_whole(): return lax.psum_scatter(low, ('x', 'core'), scatter_dimension=0, tiled=True)  27.9 us
    dot_general x16, matrix products, product(): return jnp.dot(left, right, preferred_element_type=jnp.float32)  27.4 us
    dot_general x9, matrix products, product_t(): lax.dot_general(left, right, (((0,), (0,)), ((), ())), preferred_element_...  24.6 us
    all_to_all x1, waiting for transfers between devices, moe(): lax.all_to_all(send, ('z', 'y'), split_axis=0, concat_axis=0, tiled=True)  24.4 us
  transfers between devices with their start and end apart: 35, of which 21 were waited for; matrix products, arithmetic and copies ran while one was open for 31% of the time, Pallas kernels for 4%

profile of v4, /device:TPU:6, one launch (start us, length us, event | category | flops | bytes accessed | tf_op | source)
XLA Modules:
  0.0 537.5 jit_solution(474445046744061508)
XLA Ops:
  11.2 7.0 %collective-permute-done.4 = bf16[192,768]{1,0:T(8,128)(2,1)S(1)} collective-permute-done((bf16[192,768]{1,0:T(8,128)(2,1)S(1)}, bf16[192,768]{1,0:T(8,128)(2,1)S(1)}, u32[]{:S(2)}, u32[]{:S(2)}) %collective-permute-start.4) | collective-permute-done | bytes 294944 | tf_op jit(solution)/shard_map/ppermute | solution.py:70
  34.8 21.0 %collective-permute-done = bf16[96,3200]{1,0:T(8,128)(2,1)S(1)} collective-permute-done((bf16[96,3200]{1,0:T(8,128)(2,1)S(1)}, bf16[96,3200]{1,0:T(8,128)(2,1)S(1)}, u32[]{:S(2)}, u32[]{:S(2)}) %collective-permute-start) | collective-permute-done | bytes 614432 | tf_op jit(solution)/shard_map/ppermute | solution.py:70
  61.2 9.4 %collective-permute-done.9 = bf16[96,3072]{1,0:T(8,128)(2,1)S(1)} collective-permute-done((bf16[96,3072]{1,0:T(8,128)(2,1)S(1)}, bf16[96,3072]{1,0:T(8,128)(2,1)S(1)}, u32[]{:S(2)}, u32[]{:S(2)}) %collective-permute-start.9) | collective-permute-done | bytes 589856 | tf_op jit(solution)/shard_map/ppermute | solution.py:70
  73.3 10.5 %collective-permute-done.11 = bf16[96,3072]{1,0:T(8,128)(2,1)S(1)} collective-permute-done((bf16[96,3072]{1,0:T(8,128)(2,1)S(1)}, bf16[96,3072]{1,0:T(8,128)(2,1)S(1)}, u32[]{:S(2)}, u32[]{:S(2)}) %collective-permute-start.11) | collective-permute-done | bytes 589856 | tf_op jit(solution)/shard_map/ppermute | solution.py:70
  120.5 5.9 %shard_map.290 = bf16[8,96,3072]{2,1,0:T(8,128)(2,1)S(1)} custom-call(s32[32]{0:T(128)S(1)} %stack.197.spots_ref, bf16[16,96,768]{2,1,0:T(8,128)(2,1)S(1)} %copy-done.16, bf16[16,96,768]{2,1,0:T(8,128)(2,1)} %collective-permute-done.7.refs_1_), custom_call_target="tpu_custom_call" | custom-call | bytes 9437184 | tf_op jit(solution)/shard_map/pallas_call | solution.py:122
  129.9 10.4 %shard_map.291 = bf16[8,4,96,768]{3,2,1,0:T(8,128)(2,1)S(1)} custom-call(s32[32]{0:T(128)S(1)} %stack.197.spots_ref, bf16[16,96,768]{2,1,0:T(8,128)(2,1)S(1)} %copy-done.17, bf16[16,96,768]{2,1,0:T(8,128)(2,1)} %collective-permute-done.8.refs_1_), custom_call_target="tpu_custom_call" | custom-call | bytes 9437184 | tf_op jit(solution)/shard_map/pallas_call | solution.py:122
  158.7 8.2 %all-to-all-start = ((bf16[16,64,768]{2,1,0:T(8,128)(2,1)}), bf16[16,64,768]{2,1,0:T(8,128)(2,1)}, u32[]{:S(2)}, u32[]{:S(2)}) async-start(bf16[16,64,768]{2,1,0:T(8,128)(2,1)} %pad_maximum_fusion.4), calls=%async_computation | async-start | bytes 3145728 | tf_op jit(solution)/shard_map/all_to_all | solution.py:361
  167.5 24.4 %all-to-all-done = bf16[16,64,768]{2,1,0:T(8,128)(2,1)} async-done(((bf16[16,64,768]{2,1,0:T(8,128)(2,1)}), bf16[16,64,768]{2,1,0:T(8,128)(2,1)}, u32[]{:S(2)}, u32[]{:S(2)}) %all-to-all-start) | async-done | bytes 1572896 | tf_op jit(solution)/shard_map/all_to_all | solution.py:361
  198.7 7.0 %multiply_convert_fusion = (bf16[1024,1536]{1,0:T(8,128)(2,1)}, f32[1024,1536]{1,0:T(8,128)}) fusion(bf16[1024,768]{1,0:T(8,128)(2,1)} %bitcast.367, bf16[1536,768]{0,1:T(8,128)(2,1)} %all-gather.10.cloned.1.call-done), kind=kOutput, calls=%fused_computation.7 | convolution fusion | flops 2423783424 | bytes 13369344 | tf_op jit(solution)/shard_map/dot_general | solution.py:27
  205.7 6.8 %fusion.5 = bf16[1024,1536]{1,0:T(8,128)(2,1)S(1)} fusion(f32[1024,1536]{1,0:T(8,128)} %get-tuple-element.199, bf16[1024,768]{1,0:T(8,128)(2,1)} %bitcast.365, bf16[1,1536,768]{2,1,0:T(8,128)(2,1)} %all-gather.12.cloned.1.call-done), kind=kOutput, calls=%fused_computation.6 | convolution fusion | flops 2431647744 | bytes 13369344 | tf_op jit(solution)/shard_map/dot_general | solution.py:27
  218.1 5.4 fusion.13
  237.4 6.5 %convolution_convert_fusion.7 = bf16[1536,768]{1,0:T(8,128)(2,1)} fusion(bf16[1024,1536]{1,0:T(8,128)(2,1)} %get-tuple-element.198, bf16[1024,768]{1,0:T(8,128)(2,1)} %bitcast.366), kind=kOutput, calls=%fused_computation.23 | convolution fusion | flops 2417098752 | bytes 7077888 | tf_op jit(solution)/shard_map/dot_general | solution.py:21
  246.6 15.5 %all-to-all-done.1 = bf16[16,64,768]{2,1,0:T(8,128)(2,1)} async-done(((bf16[16,64,768]{2,1,0:T(8,128)(2,1)}), bf16[16,64,768]{2,1,0:T(8,128)(2,1)}, u32[]{:S(2)}, u32[]{:S(2)}) %all-to-all-start.1) | async-done | bytes 1572896 | tf_op jit(solution)/shard_map/all_to_all | solution.py:378
  293.4 5.1 broadcast_select_fusion.1
  298.6 5.1 broadcast_select_fusion
  307.4 5.5 %multiply_reduce_fusion.6 = (f32[768]{0:T(1024)}, f32[197]{0:T(256)S(1)}, f32[197]{0:T(256)S(1)}, f32[197,768]{1,0:T(8,128)S(1)}) fusion(f32[197,768]{1,0:T(8,128)} %copy-done.32, f32[197]{0:T(256)} %copy-done.136, f32[197]{0:T(256)} %copy-done.120, f32[768]{0:T(1024)} %copy-done.89, bf16[197,3072]{1,0:T(8,128)(2,1)} %fusion.6, bf16[768,3072]{1,0:T(8,128)(2,1)} %bitcast.317), kind=kOutput, calls=%fused_computation.150 | convolution fusion | flops 930771840 | bytes 7148624 | tf_op jit(solution)/shard_map/dot_general | solution.py:27
  365.5 18.8 %collective-permute-done.17 = bf16[96,3200]{1,0:T(8,128)(2,1)S(1)} collective-permute-done((bf16[96,3200]{1,0:T(8,128)(2,1)S(1)}, bf16[96,3200]{1,0:T(8,128)(2,1)S(1)}, u32[]{:S(2)}, u32[]{:S(2)}) %collective-permute-start.17) | collective-permute-done | bytes 614432 | tf_op jit(solution)/shard_map/ppermute | solution.py:70
  385.2 13.9 %collective-permute-done.19 = bf16[96,3200]{1,0:T(8,128)(2,1)S(1)} collective-permute-done((bf16[96,3200]{1,0:T(8,128)(2,1)S(1)}, bf16[96,3200]{1,0:T(8,128)(2,1)S(1)}, u32[]{:S(2)}, u32[]{:S(2)}) %collective-permute-start.19) | collective-permute-done | bytes 614432 | tf_op jit(solution)/shard_map/ppermute | solution.py:70
  405.0 4.8 all-to-all-start.4
  411.2 27.8 %reduce-scatter.10.cloned.1.call-done = bf16[96,3072]{1,0:T(8,128)(2,1)} async-done(((bf16[768,3072]{1,0:T(8,128)(2,1)}), bf16[96,3072]{1,0:T(8,128)(2,1)}) %reduce-scatter.10.cloned.1.call-update) | async-done | bytes 589840 | tf_op jit(solution)/shard_map/reduce_scatter | solution.py:220
  441.4 6.9 %all-to-all-start.2 = ((bf16[16,56,768]{2,1,0:T(8,128)(2,1)}), bf16[16,56,768]{2,1,0:T(8,128)(2,1)}, u32[]{:S(2)}, u32[]{:S(2)}) async-start(bf16[16,56,768]{2,1,0:T(8,128)(2,1)} %fusion.21), calls=%async_computation.4 | async-start | bytes 2752512 | tf_op jit(solution)/shard_map/all_to_all | solution.py:234
  448.5 22.7 %all-to-all-done.2 = bf16[16,56,768]{2,1,0:T(8,128)(2,1)} async-done(((bf16[16,56,768]{2,1,0:T(8,128)(2,1)}), bf16[16,56,768]{2,1,0:T(8,128)(2,1)}, u32[]{:S(2)}, u32[]{:S(2)}) %all-to-all-start.2) | async-done | bytes 1376288 | tf_op jit(solution)/shard_map/all_to_all | solution.py:234
  479.5 18.5 %all-to-all-done.5 = bf16[16,48,768]{2,1,0:T(8,128)(2,1)S(1)} async-done(((bf16[16,48,768]{2,1,0:T(8,128)(2,1)}), bf16[16,48,768]{2,1,0:T(8,128)(2,1)S(1)}, u32[]{:S(2)}, u32[]{:S(2)}) %all-to-all-start.5) | async-done | bytes 1179680 | tf_op jit(solution)/shard_map/all_to_all | solution.py:237
  507.4 17.9 %all-to-all-done.3 = bf16[16,56,768]{2,1,0:T(8,128)(2,1)S(1)} async-done(((bf16[16,56,768]{2,1,0:T(8,128)(2,1)}), bf16[16,56,768]{2,1,0:T(8,128)(2,1)S(1)}, u32[]{:S(2)}, u32[]{:S(2)}) %all-to-all-start.3) | async-done | bytes 1376288 | tf_op jit(solution)/shard_map/all_to_all | solution.py:237
  (565 shorter events, 233.1 us)
Async XLA Ops:
  7.2 98.0 %all-gather.6.cloned.1.call-start = ((), (), s32[]{:S(2)}) async-start(), calls=%async_computation.11 | async-start | bytes 2949120 | tf_op jit(solution)/shard_map/all_gather | solution.py:160
  26.0 84.5 %all-gather.8.cloned.1.call-start = ((), (), s32[]{:S(2)}) async-start(), calls=%async_computation.12 | async-start | bytes 2949120 | tf_op jit(solution)/shard_map/all_gather | solution.py:161
  26.9 171.7 %all-gather.10.cloned.1.call-start = ((), (), s32[]{:S(2)}) async-start(), calls=%async_computation.13 | async-start | bytes 2949120 | tf_op jit(solution)/shard_map/all_gather | solution.py:468
  27.9 27.9 %collective-permute-start = (bf16[96,3200]{1,0:T(8,128)(2,1)S(1)}, bf16[96,3200]{1,0:T(8,128)(2,1)S(1)}, u32[]{:S(2)}, u32[]{:S(2)}) collective-permute-start(bf16[96,3200]{1,0:T(8,128)(2,1)S(1)} %concatenate.82), channel_id=1, source_target_pairs={{0,32},{32,64},{64,96},{96,0},{1,33},{33,65},{65,97},{97,1},{2,34}... | collective-permute-start | bytes 1843208 | tf_op jit(solution)/shard_map/ppermute | solution.py:70
  29.1 29.8 %collective-permute-start.1 = (bf16[96,3200]{1,0:T(8,128)(2,1)S(1)}, bf16[96,3200]{1,0:T(8,128)(2,1)S(1)}, u32[]{:S(2)}, u32[]{:S(2)}) collective-permute-start(bf16[96,3200]{1,0:T(8,128)(2,1)S(1)} %concatenate.82), channel_id=1, source_target_pairs={{0,64},{32,96},{64,0},{96,32},{1,65},{33,97},{65,1},{97,33},{2,66}... | collective-permute-start | bytes 1843208 | tf_op jit(solution)/shard_map/ppermute | solution.py:70
  31.1 29.6 %collective-permute-start.2 = (bf16[96,3200]{1,0:T(8,128)(2,1)S(1)}, bf16[96,3200]{1,0:T(8,128)(2,1)S(1)}, u32[]{:S(2)}, u32[]{:S(2)}) collective-permute-start(bf16[96,3200]{1,0:T(8,128)(2,1)S(1)} %concatenate.82), channel_id=1, source_target_pairs={{0,96},{32,0},{64,32},{96,64},{1,97},{33,1},{65,33},{97,65},{2,98}... | collective-permute-start | bytes 1843208 | tf_op jit(solution)/shard_map/ppermute | solution.py:70
  31.2 39.3 %collective-permute-start.9 = (bf16[96,3072]{1,0:T(8,128)(2,1)S(1)}, bf16[96,3072]{1,0:T(8,128)(2,1)S(1)}, u32[]{:S(2)}, u32[]{:S(2)}) collective-permute-start(bf16[96,3072]{1,0:T(8,128)(2,1)S(1)} %constant_dynamic-update-slice_fusion), channel_id=1, source_target_pairs={{0,32},{32,64},{64,96},{96,0},{1,33},{33,65},{65,97},{97,1},{2,34}... | collective-permute-start | bytes 1769480 | tf_op jit(solution)/shard_map/ppermute | solution.py:70
  34.5 38.8 %collective-permute-start.10 = (bf16[96,3072]{1,0:T(8,128)(2,1)S(1)}, bf16[96,3072]{1,0:T(8,128)(2,1)S(1)}, u32[]{:S(2)}, u32[]{:S(2)}) collective-permute-start(bf16[96,3072]{1,0:T(8,128)(2,1)S(1)} %constant_dynamic-update-slice_fusion), channel_id=1, source_target_pairs={{0,64},{32,96},{64,0},{96,32},{1,65},{33,97},{65,1},{97,33},{2,66}... | collective-permute-start | bytes 1769480 | tf_op jit(solution)/shard_map/ppermute | solution.py:70
  55.8 28.0 %collective-permute-start.11 = (bf16[96,3072]{1,0:T(8,128)(2,1)S(1)}, bf16[96,3072]{1,0:T(8,128)(2,1)S(1)}, u32[]{:S(2)}, u32[]{:S(2)}) collective-permute-start(bf16[96,3072]{1,0:T(8,128)(2,1)S(1)} %constant_dynamic-update-slice_fusion), channel_id=1, source_target_pairs={{0,96},{32,0},{64,32},{96,64},{1,97},{33,1},{65,33},{97,65},{2,98}... | collective-permute-start | bytes 1769480 | tf_op jit(solution)/shard_map/ppermute | solution.py:70
  61.1 35.4 %collective-permute-start.3 = (bf16[4,96,3200]{2,1,0:T(8,128)(2,1)S(1)}, bf16[4,96,3200]{2,1,0:T(8,128)(2,1)}, u32[]{:S(2)}, u32[]{:S(2)}) collective-permute-start(bf16[4,96,3200]{2,1,0:T(8,128)(2,1)S(1)} %pad_maximum_fusion.refs_0_), channel_id=1, source_target_pairs={{0,16},{16,0},{1,17},{17,1},{2,18},{18,2},{3,19},{19,3},{4,20},{20... | collective-permute-start | bytes 7372808 | tf_op jit(solution)/shard_map/ppermute | solution.py:83
  158.7 33.2 %all-to-all-start = ((bf16[16,64,768]{2,1,0:T(8,128)(2,1)}), bf16[16,64,768]{2,1,0:T(8,128)(2,1)}, u32[]{:S(2)}, u32[]{:S(2)}) async-start(bf16[16,64,768]{2,1,0:T(8,128)(2,1)} %pad_maximum_fusion.4), calls=%async_computation | async-start | bytes 3145728 | tf_op jit(solution)/shard_map/all_to_all | solution.py:361
  166.9 38.8 %all-gather.12.cloned.1.call-start = ((), (), s32[]{:S(2)}) async-start(), calls=%async_computation.18 | async-start | bytes 2949120 | tf_op jit(solution)/shard_map/all_gather | solution.py:469
  167.5 118.5 %reduce-scatter.16.cloned.1.call-start = ((), (), s32[]{:S(2)}) async-start(), calls=%async_computation.19 | async-start | bytes 2949120
  230.4 31.7 %all-to-all-start.1 = ((bf16[16,64,768]{2,1,0:T(8,128)(2,1)}), bf16[16,64,768]{2,1,0:T(8,128)(2,1)}, u32[]{:S(2)}, u32[]{:S(2)}) async-start(bf16[16,64,768]{2,1,0:T(8,128)(2,1)} %pad_maximum_fusion.7), calls=%async_computation.1 | async-start | bytes 3145728 | tf_op jit(solution)/shard_map/all_to_all | solution.py:378
  234.8 56.1 %reduce-scatter.8.cloned.1.call-start = ((), (), s32[]{:S(2)}) async-start(), calls=%async_computation.14 | async-start | bytes 2949120 | tf_op jit(solution)/shard_map/reduce_scatter | solution.py:385
  246.4 155.3 %reduce-scatter.12.cloned.1.call-start = ((), (), s32[]{:S(2)}) async-start(), calls=%async_computation.16 | async-start | bytes 5308416 | tf_op jit(solution)/shard_map/reduce_scatter | solution.py:220
  298.5 104.3 %reduce-scatter.14.cloned.1.call-start = ((), (), s32[]{:S(2)}) async-start(), calls=%async_computation.17 | async-start | bytes 5308416 | tf_op jit(solution)/shard_map/reduce_scatter | solution.py:220
  303.7 135.3 %reduce-scatter.10.cloned.1.call-start = ((), (), s32[]{:S(2)}) async-start(), calls=%async_computation.15 | async-start | bytes 5308416 | tf_op jit(solution)/shard_map/reduce_scatter | solution.py:220
  362.7 21.6 %collective-permute-start.17 = (bf16[96,3200]{1,0:T(8,128)(2,1)S(1)}, bf16[96,3200]{1,0:T(8,128)(2,1)S(1)}, u32[]{:S(2)}, u32[]{:S(2)}) collective-permute-start(bf16[96,3200]{1,0:T(8,128)(2,1)S(1)} %get-tuple-element.122), channel_id=1, source_target_pairs={{0,32},{32,64},{64,96},{96,0},{1,33},{33,65},{65,97},{97,1},{2,34}... | collective-permute-start | bytes 1843208 | tf_op jit(solution)/shard_map/ppermute | solution.py:70
  364.9 34.2 %collective-permute-start.19 = (bf16[96,3200]{1,0:T(8,128)(2,1)S(1)}, bf16[96,3200]{1,0:T(8,128)(2,1)S(1)}, u32[]{:S(2)}, u32[]{:S(2)}) collective-permute-start(bf16[96,3200]{1,0:T(8,128)(2,1)S(1)} %get-tuple-element.123), channel_id=1, source_target_pairs={{0,96},{32,0},{64,32},{96,64},{1,97},{33,1},{65,33},{97,65},{2,98}... | collective-permute-start | bytes 1843208 | tf_op jit(solution)/shard_map/ppermute | solution.py:70
  405.0 36.4 %all-to-all-start.4 = ((bf16[16,48,768]{2,1,0:T(8,128)(2,1)}), bf16[16,48,768]{2,1,0:T(8,128)(2,1)S(1)}, u32[]{:S(2)}, u32[]{:S(2)}) async-start(bf16[16,48,768]{2,1,0:T(8,128)(2,1)} %pad_maximum_fusion.9), calls=%async_computation.8 | async-start | bytes 2359296 | tf_op jit(solution)/shard_map/all_to_all | solution.py:234
  441.4 29.8 %all-to-all-start.2 = ((bf16[16,56,768]{2,1,0:T(8,128)(2,1)}), bf16[16,56,768]{2,1,0:T(8,128)(2,1)}, u32[]{:S(2)}, u32[]{:S(2)}) async-start(bf16[16,56,768]{2,1,0:T(8,128)(2,1)} %fusion.21), calls=%async_computation.4 | async-start | bytes 2752512 | tf_op jit(solution)/shard_map/all_to_all | solution.py:234
  472.3 25.8 %all-to-all-start.5 = ((bf16[16,48,768]{2,1,0:T(8,128)(2,1)}), bf16[16,48,768]{2,1,0:T(8,128)(2,1)S(1)}, u32[]{:S(2)}, u32[]{:S(2)}) async-start(bf16[16,48,768]{2,1,0:T(8,128)(2,1)} %broadcast_in_dim.33), calls=%async_computation.9 | async-start | bytes 2359296 | tf_op jit(solution)/shard_map/all_to_all | solution.py:237
  499.5 25.8 %all-to-all-start.3 = ((bf16[16,56,768]{2,1,0:T(8,128)(2,1)}), bf16[16,56,768]{2,1,0:T(8,128)(2,1)S(1)}, u32[]{:S(2)}, u32[]{:S(2)}) async-start(bf16[16,56,768]{2,1,0:T(8,128)(2,1)} %broadcast_in_dim.31), calls=%async_computation.5 | async-start | bytes 2752512 | tf_op jit(solution)/shard_map/all_to_all | solution.py:237
  (166 other events, 859.6 us)
Sparse Core Ops, SparseCore 0:
  26.1 35.7 all-gather.5
  64.1 32.9 all-gather.7
  98.8 31.1 all-gather.9
  169.1 32.2 all-gather.11
  218.2 27.5 reduce-scatter.15
  248.1 31.5 reduce-scatter.7
  298.7 32.0 reduce-scatter.11
  333.2 54.6 reduce-scatter.13
  390.3 48.6 reduce-scatter.9

commit v5 on v4

--- a/solution.py
+++ b/solution.py
@@ -215,9 +215,10 @@
     return sums
 
 
-def scatter_whole(part, earlier):
-    low = after(part.astype(jnp.bfloat16), earlier)
-    return lax.psum_scatter(low, ("x", "core"), scatter_dimension=0, tiled=True)
+def scatter_whole(part):
+    return lax.psum_scatter(
+        part.astype(jnp.bfloat16), ("x", "core"), scatter_dimension=0, tiled=True
+    )
 
 
 def sum_over_zy(shares, small):
@@ -323,8 +324,8 @@
     normed, saved, slope, hidden = kept
     grad_low = grad.astype(jnp.bfloat16)
     pre_grad = (product_bt(grad_low, down_w) * slope).astype(jnp.bfloat16)
-    up_grad = scatter_whole(product_t(normed, pre_grad), earlier)
-    down_grad = scatter_whole(product_t(hidden, grad_low), earlier)
+    up_grad = scatter_whole(product_t(after(normed, earlier), pre_grad))
+    down_grad = scatter_whole(product_t(hidden, after(grad_low, earlier)))
     stream_grad, gain_grad = norm_back(product_bt(pre_grad, up_w), gain, saved)
     return (grad + stream_grad, (gain_grad, up_grad, down_grad))
 
@@ -483,12 +484,16 @@
         flat_keep,
     )
     output = stream_four.astype(jnp.bfloat16).reshape(images, length, width)
+    sent = mark(moe_grads[2], moe_grads[3])
+
+    def late_product(left, right):
+        return product_t(after(left, sent), right)
+
     grad = after(grad, made)
     grad, attn_b_grads = attend_backward(
-        grad, gain_bb, in_bb, out_bb, kept_three, images, length, product_t
-    )
-    sent = mark(moe_grads[2], moe_grads[3])
-    share_b = scatter_whole(jnp.concatenate(attn_b_grads[1:], axis=1), sent)
+        grad, gain_bb, in_bb, out_bb, kept_three, images, length, late_product
+    )
+    share_b = scatter_whole(jnp.concatenate(attn_b_grads[1:], axis=1))
     grad, dense_grads = dense_backward(grad, gain_dd, up_dd, down_dd, kept_two, sent)
     grad, attn_a_grads = attend_backward(
         grad, gain_aa, in_aa, out_aa, kept_one, images, length, weight_grad
@@ -506,8 +511,10 @@
         *zip(attn_a_grads[1], attn_a_grads[2], split_rows(small_grad))
     )
     share_a = jnp.concatenate([in_a, out_a], axis=1)
-    (share_a, share_b), small_total = sum_over_zy([share_a, share_b], small_share)
-    up, down = sum_over_zy(dense_grads[1:], None)
+    (share_a, share_b, down), small_total = sum_over_zy(
+        [share_a, share_b, dense_grads[2]], small_share
+    )
+    (up,) = sum_over_zy([after(dense_grads[1], mark(share_a))], None)
     in_a, out_a = share_a[:, :wide_in], share_a[:, wide_in:]
     in_b, out_b = share_b[:, :wide_in], share_b[:, wide_in:]
     return (

time: 546 us -> 518 us (0.949)
  waiting for transfers between devices: 231 us -> 178 us
  blocking collectives: 0 us -> 33.8 us
  starting transfers between devices: 50.2 us -> 42.3 us
    all_to_all x0 -> x1, blocking collectives: none -> 33.8 us  [sum_over_zy(): lax.all_to_all(packed, ('z', 'y'), split_axis=0, concat_axis=0, tiled=True)]
    reduce_scatter x3, waiting for transfers between devices: 27.9 us -> 0.04 us  [scatter_whole(): lax.psum_scatter(part.astype(jnp.bfloat16), ('x', 'core'), scatter_dimens...]
    all_to_all x2 -> x1, waiting for transfers between devices: 22.7 us -> 7.26 us  [sum_over_zy(): lax.all_to_all(packed, ('z', 'y'), split_axis=0, concat_axis=0, tiled=True)]
    all_to_all x2 -> x1, starting transfers between devices: 11.7 us -> 4.26 us  [sum_over_zy(): lax.all_to_all(packed, ('z', 'y'), split_axis=0, concat_axis=0, tiled=True)]
    unnamed x320 -> x262, local copies, waits for them, and re-layouts: 32.2 us -> 30.4 us
  transfers between devices with their start and end apart: 35 -> 34, of which waited for: 21 -> 19; matrix products, arithmetic and copies ran while one was open for 31% -> 32% of each run, Pallas kernels for 4% -> 4%
where the time goes in v5:
time: 518 us; the launch traced here: 509 us
  waiting for transfers between devices  178 us (34%)
  matrix products  98.5 us (19%)
  local copies, waits for them, and re-layouts  68 us (13%)
  other arithmetic  44.8 us (9%)
  starting transfers between devices  42.3 us (8%)
  blocking collectives  33.8 us (7%)
  Pallas kernels  22.7 us (4%)
  between operations  20.1 us (4%)
    ppermute x12, waiting for transfers between devices, shift(): return lax.ppermute(block, axis, [(i, (i + step) % X) for i in range(X)])  93.2 us
    all_to_all x1, blocking collectives, sum_over_zy(): lax.all_to_all(packed, ('z', 'y'), split_axis=0, concat_axis=0, tiled=True)  33.8 us
    dot_general x9, matrix products, product_bt(): lax.dot_general(left, right, (((1,), (1,)), ((), ())), preferred_element_...  32.2 us
    all_to_all x2, waiting for transfers between devices, sum_over_zy(): lax.all_to_all(copies, ('z', 'y'), split_axis=0, concat_axis=0, tiled=True)  31.2 us
    unnamed x262, local copies, waits for them, and re-layouts  30.4 us
    dot_general x16, matrix products, product(): return jnp.dot(left, right, preferred_element_type=jnp.float32)  28.9 us
    dot_general x9, matrix products, product_t(): lax.dot_general(left, right, (((0,), (0,)), ((), ())), preferred_element_...  25.4 us
    all_to_all x1, waiting for transfers between devices, moe(): lax.all_to_all(send, ('z', 'y'), split_axis=0, concat_axis=0, tiled=True)  24.4 us
  transfers between devices with their start and end apart: 34, of which 19 were waited for; matrix products, arithmetic and copies ran while one was open for 32% of the time, Pallas kernels for 4%

profile of v5, /device:TPU:6, one launch (start us, length us, event | category | flops | bytes accessed | tf_op | source)
XLA Modules:
  0.0 508.6 jit_solution(17927675678053859905)
XLA Ops:
  11.2 7.0 %collective-permute-done.4 = bf16[192,768]{1,0:T(8,128)(2,1)S(1)} collective-permute-done((bf16[192,768]{1,0:T(8,128)(2,1)S(1)}, bf16[192,768]{1,0:T(8,128)(2,1)S(1)}, u32[]{:S(2)}, u32[]{:S(2)}) %collective-permute-start.4) | collective-permute-done | bytes 294944 | tf_op jit(solution)/shard_map/ppermute | solution.py:70
  20.3 4.8 collective-permute-done.6
  34.8 21.0 %collective-permute-done = bf16[96,3200]{1,0:T(8,128)(2,1)S(1)} collective-permute-done((bf16[96,3200]{1,0:T(8,128)(2,1)S(1)}, bf16[96,3200]{1,0:T(8,128)(2,1)S(1)}, u32[]{:S(2)}, u32[]{:S(2)}) %collective-permute-start) | collective-permute-done | bytes 614432 | tf_op jit(solution)/shard_map/ppermute | solution.py:70
  61.2 9.4 %collective-permute-done.9 = bf16[96,3072]{1,0:T(8,128)(2,1)S(1)} collective-permute-done((bf16[96,3072]{1,0:T(8,128)(2,1)S(1)}, bf16[96,3072]{1,0:T(8,128)(2,1)S(1)}, u32[]{:S(2)}, u32[]{:S(2)}) %collective-permute-start.9) | collective-permute-done | bytes 589856 | tf_op jit(solution)/shard_map/ppermute | solution.py:70
  73.3 10.5 %collective-permute-done.11 = bf16[96,3072]{1,0:T(8,128)(2,1)S(1)} collective-permute-done((bf16[96,3072]{1,0:T(8,128)(2,1)S(1)}, bf16[96,3072]{1,0:T(8,128)(2,1)S(1)}, u32[]{:S(2)}, u32[]{:S(2)}) %collective-permute-start.11) | collective-permute-done | bytes 589856 | tf_op jit(solution)/shard_map/ppermute | solution.py:70
  119.0 6.0 %shard_map.290 = bf16[8,96,3072]{2,1,0:T(8,128)(2,1)S(1)} custom-call(s32[32]{0:T(128)S(1)} %stack.197.spots_ref, bf16[16,96,768]{2,1,0:T(8,128)(2,1)S(1)} %copy-done.14, bf16[16,96,768]{2,1,0:T(8,128)(2,1)} %collective-permute-done.7.refs_1_), custom_call_target="tpu_custom_call" | custom-call | bytes 9437184 | tf_op jit(solution)/shard_map/pallas_call | solution.py:122
  128.4 10.4 %shard_map.291 = bf16[8,4,96,768]{3,2,1,0:T(8,128)(2,1)S(1)} custom-call(s32[32]{0:T(128)S(1)} %stack.197.spots_ref, bf16[16,96,768]{2,1,0:T(8,128)(2,1)S(1)} %copy-done.15, bf16[16,96,768]{2,1,0:T(8,128)(2,1)} %collective-permute-done.8.refs_1_), custom_call_target="tpu_custom_call" | custom-call | bytes 9437184 | tf_op jit(solution)/shard_map/pallas_call | solution.py:122
  155.1 8.1 %all-to-all-start = ((bf16[16,64,768]{2,1,0:T(8,128)(2,1)}), bf16[16,64,768]{2,1,0:T(8,128)(2,1)}, u32[]{:S(2)}, u32[]{:S(2)}) async-start(bf16[16,64,768]{2,1,0:T(8,128)(2,1)} %pad_maximum_fusion.5), calls=%async_computation | async-start | bytes 3145728 | tf_op jit(solution)/shard_map/all_to_all | solution.py:362
  163.8 24.4 %all-to-all-done = bf16[16,64,768]{2,1,0:T(8,128)(2,1)} async-done(((bf16[16,64,768]{2,1,0:T(8,128)(2,1)}), bf16[16,64,768]{2,1,0:T(8,128)(2,1)}, u32[]{:S(2)}, u32[]{:S(2)}) %all-to-all-start) | async-done | bytes 1572896 | tf_op jit(solution)/shard_map/all_to_all | solution.py:362
  194.7 7.0 %multiply_convert_fusion = (bf16[1024,1536]{1,0:T(8,128)(2,1)}, f32[1024,1536]{1,0:T(8,128)}) fusion(bf16[1024,768]{1,0:T(8,128)(2,1)} %bitcast.375, bf16[1536,768]{0,1:T(8,128)(2,1)} %all-gather.10.cloned.1.call-done), kind=kOutput, calls=%fused_computation.7 | convolution fusion | flops 2423783424 | bytes 13369344 | tf_op jit(solution)/shard_map/dot_general | solution.py:27
  201.7 6.8 %fusion.5 = bf16[1024,1536]{1,0:T(8,128)(2,1)S(1)} fusion(f32[1024,1536]{1,0:T(8,128)} %get-tuple-element.198, bf16[1024,768]{1,0:T(8,128)(2,1)} %bitcast.373, bf16[1,1536,768]{2,1,0:T(8,128)(2,1)} %all-gather.12.cloned.1.call-done), kind=kOutput, calls=%fused_computation.6 | convolution fusion | flops 2431647744 | bytes 13369344 | tf_op jit(solution)/shard_map/dot_general | solution.py:27
  214.2 5.4 %fusion.13 = f32[1024,768]{1,0:T(8,128)S(1)} fusion(bf16[1024,1536]{1,0:T(8,128)(2,1)} %get-tuple-element.197, bf16[1,1536,768]{2,1,0:T(8,128)(2,1)} %all-gather.12.cloned.1.call-done), kind=kOutput, calls=%fused_computation.46 | convolution fusion | flops 2415919104 | bytes 8650752 | tf_op jit(solution)/shard_map/dot_general | solution.py:17
  226.4 4.4 all-to-all-start.1
  231.1 6.5 %convolution_convert_fusion.7 = bf16[1536,768]{1,0:T(8,128)(2,1)} fusion(bf16[1024,1536]{1,0:T(8,128)(2,1)} %get-tuple-element.197, bf16[1024,768]{1,0:T(8,128)(2,1)} %bitcast.374), kind=kOutput, calls=%fused_computation.23 | convolution fusion | flops 2417098752 | bytes 7077888 | tf_op jit(solution)/shard_map/dot_general | solution.py:21
  242.0 16.1 %all-to-all-done.1 = bf16[16,64,768]{2,1,0:T(8,128)(2,1)} async-done(((bf16[16,64,768]{2,1,0:T(8,128)(2,1)}), bf16[16,64,768]{2,1,0:T(8,128)(2,1)}, u32[]{:S(2)}, u32[]{:S(2)}) %all-to-all-start.1) | async-done | bytes 1572896 | tf_op jit(solution)/shard_map/all_to_all | solution.py:379
  286.6 4.4 multiply_reduce_fusion.5
  298.0 6.7 %fusion.7 = bf16[197,3072]{1,0:T(8,128)(2,1)S(1)} fusion(bf16[3072,768]{1,0:T(8,128)(2,1)} %bitcast.328, f32[197,3072]{1,0:T(8,128)} %get-tuple-element.188, f32[197,768]{1,0:T(8,128)S(1)} %copy-done.37), kind=kOutput, calls=%fused_computation.17 | convolution fusion | flops 935765760 | bytes 8954880 | tf_op jit(solution)/shard_map/dot_general | solution.py:27
  340.4 5.1 convolution_convert_fusion
  355.5 18.8 %collective-permute-done.17 = bf16[96,3200]{1,0:T(8,128)(2,1)S(1)} collective-permute-done((bf16[96,3200]{1,0:T(8,128)(2,1)S(1)}, bf16[96,3200]{1,0:T(8,128)(2,1)S(1)}, u32[]{:S(2)}, u32[]{:S(2)}) %collective-permute-start.17) | collective-permute-done | bytes 614432 | tf_op jit(solution)/shard_map/ppermute | solution.py:70
  376.3 13.3 %collective-permute-done.19 = bf16[96,3200]{1,0:T(8,128)(2,1)S(1)} collective-permute-done((bf16[96,3200]{1,0:T(8,128)(2,1)S(1)}, bf16[96,3200]{1,0:T(8,128)(2,1)S(1)}, u32[]{:S(2)}, u32[]{:S(2)}) %collective-permute-start.19) | collective-permute-done | bytes 614432 | tf_op jit(solution)/shard_map/ppermute | solution.py:70
  396.0 33.8 %all_to_all.30 = bf16[16,80,768]{2,1,0:T(8,128)(2,1)S(1)} all-to-all(bf16[16,80,768]{2,1,0:T(8,128)(2,1)S(1)} %fusion.17), channel_id=1, replica_groups=mesh['x'=4,'core'=2,'z'=4,'y'=4] {'z','y'}, dimensions={0} | all-to-all | bytes 3932160 | tf_op jit(solution)/shard_map/all_to_all | solution.py:235
  439.2 24.2 %all-to-all-done.3 = bf16[16,80,768]{2,1,0:T(8,128)(2,1)S(1)} async-done(((bf16[16,80,768]{2,1,0:T(8,128)(2,1)}), bf16[16,80,768]{2,1,0:T(8,128)(2,1)S(1)}, u32[]{:S(2)}, u32[]{:S(2)}) %all-to-all-start.3) | async-done | bytes 1966112 | tf_op jit(solution)/shard_map/all_to_all | solution.py:238
  477.4 7.3 %all-to-all-done.4 = bf16[16,24,768]{2,1,0:T(8,128)(2,1)} async-done(((bf16[16,24,768]{2,1,0:T(8,128)(2,1)}), bf16[16,24,768]{2,1,0:T(8,128)(2,1)}, u32[]{:S(2)}, u32[]{:S(2)}) %all-to-all-start.4) | async-done | bytes 589856 | tf_op jit(solution)/shard_map/all_to_all | solution.py:235
  493.7 6.9 %all-to-all-done.5 = bf16[16,24,768]{2,1,0:T(8,128)(2,1)S(1)} async-done(((bf16[16,24,768]{2,1,0:T(8,128)(2,1)}), bf16[16,24,768]{2,1,0:T(8,128)(2,1)S(1)}, u32[]{:S(2)}, u32[]{:S(2)}) %all-to-all-start.5) | async-done | bytes 589856 | tf_op jit(solution)/shard_map/all_to_all | solution.py:238
  (507 shorter events, 220.3 us)
Async XLA Ops:
  7.2 99.3 %all-gather.6.cloned.1.call-start = ((), (), s32[]{:S(2)}) async-start(), calls=%async_computation.11 | async-start | bytes 2949120 | tf_op jit(solution)/shard_map/all_gather | solution.py:160
  26.0 85.8 %all-gather.8.cloned.1.call-start = ((), (), s32[]{:S(2)}) async-start(), calls=%async_computation.12 | async-start | bytes 2949120 | tf_op jit(solution)/shard_map/all_gather | solution.py:161
  26.9 167.8 %all-gather.10.cloned.1.call-start = ((), (), s32[]{:S(2)}) async-start(), calls=%async_computation.13 | async-start | bytes 2949120 | tf_op jit(solution)/shard_map/all_gather | solution.py:469
  27.9 27.9 %collective-permute-start = (bf16[96,3200]{1,0:T(8,128)(2,1)S(1)}, bf16[96,3200]{1,0:T(8,128)(2,1)S(1)}, u32[]{:S(2)}, u32[]{:S(2)}) collective-permute-start(bf16[96,3200]{1,0:T(8,128)(2,1)S(1)} %concatenate.79), channel_id=1, source_target_pairs={{0,32},{32,64},{64,96},{96,0},{1,33},{33,65},{65,97},{97,1},{2,34}... | collective-permute-start | bytes 1843208 | tf_op jit(solution)/shard_map/ppermute | solution.py:70
  29.1 29.8 %collective-permute-start.1 = (bf16[96,3200]{1,0:T(8,128)(2,1)S(1)}, bf16[96,3200]{1,0:T(8,128)(2,1)S(1)}, u32[]{:S(2)}, u32[]{:S(2)}) collective-permute-start(bf16[96,3200]{1,0:T(8,128)(2,1)S(1)} %concatenate.79), channel_id=1, source_target_pairs={{0,64},{32,96},{64,0},{96,32},{1,65},{33,97},{65,1},{97,33},{2,66}... | collective-permute-start | bytes 1843208 | tf_op jit(solution)/shard_map/ppermute | solution.py:70
  31.1 29.6 %collective-permute-start.2 = (bf16[96,3200]{1,0:T(8,128)(2,1)S(1)}, bf16[96,3200]{1,0:T(8,128)(2,1)S(1)}, u32[]{:S(2)}, u32[]{:S(2)}) collective-permute-start(bf16[96,3200]{1,0:T(8,128)(2,1)S(1)} %concatenate.79), channel_id=1, source_target_pairs={{0,96},{32,0},{64,32},{96,64},{1,97},{33,1},{65,33},{97,65},{2,98}... | collective-permute-start | bytes 1843208 | tf_op jit(solution)/shard_map/ppermute | solution.py:70
  31.2 39.3 %collective-permute-start.9 = (bf16[96,3072]{1,0:T(8,128)(2,1)S(1)}, bf16[96,3072]{1,0:T(8,128)(2,1)S(1)}, u32[]{:S(2)}, u32[]{:S(2)}) collective-permute-start(bf16[96,3072]{1,0:T(8,128)(2,1)S(1)} %constant_dynamic-update-slice_fusion), channel_id=1, source_target_pairs={{0,32},{32,64},{64,96},{96,0},{1,33},{33,65},{65,97},{97,1},{2,34}... | collective-permute-start | bytes 1769480 | tf_op jit(solution)/shard_map/ppermute | solution.py:70
  34.5 38.8 %collective-permute-start.10 = (bf16[96,3072]{1,0:T(8,128)(2,1)S(1)}, bf16[96,3072]{1,0:T(8,128)(2,1)S(1)}, u32[]{:S(2)}, u32[]{:S(2)}) collective-permute-start(bf16[96,3072]{1,0:T(8,128)(2,1)S(1)} %constant_dynamic-update-slice_fusion), channel_id=1, source_target_pairs={{0,64},{32,96},{64,0},{96,32},{1,65},{33,97},{65,1},{97,33},{2,66}... | collective-permute-start | bytes 1769480 | tf_op jit(solution)/shard_map/ppermute | solution.py:70
  55.8 28.0 %collective-permute-start.11 = (bf16[96,3072]{1,0:T(8,128)(2,1)S(1)}, bf16[96,3072]{1,0:T(8,128)(2,1)S(1)}, u32[]{:S(2)}, u32[]{:S(2)}) collective-permute-start(bf16[96,3072]{1,0:T(8,128)(2,1)S(1)} %constant_dynamic-update-slice_fusion), channel_id=1, source_target_pairs={{0,96},{32,0},{64,32},{96,64},{1,97},{33,1},{65,33},{97,65},{2,98}... | collective-permute-start | bytes 1769480 | tf_op jit(solution)/shard_map/ppermute | solution.py:70
  61.1 35.3 %collective-permute-start.3 = (bf16[4,96,3200]{2,1,0:T(8,128)(2,1)S(1)}, bf16[4,96,3200]{2,1,0:T(8,128)(2,1)}, u32[]{:S(2)}, u32[]{:S(2)}) collective-permute-start(bf16[4,96,3200]{2,1,0:T(8,128)(2,1)S(1)} %pad_maximum_fusion.1.refs_0_), channel_id=1, source_target_pairs={{0,16},{16,0},{1,17},{17,1},{2,18},{18,2},{3,19},{19,3},{4,20},{20... | collective-permute-start | bytes 7372808 | tf_op jit(solution)/shard_map/ppermute | solution.py:83
  111.8 16.4 %collective-permute-start.8 = (bf16[16,96,768]{2,1,0:T(8,128)(2,1)}, bf16[16,96,768]{2,1,0:T(8,128)(2,1)}, u32[]{:S(2)}, u32[]{:S(2)}) collective-permute-start(bf16[16,96,768]{2,1,0:T(8,128)(2,1)} %all-gather.8.cloned.1.call-done.refs_0_), channel_id=1, source_target_pairs={{0,16},{16,0},{1,17},{17,1},{2,18},{18,2},{3,19},{19,3},{4,20},{20... | collective-permute-start | bytes 7077896 | tf_op jit(solution)/shard_map/ppermute | solution.py:83
  155.1 33.1 %all-to-all-start = ((bf16[16,64,768]{2,1,0:T(8,128)(2,1)}), bf16[16,64,768]{2,1,0:T(8,128)(2,1)}, u32[]{:S(2)}, u32[]{:S(2)}) async-start(bf16[16,64,768]{2,1,0:T(8,128)(2,1)} %pad_maximum_fusion.5), calls=%async_computation | async-start | bytes 3145728 | tf_op jit(solution)/shard_map/all_to_all | solution.py:362
  163.2 38.5 %all-gather.12.cloned.1.call-start = ((), (), s32[]{:S(2)}) async-start(), calls=%async_computation.18 | async-start | bytes 2949120 | tf_op jit(solution)/shard_map/all_gather | solution.py:470
  163.8 111.2 %reduce-scatter.16.cloned.1.call-start = ((), (), s32[]{:S(2)}) async-start(), calls=%async_computation.19 | async-start | bytes 2949120
  226.4 31.7 %all-to-all-start.1 = ((bf16[16,64,768]{2,1,0:T(8,128)(2,1)}), bf16[16,64,768]{2,1,0:T(8,128)(2,1)}, u32[]{:S(2)}, u32[]{:S(2)}) async-start(bf16[16,64,768]{2,1,0:T(8,128)(2,1)} %pad_maximum_fusion.8), calls=%async_computation.1 | async-start | bytes 3145728 | tf_op jit(solution)/shard_map/all_to_all | solution.py:379
  230.8 47.3 %reduce-scatter.8.cloned.1.call-start = ((), (), s32[]{:S(2)}) async-start(), calls=%async_computation.14 | async-start | bytes 2949120 | tf_op jit(solution)/shard_map/reduce_scatter | solution.py:386
  237.6 155.9 %reduce-scatter.10.cloned.1.call-start = ((), (), s32[]{:S(2)}) async-start(), calls=%async_computation.15 | async-start | bytes 5308416 | tf_op jit(solution)/shard_map/reduce_scatter | solution.py:219
  286.6 108.1 %reduce-scatter.12.cloned.1.call-start = ((), (), s32[]{:S(2)}) async-start(), calls=%async_computation.16 | async-start | bytes 5308416 | tf_op jit(solution)/shard_map/reduce_scatter | solution.py:219
  296.0 171.1 %reduce-scatter.14.cloned.1.call-start = ((), (), s32[]{:S(2)}) async-start(), calls=%async_computation.17 | async-start | bytes 5308416 | tf_op jit(solution)/shard_map/reduce_scatter | solution.py:219
  352.6 21.7 %collective-permute-start.17 = (bf16[96,3200]{1,0:T(8,128)(2,1)S(1)}, bf16[96,3200]{1,0:T(8,128)(2,1)S(1)}, u32[]{:S(2)}, u32[]{:S(2)}) collective-permute-start(bf16[96,3200]{1,0:T(8,128)(2,1)S(1)} %get-tuple-element.125), channel_id=1, source_target_pairs={{0,32},{32,64},{64,96},{96,0},{1,33},{33,65},{65,97},{97,1},{2,34}... | collective-permute-start | bytes 1843208 | tf_op jit(solution)/shard_map/ppermute | solution.py:70
  353.7 22.6 %collective-permute-start.18 = (bf16[96,3200]{1,0:T(8,128)(2,1)S(1)}, bf16[96,3200]{1,0:T(8,128)(2,1)S(1)}, u32[]{:S(2)}, u32[]{:S(2)}) collective-permute-start(bf16[96,3200]{1,0:T(8,128)(2,1)S(1)} %get-tuple-element.127), channel_id=1, source_target_pairs={{0,64},{32,96},{64,0},{96,32},{1,65},{33,97},{65,1},{97,33},{2,66}... | collective-permute-start | bytes 1843208 | tf_op jit(solution)/shard_map/ppermute | solution.py:70
  354.4 35.2 %collective-permute-start.19 = (bf16[96,3200]{1,0:T(8,128)(2,1)S(1)}, bf16[96,3200]{1,0:T(8,128)(2,1)S(1)}, u32[]{:S(2)}, u32[]{:S(2)}) collective-permute-start(bf16[96,3200]{1,0:T(8,128)(2,1)S(1)} %get-tuple-element.126), channel_id=1, source_target_pairs={{0,96},{32,0},{64,32},{96,64},{1,97},{33,1},{65,33},{97,65},{2,98}... | collective-permute-start | bytes 1843208 | tf_op jit(solution)/shard_map/ppermute | solution.py:70
  431.5 31.9 %all-to-all-start.3 = ((bf16[16,80,768]{2,1,0:T(8,128)(2,1)}), bf16[16,80,768]{2,1,0:T(8,128)(2,1)S(1)}, u32[]{:S(2)}, u32[]{:S(2)}) async-start(bf16[16,80,768]{2,1,0:T(8,128)(2,1)} %broadcast_in_dim.31), calls=%async_computation.6 | async-start | bytes 3932160 | tf_op jit(solution)/shard_map/all_to_all | solution.py:238
  469.2 15.5 %all-to-all-start.4 = ((bf16[16,24,768]{2,1,0:T(8,128)(2,1)}), bf16[16,24,768]{2,1,0:T(8,128)(2,1)}, u32[]{:S(2)}, u32[]{:S(2)}) async-start(bf16[16,24,768]{2,1,0:T(8,128)(2,1)} %bitcast.367), calls=%async_computation.8 | async-start | bytes 1179648 | tf_op jit(solution)/shard_map/all_to_all | solution.py:235
  (136 other events, 686.2 us)
Sparse Core Ops, SparseCore 0:
  26.1 35.7 all-gather.5
  64.1 32.9 all-gather.7
  98.8 31.1 all-gather.9
  165.4 32.2 all-gather.11
  214.3 27.8 reduce-scatter.15
  244.4 31.5 reduce-scatter.7
  286.7 34.8 reduce-scatter.9
  324.0 54.9 reduce-scatter.11
  381.5 47.7 reduce-scatter.13

commit v6 on v5

--- a/solution.py
+++ b/solution.py
@@ -356,14 +356,13 @@
     slot_gate = jnp.sum(pick_first * gate_first + pick_second * gate_second, axis=0)
     send_rows = product_t(select, normed).astype(jnp.bfloat16)
     send_grad = (product_t(select, grad_low) * slot_gate[:, None]).astype(jnp.bfloat16)
-    send = jnp.concatenate(
-        [send_rows.reshape(experts, SLOTS, width), send_grad.reshape(experts, SLOTS, width)], axis=1
-    )
-    received = lax.all_to_all(send, ("z", "y"), split_axis=0, concat_axis=0, tiled=True)
-    partner = core_swap(received)
-
-    flat = jnp.concatenate([received[:, :SLOTS], partner[:, :SLOTS]], axis=0).reshape(-1, width)
-    flat_grad = jnp.concatenate([received[:, SLOTS:], partner[:, SLOTS:]], axis=0).reshape(-1, width)
+    def dispatch(rows_out):
+        came = lax.all_to_all(
+            rows_out.reshape(experts, SLOTS, width), ("z", "y"), split_axis=0, concat_axis=0, tiled=True
+        ).reshape(slots, width)
+        return jnp.concatenate([came, core_swap(came)], axis=0)
+
+    flat, flat_grad = dispatch(send_rows), dispatch(send_grad)
     hidden, slope = gelu_parts(product_bt(flat, up_half))
     hidden = hidden.astype(jnp.bfloat16)
     partial_out = product(hidden, down_half)

time: 518 us -> 521 us (level)
    all_to_all x1 -> x2, starting transfers between devices: 8.09 us -> 12.5 us  [dispatch(): lax.all_to_all(rows_out.reshape(experts, SLOTS, width), ('z', 'y'), split...]
    all_to_all x1 -> x2, waiting for transfers between devices: 24.4 us -> 24.8 us  [dispatch(): lax.all_to_all(rows_out.reshape(experts, SLOTS, width), ('z', 'y'), split...]
    unnamed x262 -> x256, local copies, waits for them, and re-layouts: 30.4 us -> 30.2 us
  transfers between devices with their start and end apart: 34 -> 36, of which waited for: 19 -> 19; matrix products, arithmetic and copies ran while one was open for 32% -> 32% of each run, Pallas kernels for 4% -> 4%
where the time goes in v6:
time: 521 us; the launch traced here: 511 us
  waiting for transfers between devices  177 us (34%)
  matrix products  103 us (20%)
  local copies, waits for them, and re-layouts  66.2 us (13%)
  starting transfers between devices  46.5 us (9%)
  other arithmetic  42.3 us (8%)
  blocking collectives  33.8 us (6%)
  Pallas kernels  22.6 us (4%)
  between operations  20.3 us (4%)
    ppermute x12, waiting for transfers between devices, shift(): return lax.ppermute(block, axis, [(i, (i + step) % X) for i in range(X)])  94.1 us
    all_to_all x1, blocking collectives, sum_over_zy(): lax.all_to_all(packed, ('z', 'y'), split_axis=0, concat_axis=0, tiled=True)  33.8 us
    dot_general x9, matrix products, product_bt(): lax.dot_general(left, right, (((1,), (1,)), ((), ())), preferred_element_...  32.3 us
    all_to_all x2, waiting for transfers between devices, sum_over_zy(): lax.all_to_all(copies, ('z', 'y'), split_axis=0, concat_axis=0, tiled=True)  31.2 us
    unnamed x256, local copies, waits for them, and re-layouts  30.2 us
    dot_general x9, matrix products, product_t(): lax.dot_general(left, right, (((0,), (0,)), ((), ())), preferred_element_...  29.5 us
    dot_general x16, matrix products, product(): return jnp.dot(left, right, preferred_element_type=jnp.float32)  28.8 us
    all_to_all x2, waiting for transfers between devices, dispatch(): lax.all_to_all(rows_out.reshape(experts, SLOTS, width), ('z', 'y'), split...  24.8 us
  transfers between devices with their start and end apart: 36, of which 19 were waited for; matrix products, arithmetic and copies ran while one was open for 32% of the time, Pallas kernels for 4%

profile of v6, /device:TPU:6, one launch (start us, length us, event | category | flops | bytes accessed | tf_op | source)
XLA Modules:
  0.0 511.2 jit_solution(11593318026239597200)
XLA Ops:
  11.2 7.0 %collective-permute-done.4 = bf16[192,768]{1,0:T(8,128)(2,1)S(1)} collective-permute-done((bf16[192,768]{1,0:T(8,128)(2,1)S(1)}, bf16[192,768]{1,0:T(8,128)(2,1)S(1)}, u32[]{:S(2)}, u32[]{:S(2)}) %collective-permute-start.4) | collective-permute-done | bytes 294944 | tf_op jit(solution)/shard_map/ppermute | solution.py:70
  20.3 4.7 collective-permute-done.6
  35.6 21.0 %collective-permute-done = bf16[96,3200]{1,0:T(8,128)(2,1)S(1)} collective-permute-done((bf16[96,3200]{1,0:T(8,128)(2,1)S(1)}, bf16[96,3200]{1,0:T(8,128)(2,1)S(1)}, u32[]{:S(2)}, u32[]{:S(2)}) %collective-permute-start) | collective-permute-done | bytes 614432 | tf_op jit(solution)/shard_map/ppermute | solution.py:70
  62.0 9.3 %collective-permute-done.9 = bf16[96,3072]{1,0:T(8,128)(2,1)S(1)} collective-permute-done((bf16[96,3072]{1,0:T(8,128)(2,1)S(1)}, bf16[96,3072]{1,0:T(8,128)(2,1)S(1)}, u32[]{:S(2)}, u32[]{:S(2)}) %collective-permute-start.9) | collective-permute-done | bytes 589856 | tf_op jit(solution)/shard_map/ppermute | solution.py:70
  74.1 10.4 %collective-permute-done.11 = bf16[96,3072]{1,0:T(8,128)(2,1)S(1)} collective-permute-done((bf16[96,3072]{1,0:T(8,128)(2,1)S(1)}, bf16[96,3072]{1,0:T(8,128)(2,1)S(1)}, u32[]{:S(2)}, u32[]{:S(2)}) %collective-permute-start.11) | collective-permute-done | bytes 589856 | tf_op jit(solution)/shard_map/ppermute | solution.py:70
  119.4 5.9 %shard_map.290 = bf16[8,96,3072]{2,1,0:T(8,128)(2,1)S(1)} custom-call(s32[32]{0:T(128)S(1)} %stack.197.spots_ref, bf16[16,96,768]{2,1,0:T(8,128)(2,1)S(1)} %copy-done.14, bf16[16,96,768]{2,1,0:T(8,128)(2,1)} %collective-permute-done.7.refs_1_), custom_call_target="tpu_custom_call" | custom-call | bytes 9437184 | tf_op jit(solution)/shard_map/pallas_call | solution.py:122
  128.8 10.4 %shard_map.291 = bf16[8,4,96,768]{3,2,1,0:T(8,128)(2,1)S(1)} custom-call(s32[32]{0:T(128)S(1)} %stack.197.spots_ref, bf16[16,96,768]{2,1,0:T(8,128)(2,1)S(1)} %copy-done.15, bf16[16,96,768]{2,1,0:T(8,128)(2,1)} %collective-permute-done.8.refs_1_), custom_call_target="tpu_custom_call" | custom-call | bytes 9437184 | tf_op jit(solution)/shard_map/pallas_call | solution.py:122
  154.6 8.2 %all-to-all-start = ((bf16[16,32,768]{2,1,0:T(8,128)(2,1)}), bf16[16,32,768]{2,1,0:T(8,128)(2,1)}, u32[]{:S(2)}, u32[]{:S(2)}) async-start(bf16[16,32,768]{2,1,0:T(8,128)(2,1)} %bitcast.386), calls=%async_computation | async-start | bytes 1572864 | tf_op jit(solution)/shard_map/all_to_all | solution.py:360
  166.2 11.3 %all-to-all-done = bf16[16,32,768]{2,1,0:T(8,128)(2,1)} async-done(((bf16[16,32,768]{2,1,0:T(8,128)(2,1)}), bf16[16,32,768]{2,1,0:T(8,128)(2,1)}, u32[]{:S(2)}, u32[]{:S(2)}) %all-to-all-start) | async-done | bytes 786464 | tf_op jit(solution)/shard_map/all_to_all | solution.py:360
  182.0 13.5 %all-to-all-done.1 = bf16[16,32,768]{2,1,0:T(8,128)(2,1)} async-done(((bf16[16,32,768]{2,1,0:T(8,128)(2,1)}), bf16[16,32,768]{2,1,0:T(8,128)(2,1)}, u32[]{:S(2)}, u32[]{:S(2)}) %all-to-all-start.1) | async-done | bytes 786464 | tf_op jit(solution)/shard_map/all_to_all | solution.py:360
  195.9 7.0 %multiply_convert_fusion = (bf16[1024,1536]{1,0:T(8,128)(2,1)}, f32[1024,1536]{1,0:T(8,128)}) fusion(bf16[1536,768]{0,1:T(8,128)(2,1)} %all-gather.10.cloned.1.call-done, bf16[512,768]{1,0:T(8,128)(2,1)} %collective-permute-done.13, bf16[512,768]{1,0:T(8,128)(2,1)} %bitcast.62), kind=kOutput, calls=%fused_computation.7 | convolution fusion | flops 2426929152 | bytes 13369344 | tf_op jit(solution)/shard_map/dot_general | solution.py:27
  202.9 7.1 %fusion.5 = bf16[1024,1536]{1,0:T(8,128)(2,1)S(1)} fusion(f32[1024,1536]{1,0:T(8,128)} %get-tuple-element.194, bf16[1,1536,768]{2,1,0:T(8,128)(2,1)} %all-gather.12.cloned.1.call-done, bf16[512,768]{1,0:T(8,128)(2,1)} %collective-permute-done.15, bf16[512,768]{1,0:T(8,128)(2,1)} %bitcast.72), kind=kOutput, calls=%fused_computation.6 | convolution fusion | flops 2434793472 | bytes 13369344 | tf_op jit(solution)/shard_map/dot_general | solution.py:27
  211.7 5.3 %convolution_convert_fusion.6 = bf16[1536,768]{1,0:T(8,128)(2,1)} fusion(bf16[1024,1536]{1,0:T(8,128)(2,1)S(1)} %fusion.5, bf16[512,768]{1,0:T(8,128)(2,1)} %collective-permute-done.13, bf16[512,768]{1,0:T(8,128)(2,1)} %bitcast.62), kind=kOutput, calls=%fused_computation.22 | convolution fusion | flops 2420244480 | bytes 7077888 | tf_op jit(solution)/shard_map/dot_general | solution.py:21
  217.1 5.4 %fusion.13 = f32[1024,768]{1,0:T(8,128)S(1)} fusion(bf16[1024,1536]{1,0:T(8,128)(2,1)} %get-tuple-element.193, bf16[1,1536,768]{2,1,0:T(8,128)(2,1)} %all-gather.12.cloned.1.call-done), kind=kOutput, calls=%fused_computation.46 | convolution fusion | flops 2415919104 | bytes 8650752 | tf_op jit(solution)/shard_map/dot_general | solution.py:17
  234.1 6.4 %convolution_convert_fusion.7 = bf16[1536,768]{1,0:T(8,128)(2,1)} fusion(bf16[1024,1536]{1,0:T(8,128)(2,1)} %get-tuple-element.193, bf16[512,768]{1,0:T(8,128)(2,1)} %collective-permute-done.15, bf16[512,768]{1,0:T(8,128)(2,1)} %bitcast.72), kind=kOutput, calls=%fused_computation.23 | convolution fusion | flops 2420244480 | bytes 7077888 | tf_op jit(solution)/shard_map/dot_general | solution.py:21
  245.2 14.8 %all-to-all-done.2 = bf16[16,64,768]{2,1,0:T(8,128)(2,1)} async-done(((bf16[16,64,768]{2,1,0:T(8,128)(2,1)}), bf16[16,64,768]{2,1,0:T(8,128)(2,1)}, u32[]{:S(2)}, u32[]{:S(2)}) %all-to-all-start.2) | async-done | bytes 1572896 | tf_op jit(solution)/shard_map/all_to_all | solution.py:378
  299.8 6.5 %fusion.7 = bf16[197,3072]{1,0:T(8,128)(2,1)S(1)} fusion(bf16[3072,768]{1,0:T(8,128)(2,1)} %bitcast.324, f32[197,3072]{1,0:T(8,128)} %get-tuple-element.184, f32[197,768]{1,0:T(8,128)S(1)} %copy-done.37), kind=kOutput, calls=%fused_computation.17 | convolution fusion | flops 935765760 | bytes 8954880 | tf_op jit(solution)/shard_map/dot_general | solution.py:27
  342.0 5.1 convolution_convert_fusion
  357.0 19.7 %collective-permute-done.18 = bf16[96,3200]{1,0:T(8,128)(2,1)S(1)} collective-permute-done((bf16[96,3200]{1,0:T(8,128)(2,1)S(1)}, bf16[96,3200]{1,0:T(8,128)(2,1)S(1)}, u32[]{:S(2)}, u32[]{:S(2)}) %collective-permute-start.18) | collective-permute-done | bytes 614432 | tf_op jit(solution)/shard_map/ppermute | solution.py:70
  378.6 13.3 %collective-permute-done.20 = bf16[96,3200]{1,0:T(8,128)(2,1)S(1)} collective-permute-done((bf16[96,3200]{1,0:T(8,128)(2,1)S(1)}, bf16[96,3200]{1,0:T(8,128)(2,1)S(1)}, u32[]{:S(2)}, u32[]{:S(2)}) %collective-permute-start.20) | collective-permute-done | bytes 614432 | tf_op jit(solution)/shard_map/ppermute | solution.py:70
  398.3 33.8 %all_to_all.35 = bf16[16,80,768]{2,1,0:T(8,128)(2,1)S(1)} all-to-all(bf16[16,80,768]{2,1,0:T(8,128)(2,1)S(1)} %fusion.17), channel_id=1, replica_groups=mesh['x'=4,'core'=2,'z'=4,'y'=4] {'z','y'}, dimensions={0} | all-to-all | bytes 3932160 | tf_op jit(solution)/shard_map/all_to_all | solution.py:235
  441.5 24.2 %all-to-all-done.4 = bf16[16,80,768]{2,1,0:T(8,128)(2,1)S(1)} async-done(((bf16[16,80,768]{2,1,0:T(8,128)(2,1)}), bf16[16,80,768]{2,1,0:T(8,128)(2,1)S(1)}, u32[]{:S(2)}, u32[]{:S(2)}) %all-to-all-start.4) | async-done | bytes 1966112 | tf_op jit(solution)/shard_map/all_to_all | solution.py:238
  479.7 7.3 %all-to-all-done.5 = bf16[16,24,768]{2,1,0:T(8,128)(2,1)} async-done(((bf16[16,24,768]{2,1,0:T(8,128)(2,1)}), bf16[16,24,768]{2,1,0:T(8,128)(2,1)}, u32[]{:S(2)}, u32[]{:S(2)}) %all-to-all-start.5) | async-done | bytes 589856 | tf_op jit(solution)/shard_map/all_to_all | solution.py:235
  496.0 7.0 %all-to-all-done.6 = bf16[16,24,768]{2,1,0:T(8,128)(2,1)S(1)} async-done(((bf16[16,24,768]{2,1,0:T(8,128)(2,1)}), bf16[16,24,768]{2,1,0:T(8,128)(2,1)S(1)}, u32[]{:S(2)}, u32[]{:S(2)}) %all-to-all-start.6) | async-done | bytes 589856 | tf_op jit(solution)/shard_map/all_to_all | solution.py:238
  (500 shorter events, 226.1 us)
Async XLA Ops:
  7.2 100.0 %all-gather.6.cloned.1.call-start = ((), (), s32[]{:S(2)}) async-start(), calls=%async_computation.12 | async-start | bytes 2949120 | tf_op jit(solution)/shard_map/all_gather | solution.py:160
  26.0 86.6 %all-gather.8.cloned.1.call-start = ((), (), s32[]{:S(2)}) async-start(), calls=%async_computation.13 | async-start | bytes 2949120 | tf_op jit(solution)/shard_map/all_gather | solution.py:161
  26.9 168.9 %all-gather.10.cloned.1.call-start = ((), (), s32[]{:S(2)}) async-start(), calls=%async_computation.14 | async-start | bytes 2949120 | tf_op jit(solution)/shard_map/all_gather | solution.py:468
  27.7 175.2 %all-gather.12.cloned.1.call-start = ((), (), s32[]{:S(2)}) async-start(), calls=%async_computation.19 | async-start | bytes 2949120 | tf_op jit(solution)/shard_map/all_gather | solution.py:469
  28.7 28.0 %collective-permute-start = (bf16[96,3200]{1,0:T(8,128)(2,1)S(1)}, bf16[96,3200]{1,0:T(8,128)(2,1)S(1)}, u32[]{:S(2)}, u32[]{:S(2)}) collective-permute-start(bf16[96,3200]{1,0:T(8,128)(2,1)S(1)} %concatenate.76), channel_id=1, source_target_pairs={{0,32},{32,64},{64,96},{96,0},{1,33},{33,65},{65,97},{97,1},{2,34}... | collective-permute-start | bytes 1843208 | tf_op jit(solution)/shard_map/ppermute | solution.py:70
  29.9 29.7 %collective-permute-start.1 = (bf16[96,3200]{1,0:T(8,128)(2,1)S(1)}, bf16[96,3200]{1,0:T(8,128)(2,1)S(1)}, u32[]{:S(2)}, u32[]{:S(2)}) collective-permute-start(bf16[96,3200]{1,0:T(8,128)(2,1)S(1)} %concatenate.76), channel_id=1, source_target_pairs={{0,64},{32,96},{64,0},{96,32},{1,65},{33,97},{65,1},{97,33},{2,66}... | collective-permute-start | bytes 1843208 | tf_op jit(solution)/shard_map/ppermute | solution.py:70
  31.9 29.6 %collective-permute-start.2 = (bf16[96,3200]{1,0:T(8,128)(2,1)S(1)}, bf16[96,3200]{1,0:T(8,128)(2,1)S(1)}, u32[]{:S(2)}, u32[]{:S(2)}) collective-permute-start(bf16[96,3200]{1,0:T(8,128)(2,1)S(1)} %concatenate.76), channel_id=1, source_target_pairs={{0,96},{32,0},{64,32},{96,64},{1,97},{33,1},{65,33},{97,65},{2,98}... | collective-permute-start | bytes 1843208 | tf_op jit(solution)/shard_map/ppermute | solution.py:70
  32.0 39.3 %collective-permute-start.9 = (bf16[96,3072]{1,0:T(8,128)(2,1)S(1)}, bf16[96,3072]{1,0:T(8,128)(2,1)S(1)}, u32[]{:S(2)}, u32[]{:S(2)}) collective-permute-start(bf16[96,3072]{1,0:T(8,128)(2,1)S(1)} %constant_dynamic-update-slice_fusion), channel_id=1, source_target_pairs={{0,32},{32,64},{64,96},{96,0},{1,33},{33,65},{65,97},{97,1},{2,34}... | collective-permute-start | bytes 1769480 | tf_op jit(solution)/shard_map/ppermute | solution.py:70
  35.3 38.9 %collective-permute-start.10 = (bf16[96,3072]{1,0:T(8,128)(2,1)S(1)}, bf16[96,3072]{1,0:T(8,128)(2,1)S(1)}, u32[]{:S(2)}, u32[]{:S(2)}) collective-permute-start(bf16[96,3072]{1,0:T(8,128)(2,1)S(1)} %constant_dynamic-update-slice_fusion), channel_id=1, source_target_pairs={{0,64},{32,96},{64,0},{96,32},{1,65},{33,97},{65,1},{97,33},{2,66}... | collective-permute-start | bytes 1769480 | tf_op jit(solution)/shard_map/ppermute | solution.py:70
  56.7 27.9 %collective-permute-start.11 = (bf16[96,3072]{1,0:T(8,128)(2,1)S(1)}, bf16[96,3072]{1,0:T(8,128)(2,1)S(1)}, u32[]{:S(2)}, u32[]{:S(2)}) collective-permute-start(bf16[96,3072]{1,0:T(8,128)(2,1)S(1)} %constant_dynamic-update-slice_fusion), channel_id=1, source_target_pairs={{0,96},{32,0},{64,32},{96,64},{1,97},{33,1},{65,33},{97,65},{2,98}... | collective-permute-start | bytes 1769480 | tf_op jit(solution)/shard_map/ppermute | solution.py:70
  61.9 35.2 %collective-permute-start.3 = (bf16[4,96,3200]{2,1,0:T(8,128)(2,1)S(1)}, bf16[4,96,3200]{2,1,0:T(8,128)(2,1)}, u32[]{:S(2)}, u32[]{:S(2)}) collective-permute-start(bf16[4,96,3200]{2,1,0:T(8,128)(2,1)S(1)} %pad_maximum_fusion.1.refs_0_), channel_id=1, source_target_pairs={{0,16},{16,0},{1,17},{17,1},{2,18},{18,2},{3,19},{19,3},{4,20},{20... | collective-permute-start | bytes 7372808 | tf_op jit(solution)/shard_map/ppermute | solution.py:83
  112.5 16.1 %collective-permute-start.8 = (bf16[16,96,768]{2,1,0:T(8,128)(2,1)}, bf16[16,96,768]{2,1,0:T(8,128)(2,1)}, u32[]{:S(2)}, u32[]{:S(2)}) collective-permute-start(bf16[16,96,768]{2,1,0:T(8,128)(2,1)} %all-gather.8.cloned.1.call-done.refs_0_), channel_id=1, source_target_pairs={{0,16},{16,0},{1,17},{17,1},{2,18},{18,2},{3,19},{19,3},{4,20},{20... | collective-permute-start | bytes 7077896 | tf_op jit(solution)/shard_map/ppermute | solution.py:83
  154.6 22.9 %all-to-all-start = ((bf16[16,32,768]{2,1,0:T(8,128)(2,1)}), bf16[16,32,768]{2,1,0:T(8,128)(2,1)}, u32[]{:S(2)}, u32[]{:S(2)}) async-start(bf16[16,32,768]{2,1,0:T(8,128)(2,1)} %bitcast.386), calls=%async_computation | async-start | bytes 1572864 | tf_op jit(solution)/shard_map/all_to_all | solution.py:360
  177.5 17.9 %all-to-all-start.1 = ((bf16[16,32,768]{2,1,0:T(8,128)(2,1)}), bf16[16,32,768]{2,1,0:T(8,128)(2,1)}, u32[]{:S(2)}, u32[]{:S(2)}) async-start(bf16[16,32,768]{2,1,0:T(8,128)(2,1)} %bitcast.385), calls=%async_computation.1 | async-start | bytes 1572864 | tf_op jit(solution)/shard_map/all_to_all | solution.py:360
  181.8 95.0 %reduce-scatter.16.cloned.1.call-start = ((), (), s32[]{:S(2)}) async-start(), calls=%async_computation.20 | async-start | bytes 2949120
  229.6 30.4 %all-to-all-start.2 = ((bf16[16,64,768]{2,1,0:T(8,128)(2,1)}), bf16[16,64,768]{2,1,0:T(8,128)(2,1)}, u32[]{:S(2)}, u32[]{:S(2)}) async-start(bf16[16,64,768]{2,1,0:T(8,128)(2,1)} %pad_maximum_fusion.7), calls=%async_computation.2 | async-start | bytes 3145728 | tf_op jit(solution)/shard_map/all_to_all | solution.py:378
  234.0 45.9 %reduce-scatter.8.cloned.1.call-start = ((), (), s32[]{:S(2)}) async-start(), calls=%async_computation.15 | async-start | bytes 2949120 | tf_op jit(solution)/shard_map/reduce_scatter | solution.py:385
  240.6 155.2 %reduce-scatter.10.cloned.1.call-start = ((), (), s32[]{:S(2)}) async-start(), calls=%async_computation.16 | async-start | bytes 5308416 | tf_op jit(solution)/shard_map/reduce_scatter | solution.py:219
  288.4 108.6 %reduce-scatter.12.cloned.1.call-start = ((), (), s32[]{:S(2)}) async-start(), calls=%async_computation.17 | async-start | bytes 5308416 | tf_op jit(solution)/shard_map/reduce_scatter | solution.py:219
  297.9 171.6 %reduce-scatter.14.cloned.1.call-start = ((), (), s32[]{:S(2)}) async-start(), calls=%async_computation.18 | async-start | bytes 5308416 | tf_op jit(solution)/shard_map/reduce_scatter | solution.py:219
  354.2 22.5 %collective-permute-start.18 = (bf16[96,3200]{1,0:T(8,128)(2,1)S(1)}, bf16[96,3200]{1,0:T(8,128)(2,1)S(1)}, u32[]{:S(2)}, u32[]{:S(2)}) collective-permute-start(bf16[96,3200]{1,0:T(8,128)(2,1)S(1)} %get-tuple-element.125), channel_id=1, source_target_pairs={{0,32},{32,64},{64,96},{96,0},{1,33},{33,65},{65,97},{97,1},{2,34}... | collective-permute-start | bytes 1843208 | tf_op jit(solution)/shard_map/ppermute | solution.py:70
  355.3 23.3 %collective-permute-start.19 = (bf16[96,3200]{1,0:T(8,128)(2,1)S(1)}, bf16[96,3200]{1,0:T(8,128)(2,1)S(1)}, u32[]{:S(2)}, u32[]{:S(2)}) collective-permute-start(bf16[96,3200]{1,0:T(8,128)(2,1)S(1)} %get-tuple-element.127), channel_id=1, source_target_pairs={{0,64},{32,96},{64,0},{96,32},{1,65},{33,97},{65,1},{97,33},{2,66}... | collective-permute-start | bytes 1843208 | tf_op jit(solution)/shard_map/ppermute | solution.py:70
  356.1 35.8 %collective-permute-start.20 = (bf16[96,3200]{1,0:T(8,128)(2,1)S(1)}, bf16[96,3200]{1,0:T(8,128)(2,1)S(1)}, u32[]{:S(2)}, u32[]{:S(2)}) collective-permute-start(bf16[96,3200]{1,0:T(8,128)(2,1)S(1)} %get-tuple-element.126), channel_id=1, source_target_pairs={{0,96},{32,0},{64,32},{96,64},{1,97},{33,1},{65,33},{97,65},{2,98}... | collective-permute-start | bytes 1843208 | tf_op jit(solution)/shard_map/ppermute | solution.py:70
  433.8 31.9 %all-to-all-start.4 = ((bf16[16,80,768]{2,1,0:T(8,128)(2,1)}), bf16[16,80,768]{2,1,0:T(8,128)(2,1)S(1)}, u32[]{:S(2)}, u32[]{:S(2)}) async-start(bf16[16,80,768]{2,1,0:T(8,128)(2,1)} %broadcast_in_dim.31), calls=%async_computation.7 | async-start | bytes 3932160 | tf_op jit(solution)/shard_map/all_to_all | solution.py:238
  (135 other events, 735.2 us)
Sparse Core Ops, SparseCore 0:
  26.1 35.7 all-gather.5
  64.1 32.9 all-gather.7
  98.8 31.1 all-gather.9
  131.5 33.0 all-gather.11
  217.2 27.3 reduce-scatter.15
  246.8 31.5 reduce-scatter.7
  288.6 35.3 reduce-scatter.9
  326.4 56.4 reduce-scatter.11
  385.3 46.0 reduce-scatter.13
